TPU v7x, 32 devices: a whole 2x2x4 slice. The times are simulated.
32 devices in a mesh: dp: 8 (over z, x), fsdp: 4 (over y, core).
Axes of the slice: x: 2, y: 2, z: 4, core: 2. Of those that a mesh axis runs over, the one named last changes fastest.
Arguments:
- cached: bfloat16 [8, 4, 256, 1024], P('dp', 'fsdp'), may hold values from -60 to 60
- send_rows: int32 [8, 4, 8, 64], P('dp', 'fsdp'), may hold values from -1 to 255, as said below
- take_rows: int32 [8, 4, 256], P('dp', 'fsdp'), may hold values from -1 to 511, as said below
- utt_index: int32 [8, 4, 256], P('dp', 'fsdp'), may hold values from 0 to 9, never falling along the last dimension, each value on 1 to 64 neighbouring positions
- upstream: bfloat16 [8, 4, 512, 1536], P('dp', 'fsdp'), may hold values from -6 to 6
- in_proj: bfloat16 [512, 1536], P(None, 'fsdp'), may hold values from -2 to 2
- norm_gain: bfloat16 [1536], P('fsdp'), may hold values from 0.099609375 to 1.8984375
- conv_kernel: bfloat16 [31, 1536], P(None, 'fsdp'), may hold values from -1 to 1
Outputs:
- grad_proj: float32 [512, 1536], P(None, 'fsdp')
- grad_kernel: float32 [31, 1536], P(None, 'fsdp')
- grad_gain: float32 [1536], P('fsdp')
- step_loss: float32 [8, 4], P('dp', 'fsdp')
Inputs may be any that keep to these rules, and one draw needn't show every extreme that they name: `send_rows`: entry [s, g, d, j] is -1 or the cache row of sender s (same fsdp group g) sent as entry j of its slot for device d. The used entries of a slot come first; a sender's used entries for one device lie in one aligned block of 64 cache rows; a sender's entries name distinct rows. Each device receives from 4 senders of its group, and some device of each group receives 64 rows from each of them. `take_rows`: entry [d, g, r] is -1 or s * 64 + j for a used entry send_rows[s, g, d, j]; each used entry is named once. The -1 entries of a device come last, the rows from one sender stand together, and some device of each group has no -1 entry. Sender 8 - 1 fills its whole slot for every device that it serves.
All inputs are finite; a program needn't handle non-finite values.
Results may differ from a plain program's by a relative error of at most 0.003.
Values may be sent and summed in bfloat16 or wider, within the bound.
No kernel may reach another device: no remote copies, remote signals or barrier semaphores. Data moves between devices by JAX's collectives and lax.ppermute only.
A program may use at most 64 MiB of HBM per device.

v0:
```python
import jax
import jax.numpy as jnp
from jax import lax
from jax.sharding import PartitionSpec as P


def spread_conv(source_field, kernel_taps, tap_weights):
    tap_count = kernel_taps.shape[0]
    half_width = tap_count // 2
    step_count = source_field.shape[0]
    padded = jnp.pad(source_field, ((half_width, half_width), (0, 0)))
    summed = jnp.zeros_like(source_field)
    for offset in range(tap_count):
        summed = summed + kernel_taps[offset] * (
            tap_weights[:, offset : offset + 1] * padded[offset : offset + step_count]
        )
    return summed


def build_mask(live_steps, utterances, tap_count):
    half_width = tap_count // 2
    step_count = live_steps.shape[0]
    live_pad = jnp.pad(live_steps, (half_width, half_width))
    utter_pad = jnp.pad(utterances, (half_width, half_width), constant_values=-1)
    columns = []
    for offset in range(tap_count):
        columns.append(
            live_steps
            & live_pad[offset : offset + step_count]
            & (utterances == utter_pad[offset : offset + step_count])
        )
    return jnp.stack(columns, axis=1).astype(jnp.float32)


def layer_terms(encoded, live_steps, utterances, grad_above, gain, kernel):
    tap_count = kernel.shape[0]
    half_width = tap_count // 2
    step_count = encoded.shape[0]
    tap_weights = build_mask(live_steps, utterances, tap_count)
    row_mean = jnp.mean(encoded, axis=1, keepdims=True)
    centered = encoded - row_mean
    row_var = jnp.mean(centered * centered, axis=1, keepdims=True)
    inv_std = lax.rsqrt(row_var + 1e-05)
    normalized = centered * inv_std
    gain_f32 = gain.astype(jnp.float32)
    kernel_taps = kernel.astype(jnp.float32)
    normed = normalized * gain_f32
    conv_out = spread_conv(normed, kernel_taps, tap_weights)
    gate_sig = jax.nn.sigmoid(conv_out)
    output = encoded + conv_out * gate_sig
    scale = (encoded.shape[0] * encoded.shape[1]) ** (-0.5)
    grad_out = (
        jnp.where(live_steps[:, None], grad_above.astype(jnp.float32), jnp.zeros((), jnp.float32))
        * scale
    )
    device_loss = jnp.sum(output * grad_out)
    grad_conv = grad_out * (gate_sig * (1.0 + conv_out * (1.0 - gate_sig)))
    grad_normed = spread_conv(grad_conv, kernel_taps[::-1], tap_weights)
    padded = jnp.pad(normed, ((half_width, half_width), (0, 0)))
    grad_taps = jnp.stack(
        [
            jnp.sum(
                grad_conv
                * tap_weights[:, offset : offset + 1]
                * padded[offset : offset + step_count],
                axis=0,
            )
            for offset in range(tap_count)
        ]
    )
    grad_scale = jnp.sum(grad_normed * normalized, axis=0)
    grad_hat = grad_normed * gain_f32
    grad_x = grad_out + inv_std * (
        grad_hat
        - jnp.mean(grad_hat, axis=1, keepdims=True)
        - normalized * jnp.mean(grad_hat * normalized, axis=1, keepdims=True)
    )
    return (device_loss, grad_x.astype(jnp.bfloat16), grad_taps, grad_scale)


def per_device(cached, send_rows, take_rows, utt_index, upstream, in_proj, norm_gain, conv_kernel):
    cache_rows = cached[0, 0]
    wanted = send_rows[0, 0]
    outgoing = jnp.where(
        (wanted >= 0)[:, :, None],
        cache_rows[jnp.maximum(wanted, 0)],
        jnp.zeros((), cache_rows.dtype),
    )
    proj_full, taps_full, gain_full = (
        lax.all_gather(in_proj, "fsdp", axis=1, tiled=True),
        lax.all_gather(conv_kernel, "fsdp", axis=1, tiled=True),
        lax.all_gather(norm_gain[None, :], "fsdp", axis=1, tiled=True),
    )
    take_list = take_rows[0, 0]
    is_live = take_list >= 0
    safe_index = jnp.maximum(take_list, 0)
    pair_count = take_list.shape[0]
    step_width = cache_rows.shape[1] // 2
    arrived = lax.all_to_all(outgoing, "dp", split_axis=0, concat_axis=0, tiled=True)
    flat_rows = arrived.reshape(-1, arrived.shape[2])
    work_rows = jnp.where(is_live[:, None], flat_rows[safe_index], jnp.zeros((), flat_rows.dtype))
    frames = work_rows.reshape(2 * pair_count, step_width)
    encoded = jnp.dot(frames, proj_full, preferred_element_type=jnp.float32)
    live_steps = jnp.repeat(is_live, 2)
    utterances = jnp.repeat(utt_index[0, 0], 2)
    device_loss, grad_x, grad_taps, grad_scale = layer_terms(
        encoded, live_steps, utterances, upstream[0, 0], gain_full[0], taps_full
    )
    grad_weight = lax.dot_general(
        frames, grad_x, (((0,), (0,)), ((), ())), preferred_element_type=jnp.float32
    )
    shard_cols = in_proj.shape[1]
    totals = lax.psum((grad_weight, grad_taps, grad_scale[None, :]), ("dp", "fsdp"))
    col_start = lax.axis_index("fsdp") * shard_cols
    weight_part, taps_part, scale_part = [
        lax.dynamic_slice_in_dim(summed_item, col_start, shard_cols, 1) for summed_item in totals
    ]
    return (weight_part, taps_part, scale_part[0], device_loss.reshape(1, 1))


def solution(mesh):
    placed = (
        P("dp", "fsdp", None, None),
        P("dp", "fsdp", None, None),
        P("dp", "fsdp", None),
        P("dp", "fsdp", None),
        P("dp", "fsdp", None, None),
        P(None, "fsdp"),
        P("fsdp"),
        P(None, "fsdp"),
    )
    return jax.shard_map(
        per_device,
        mesh=mesh,
        in_specs=placed,
        out_specs=(P(None, "fsdp"), P(None, "fsdp"), P("fsdp"), P("dp", "fsdp")),
        check_vma=False,
    )
```

profile of v0, /device:TPU:0, one launch (start us, length us, event | category | flops | bytes accessed | tf_op | source)
XLA Modules:
  0.0 283.5 jit_solution(2864807368790773936)
XLA Ops:
  7.2 0.0 copy-start
  7.2 0.0 all-gather.4.cloned.1.call-start
  7.2 0.7 all-gather.4.cloned.1.call-update
  7.9 0.7 broadcast_maximum_fusion
  8.6 0.7 compare_bitcast_fusion
  9.3 0.1 reshape.100
  9.4 0.0 copy-done
  9.4 2.1 gather_fusion
  11.4 0.0 copy-start.5
  11.5 0.0 copy-start.3
  11.5 0.0 copy-start.4
  11.5 0.0 copy-start.2
  11.5 1.1 broadcast_select_fusion
  12.6 7.3 %all-to-all-start = ((bf16[8,64,1024]{2,1,0:T(8,128)(2,1)}), bf16[8,64,1024]{2,1,0:T(8,128)(2,1)S(1)}, u32[]{:S(2)}, u32[]{:S(2)}) async-start(bf16[8,64,1024]{2,1,0:T(8,128)(2,1)} %broadcast_select_fusion), calls=%async_computation | async-start | bytes 2097152 | tf_op jit(solution)/shard_map/all_to_all | solution.py:99
  19.9 0.0 all-reduce.7.cloned.1.call-start
  19.9 0.0 copy-done.5
  19.9 0.1 broadcast_in_dim.62
  20.0 0.2 broadcast_in_dim.63
  20.2 0.0 copy-done.3
  20.2 0.1 broadcast_in_dim.70
  20.3 0.1 reshape.94
  20.5 0.1 fusion.58
  20.7 0.1 fusion.50
  20.9 0.1 fusion.42
  21.1 0.1 fusion.66
  21.2 0.1 broadcast_in_dim.71
  21.3 0.2 and.227
  21.5 0.2 stack.220
  21.7 0.0 copy-done.4
  21.7 5.2 %all-gather.1 = bf16[4,1,384]{2,1,0:T(2,128)(2,1)S(1)} all-gather(bf16[1,1,384]{2,1,0:T(2,128)(2,1)S(1)} %reshape.120), channel_id=2, replica_groups=mesh['dp'=8,'fsdp'=4] {'fsdp'}, dimensions={0}, use_global_device_ids=true | all-gather | bytes 3840 | tf_op jit(solution)/shard_map/all_gather | solution.py:92
  26.9 0.0 copy-done.2
  26.9 5.3 %all_gather.10 = bf16[31,1536]{1,0:T(8,128)(2,1)S(1)} all-gather(bf16[31,384]{1,0:T(8,128)(2,1)S(1)} %copy-done.2), channel_id=1, replica_groups=mesh['dp'=8,'fsdp'=4] {'fsdp'}, dimensions={1}, use_global_device_ids=true | all-gather | bytes 119040 | tf_op jit(solution)/shard_map/all_gather | solution.py:91
  32.3 0.2 slice_reduce_fusion.29
  32.5 0.3 slice_reduce_fusion.30
  32.9 12.8 %all-to-all-done = bf16[8,64,1024]{2,1,0:T(8,128)(2,1)S(1)} async-done(((bf16[8,64,1024]{2,1,0:T(8,128)(2,1)}), bf16[8,64,1024]{2,1,0:T(8,128)(2,1)S(1)}, u32[]{:S(2)}, u32[]{:S(2)}) %all-to-all-start) | async-done | bytes 1048608 | tf_op jit(solution)/shard_map/all_to_all | solution.py:99
  45.6 1.2 gather_fusion.1
  46.8 0.2 gather.10
  47.0 0.0 all-gather.4.cloned.1.call-done
  47.0 2.5 fusion.109
  49.5 0.5 multiply_reduce_fusion.33
  50.0 0.0 copy-start.1
  50.0 0.5 fusion.8
  50.5 0.9 copy-done.1
  51.4 31.9 %multiply_reduce_fusion.1 = (f32[1536]{0:T(1024)S(1)}, f32[1536]{0:T(1024)S(1)}, f32[1536]{0:T(1024)S(1)}, f32[1536]{0:T(1024)S(1)}, f32[1536]{0:T(1024)S(1)}, /...) fusion(f32[512,1536]{1,0:T(8,128)S(1)} %fusion.8, ...), kind=kLoop, calls=%fused_computation.10 | loop fusion | flops 102222336 | bytes 11319808 | tf_op jit(solution)/shard_map/reduce_sum | solution.py:62
  83.3 6.8 %multiply_reduce_fusion.10 = (f32[1536]{0:T(1024)S(1)}, f32[1536]{0:T(1024)S(1)}, f32[1536]{0:T(1024)S(1)}, f32[1536]{0:T(1024)S(1)}, f32[1536]{0:T(1024)S(1)}, ...) fusion(f32[512,1536]{1,0:T(8,128)S(1)} %get-tuple-element.72, ...), kind=kLoop, calls=%fused_computation.19 | loop fusion | flops 21219840 | bytes 6365184 | tf_op jit(solution)/shard_map/reduce_sum | solution.py:62
  90.1 6.6 %multiply_reduce_fusion.16 = (f32[1536]{0:T(1024)S(1)}, f32[1536]{0:T(1024)S(1)}, f32[1536]{0:T(1024)S(1)}, f32[1536]{0:T(1024)S(1)}, f32[1536]{0:T(1024)S(1)}, ...) fusion(f32[512,1536]{1,0:T(8,128)S(1)} %fusion.8, ...), kind=kLoop, calls=%fused_computation.25 | loop fusion | flops 21219840 | bytes 6365184 | tf_op jit(solution)/shard_map/reduce_sum | solution.py:62
  96.7 3.1 %multiply_reduce_fusion.20 = (f32[1536]{0:T(1024)S(1)}, f32[1536]{0:T(1024)S(1)}, f32[1536]{0:T(1024)S(1)}, f32[1536]{0:T(1024)S(1)}) fusion(f32[512,1536]{1,0:T(8,128)S(1)} %get-tuple-element.72, f32[512,1536]{1,0:T(8,128)S(1)} %fusion.8, f32[512]{0:T(512)S(1)} %bitcast.59, f32[512]{0:T(512)S(1)} %bitcast.62, f32[512]{0:T(512)S(1)} %bitcast.65, ...), kind=kLoop, calls=%fused_computation.29 | loop fusion | flops 9431040 | bytes 6324224 | tf_op jit(solution)/shard_map/reduce_sum | solution.py:62
  100.2 28.3 %multiply_reduce_fusion = (f32[1536]{0:T(1024)S(1)}, f32[512]{0:T(512)S(1)}, f32[512]{0:T(512)S(1)}, f32[]{:T(128)}, f32[512,1536]{1,0:T(8,128)S(1)}) fusion(f32[512,1536]{1,0:T(8,128)S(1)} %get-tuple-element.137, f32[512]{0:T(512)S(1)} %add_rsqrt_fusion, f32[512]{0:T(512)S(1)} %broadcast_multiply_fusion.2, f32[1536]{0:T(1024)S(1)} %reshape.122, ...), kind=kLoop, calls=%fused_computation.9 | loop fusion | flops 86504960 | bytes 14430724 | tf_op jit(solution)/shard_map/reduce_sum | solution.py:71
  128.5 3.6 %fusion.9 = f32[512,1536]{1,0:T(8,128)} fusion(f32[512,1536]{1,0:T(8,128)S(1)} %get-tuple-element.74, f32[512,1536]{1,0:T(8,128)S(1)} %get-tuple-element.137, bf16[1,1,512,1536]{3,2,1,0:T(8,128)(2,1)S(1)} %copy-done.1, f32[1536]{0:T(1024)S(1)} %reshape.122, f32[512]{0:T(512)S(1)} %get-tuple-element.138, f32[512]{0:T(512)S(1)} %get-tuple-element.139, ...), kind=kOutput, calls=%fused_computation.52 | convolution fusion | flops 815005696 | bytes 11549184 | tf_op jit(solution)/shard_map/dot_general | solution.py:109
  132.1 2.8 stack.252
  134.8 0.0 all-reduce.7.cloned.1.call-update
  134.9 38.2 %psum.23 = f32[1,1536]{1,0:T(1,128)S(1)} all-reduce(f32[1,1536]{1,0:T(1,128)S(1)} %broadcast_in_dim.73), channel_id=1, replica_groups=mesh['dp'=8,'fsdp'=4] {'dp','fsdp'}, use_global_device_ids=true, to_apply=%region_38.39 | all-reduce | flops 1536 | bytes 12288 | tf_op jit(solution)/shard_map/psum | solution.py:113
  173.1 0.6 dynamic-slice_reduce_fusion
  173.7 99.5 %all-reduce.7.cloned.1.call-done = (f32[512,1536]{1,0:T(8,128)}, f32[31,1536]{1,0:T(8,128)}) async-done(((f32[512,1536]{1,0:T(8,128)}, f32[31,1536]{1,0:T(8,128)}), (f32[512,1536]{1,0:T(8,128)}, f32[31,1536]{1,0:T(8,128)})) %all-reduce.7.cloned.1.call-update) | async-done | bytes 3336208 | tf_op jit(solution)/shard_map/psum | solution.py:113
  273.1 2.1 constant_dynamic-slice_fusion.1
  275.2 1.4 constant_dynamic-slice_fusion
  (77 shorter events, 0.6 us)
Async XLA Ops:
  7.2 2.2 copy-start
  7.2 39.8 %all-gather.4.cloned.1.call-start = ((), (), s32[]{:S(2)}) async-start(), calls=%async_computation.1 | async-start | bytes 1966080 | tf_op jit(solution)/shard_map/all_gather | solution.py:90
  11.4 8.5 %copy-start.5 = (s32[1,1,256]{2,1,0:T(1,128)S(1)}, s32[1,1,256]{2,1,0:T(1,128)}, u32[]{:S(2)}) copy-start(s32[1,1,256]{2,1,0:T(1,128)} %param.10) | copy-start | bytes 3076
  11.5 8.7 %copy-start.3 = (s32[1,1,256]{2,1,0:T(1,128)S(1)}, s32[1,1,256]{2,1,0:T(1,128)}, u32[]{:S(2)}) copy-start(s32[1,1,256]{2,1,0:T(1,128)} %param.11) | copy-start | bytes 3076
  11.5 10.2 %copy-start.4 = (bf16[384]{0:T(512)(128)(2,1)S(1)}, bf16[384]{0:T(512)(128)(2,1)}, u32[]{:S(2)}) copy-start(bf16[384]{0:T(512)(128)(2,1)} %param.14) | copy-start | bytes 2308
  11.5 15.4 %copy-start.2 = (bf16[31,384]{1,0:T(8,128)(2,1)S(1)}, bf16[31,384]{1,0:T(8,128)(2,1)}, u32[]{:S(2)}) copy-start(bf16[31,384]{1,0:T(8,128)(2,1)} %param.15) | copy-start | bytes 71428
  12.6 33.0 %all-to-all-start = ((bf16[8,64,1024]{2,1,0:T(8,128)(2,1)}), bf16[8,64,1024]{2,1,0:T(8,128)(2,1)S(1)}, u32[]{:S(2)}, u32[]{:S(2)}) async-start(bf16[8,64,1024]{2,1,0:T(8,128)(2,1)} %broadcast_select_fusion), calls=%async_computation | async-start | bytes 2097152 | tf_op jit(solution)/shard_map/all_to_all | solution.py:99
  19.9 253.3 %all-reduce.7.cloned.1.call-start = ((), (), s32[]{:S(2)}) async-start(), calls=%async_computation.2 | async-start | bytes 6684672 | tf_op jit(solution)/shard_map/psum | solution.py:113
  50.0 1.4 copy-start.1
Sparse Core Ops, SparseCore 0:
  9.6 22.3 all-gather.3
  135.0 138.1 all-reduce.6
where the time goes:
time: 284 us; the launch traced here: 283 us
  waiting for transfers between devices  113 us (40%)
  other arithmetic  80.5 us (28%)
  blocking collectives  48.7 us (17%)
  between operations  14.7 us (5%)
  local copies, waits for them, and re-layouts  13.2 us (5%)
  starting transfers between devices  7.33 us (3%)
  matrix products  6.1 us (2%)
    psum x1, waiting for transfers between devices, per_device(): lax.psum((grad_weight, grad_taps, grad_scale[None, :]), ('dp', 'fsdp'))  99.5 us
    reduce_sum x4, other arithmetic, layer_terms(): jnp.sum(grad_conv * tap_weights[:, offset:offset + 1] * padded[offset:off...  48.3 us
    psum x1, blocking collectives, per_device(): lax.psum((grad_weight, grad_taps, grad_scale[None, :]), ('dp', 'fsdp'))  38.2 us
    reduce_sum x1, other arithmetic, layer_terms(): grad_scale = jnp.sum(grad_normed * normalized, axis=0)  28.3 us
    all_to_all x1, waiting for transfers between devices, per_device(): lax.all_to_all(outgoing, 'dp', split_axis=0, concat_axis=0, tiled=True)  12.8 us
    all_to_all x1, starting transfers between devices, per_device(): lax.all_to_all(outgoing, 'dp', split_axis=0, concat_axis=0, tiled=True)  7.25 us
  transfers between devices with their start and end apart: 3, of which 2 were waited for; matrix products, arithmetic and copies ran while one was open for 3% of the time, Pallas kernels for 0%

commit v1 on v0

v1 whole, which is shorter than its diff:
```python
import functools
import math

import jax
import jax.numpy as jnp
import numpy as np
from jax import lax
from jax.experimental import pallas as pl
from jax.experimental.pallas import tpu as pltpu
from jax.sharding import PartitionSpec as P

GAP = 16
POINTS = 256
FREQS = 128
STARTS = (0, 224, 432)
LENGTHS = (224, 208, 224)
BLOCK_STEPS = ((0, 208), (128, 384), (304, 512))
WIDE_STEPS = ((0, 224), (112, 400), (288, 512))
BLOCK_K = ((208, 208, 224), (256, 256, 256), (208, 208, 224))
WIDE_K = ((224, 224, 320), (288, 288, 320), (224, 224, 320))
AHEAD_AT = tuple(int(v) for v in np.cumsum([0] + [sum(k) for k in WIDE_K + BLOCK_K]))
BEHIND_AT = tuple(int(v) for v in np.cumsum([0] + [b - a for a, b in WIDE_STEPS + BLOCK_STEPS]))
CH = 256
ROWS = 64
F32 = jnp.float32
BF16 = jnp.bfloat16
VMEM_LIMIT = 40 * 1024 * 1024


def k_slices(steps, sizes):
    out = []
    for size in sizes:
        first = steps[0] if steps[0] + size <= 512 else 512 - size
        out.append((first, first + size))
    return out


def split(value):
    hi = value.astype(BF16)
    return hi, (value - hi.astype(F32)).astype(BF16)


def split_np(value):
    hi = value.astype(jnp.bfloat16)
    lo = (value - hi.astype(np.float64)).astype(jnp.bfloat16)
    return hi, lo


def transforms(tap_count):
    omega = 2 * np.pi * (np.arange(FREQS) + 0.5) / POINTS
    angle = omega[:, None] * np.arange(POINTS)[None, :]
    forward = np.concatenate([np.cos(angle), -np.sin(angle)], axis=0)
    f_hi, f_lo = split_np(forward)
    back = np.concatenate([f_hi.T, f_lo.T, f_hi.T], axis=1)
    shift = omega[:, None] * (np.arange(32) - tap_count // 2)[None, :]
    tap_ok = (np.arange(32) < tap_count)[None, :]
    taps = np.concatenate([np.cos(shift), np.sin(shift)], axis=0) * tap_ok / FREQS
    t_hi, t_lo = split_np(taps)
    tap_fwd = np.concatenate([t_hi, t_lo], axis=1)
    lag = np.concatenate([np.cos(shift), -np.sin(shift)], axis=0) * tap_ok / FREQS
    l_hi, l_lo = split_np(lag.T)
    lags = np.concatenate([l_hi, l_lo, l_hi], axis=1)
    return f_hi, f_lo, back, tap_fwd, lags


def dot(a, b):
    return jnp.dot(a, b, preferred_element_type=F32)


def dot_t(a, b):
    return lax.dot_general(a, b, (((0,), (0,)), ((), ())), preferred_element_type=F32)


def pick_kernel(index_ref, rows_ref, out_ref):
    count = rows_ref.shape[0]
    total = index_ref.shape[1]
    number = lax.broadcasted_iota(jnp.int32, (count, total), 0)
    choose = jnp.where(number == index_ref[...], 1.0, 0.0).astype(BF16)
    out_ref[...] = dot_t(choose, rows_ref[...]).astype(BF16)


def prep_kernel(pos_ref, hi_ref, lo_ref, back_ref, ahead_ref, behind_ref):
    f_hi = hi_ref[...]
    f_lo = lo_ref[...]
    back = back_ref[...]
    for part in range(6):
        sizes = (WIDE_K + BLOCK_K)[part]
        steps = (WIDE_STEPS + BLOCK_STEPS)[part]
        total = sum(sizes)
        place = pos_ref[part : part + 1, :total]
        number = lax.broadcasted_iota(jnp.int32, (POINTS, total), 0)
        hot = jnp.where(number == place, 1.0, 0.0).astype(BF16)
        lane = lax.broadcasted_iota(jnp.int32, (1, total), 1)
        middle = (lane >= sizes[0]) & (lane < sizes[0] + sizes[1])
        ahead = jnp.where(middle, dot(f_lo, hot), dot(f_hi, hot)).astype(BF16)
        ahead_ref[:, AHEAD_AT[part] : AHEAD_AT[part + 1]] = ahead
        held = steps[1] - steps[0]
        padded = -(-held // 128) * 128
        wide = dot_t(hot[:, :padded], back)
        behind_ref[BEHIND_AT[part] : BEHIND_AT[part + 1]] = wide[:held].astype(BF16)


def layer_kernel(
    core_ref, arrived_ref, take_ref, tapf_ref, lag_ref, params_hbm, up_hbm, ahead_hbm, behind_hbm,
    keep_ref, send_ref, loss_ref,
    params_ref, up_ref, ahead_ref, behind_ref, sems,
    frames_ref, frames_t_ref, x_ref, h_ref, stat_ref, acc_ref, acc2_ref,
    hi_ref, lo_ref, ghi_ref, glo_ref, spec_ref, nspec_ref, phi_ref, plo_ref,
    coef_ref, c_ref, small_ref, lossacc_ref,
):
    copies = [
        pltpu.make_async_copy(source, target, sems.at[k])
        for k, (source, target) in enumerate(
            ((params_hbm, params_ref), (ahead_hbm, ahead_ref), (behind_hbm, behind_ref), (up_hbm, up_ref))
        )
    ]
    for copy in copies:
        copy.start()
    steps, width = up_ref.shape
    slots, pair_width = arrived_ref.shape
    depth = pair_width // 2
    chunks = width // CH
    scale = (steps * width) ** -0.5
    tiles = [slice(r, r + ROWS) for r in range(0, steps, ROWS)]
    wide_of = [slice(AHEAD_AT[j], AHEAD_AT[j + 1]) for j in range(3)]
    block_of = [slice(AHEAD_AT[j], AHEAD_AT[j + 1]) for j in range(3, 6)]
    back_wide = [slice(BEHIND_AT[j], BEHIND_AT[j + 1]) for j in range(3)]
    back_block = [slice(BEHIND_AT[j], BEHIND_AT[j + 1]) for j in range(3, 6)]

    take = take_ref[...]
    number = lax.broadcasted_iota(jnp.int32, (slots, steps), 0)
    odd = lax.broadcasted_iota(jnp.int32, (slots, steps), 1) % 2
    here = number == take
    even_hot = jnp.where(here & (odd == 0), 1.0, 0.0).astype(BF16)
    odd_hot = jnp.where(here & (odd == 1), 1.0, 0.0).astype(BF16)
    frames = dot_t(even_hot, arrived_ref[:, :depth]) + dot_t(odd_hot, arrived_ref[:, depth:])
    frames_ref[...] = frames.astype(BF16)
    frames_t_ref[...] = jnp.transpose(frames).astype(BF16)
    live = dot_t(even_hot + odd_hot, jnp.ones((slots, 128), BF16))
    stat_ref[2] = live * scale

    acc_ref[...] = jnp.zeros_like(acc_ref)
    copies[0].wait()

    def project(i, carry):
        cols = pl.ds(pl.multiple_of(i * CH, CH), CH)
        x = dot(frames_ref[...], params_ref[:depth, cols])
        x_ref[:, cols] = x
        acc_ref[...] += x[:, :128] + x[:, 128:]
        return carry

    lax.fori_loop(0, chunks, project, 0)
    mean = jnp.sum(acc_ref[...], axis=1, keepdims=True) * (1.0 / width)
    stat_ref[0] = jnp.broadcast_to(mean, (steps, 128))

    for rows in tiles:
        m = stat_ref[0, rows]
        total = jnp.zeros((ROWS, 128), F32)
        for k in range(width // 128):
            d = x_ref[rows, k * 128 : (k + 1) * 128] - m
            total = total + d * d
        var = jnp.sum(total, axis=1, keepdims=True) * (1.0 / width)
        stat_ref[1, rows] = jnp.broadcast_to(lax.rsqrt(var + 1e-05), (ROWS, 128))

    acc_ref[...] = jnp.zeros_like(acc_ref)
    acc2_ref[...] = jnp.zeros_like(acc2_ref)
    lossacc_ref[...] = jnp.zeros_like(lossacc_ref)

    for copy in copies[1:]:
        copy.wait()

    def twice(value):
        return jnp.concatenate([value, value], axis=1)

    def stack(hi, lo, slices):
        (a, b), (c, d), (e, f) = slices
        return jnp.concatenate([hi[a:b], hi[c:d], lo[e:f]], axis=0)

    def middle(i, carry):
        cols = pl.ds(pl.multiple_of(i * CH, CH), CH)
        gain = params_ref[depth + 16 : depth + 32, cols][15:16].astype(F32)
        taps = params_ref[depth : depth + 32, cols]
        coef_ref[...] = dot(tapf_ref[...], jnp.concatenate([taps, taps], axis=0))
        for rows in tiles:
            xhat = (x_ref[rows, cols] - twice(stat_ref[0, rows])) * twice(stat_ref[1, rows])
            hi, lo = split(xhat * gain)
            hi_ref[rows] = hi
            lo_ref[rows] = lo
        for j in range(3):
            nspec_ref[j] = dot(ahead_ref[:, block_of[j]], stack(hi_ref, lo_ref, k_slices(BLOCK_STEPS[j], BLOCK_K[j])))
        for j in range(3):
            for f in range(0, FREQS, 32):
                lower, upper = slice(f, f + 32), slice(FREQS + f, FREQS + f + 32)
                re, im = nspec_ref[j, lower], nspec_ref[j, upper]
                cre, cim = coef_ref[lower], coef_ref[upper]
                hi, lo = split(re * cre - im * cim)
                phi_ref[j, lower] = hi
                plo_ref[j, lower] = lo
                hi, lo = split(re * cim + im * cre)
                phi_ref[j, upper] = hi
                plo_ref[j, upper] = lo
        parts = [
            dot(behind_ref[back_wide[j]], jnp.concatenate([phi_ref[j], phi_ref[j], plo_ref[j]], axis=0))
            for j in range(3)
        ]
        c_ref[0:112] = parts[0][0:112]
        c_ref[112:224] = parts[0][112:224] + parts[1][0:112]
        c_ref[224:288] = parts[1][112:176]
        c_ref[288:400] = parts[1][176:288] + parts[2][0:112]
        c_ref[400:512] = parts[2][112:224]
        loss = jnp.zeros((1, CH), F32)
        for rows in tiles:
            conv = c_ref[rows]
            sig = jax.nn.sigmoid(conv)
            go = up_ref[rows, cols].astype(F32) * twice(stat_ref[2, rows])
            out = x_ref[rows, cols] + conv * sig
            loss = loss + jnp.sum(out * go, axis=0, keepdims=True)
            hi, lo = split(go * (sig * (1.0 + conv * (1.0 - sig))))
            ghi_ref[rows] = hi
            glo_ref[rows] = lo
        lossacc_ref[...] += loss
        for j in range(3):
            spec_ref[j] = dot(ahead_ref[:, wide_of[j]], stack(ghi_ref, glo_ref, k_slices(WIDE_STEPS[j], WIDE_K[j])))
        for f in range(0, FREQS, 32):
            lower, upper = slice(f, f + 32), slice(FREQS + f, FREQS + f + 32)
            cre, cim = coef_ref[lower], coef_ref[upper]
            zre = jnp.zeros((32, CH), F32)
            zim = jnp.zeros((32, CH), F32)
            for j in range(3):
                nre, nim = nspec_ref[j, lower], nspec_ref[j, upper]
                re, im = spec_ref[j, lower], spec_ref[j, upper]
                zre = zre + (nre * re + nim * im)
                zim = zim + (nim * re - nre * im)
                hi, lo = split(re * cre + im * cim)
                phi_ref[j, lower] = hi
                plo_ref[j, lower] = lo
                hi, lo = split(im * cre - re * cim)
                phi_ref[j, upper] = hi
                plo_ref[j, upper] = lo
            hi, lo = split(zre)
            phi_ref[3, lower] = hi
            plo_ref[3, lower] = lo
            hi, lo = split(zim)
            phi_ref[3, upper] = hi
            plo_ref[3, upper] = lo
        tap_grad = dot(lag_ref[...], jnp.concatenate([phi_ref[3], phi_ref[3], plo_ref[3]], axis=0))
        parts = [
            dot(behind_ref[back_block[j]], jnp.concatenate([phi_ref[j], phi_ref[j], plo_ref[j]], axis=0))
            for j in range(3)
        ]
        c_ref[0:128] = parts[0][0:128]
        c_ref[128:208] = parts[0][128:208] + parts[1][0:80]
        c_ref[208:304] = parts[1][80:176]
        c_ref[304:384] = parts[1][176:256] + parts[2][0:80]
        c_ref[384:512] = parts[2][80:208]
        gain_grad = jnp.zeros((1, CH), F32)
        for rows in tiles:
            gn = c_ref[rows]
            xhat = (x_ref[rows, cols] - twice(stat_ref[0, rows])) * twice(stat_ref[1, rows])
            gain_grad = gain_grad + jnp.sum(gn * xhat, axis=0, keepdims=True)
            h = gn * gain
            hx = h * xhat
            h_ref[rows, cols] = h
            acc_ref[rows] += h[:, :128] + h[:, 128:]
            acc2_ref[rows] += hx[:, :128] + hx[:, 128:]
        last = lax.broadcasted_iota(jnp.int32, (32, CH), 0) == 31
        small_ref[:, cols] = jnp.where(last, gain_grad, tap_grad)
        return carry

    lax.fori_loop(0, chunks, middle, 0)
    loss_ref[...] = jnp.sum(lossacc_ref[...], axis=1, keepdims=True)
    for rows in tiles:
        m1 = jnp.sum(acc_ref[rows], axis=1, keepdims=True) * (1.0 / width)
        m2 = jnp.sum(acc2_ref[rows], axis=1, keepdims=True) * (1.0 / width)
        acc_ref[rows] = jnp.broadcast_to(m1, (ROWS, 128))
        acc2_ref[rows] = jnp.broadcast_to(m2, (ROWS, 128))

    halves, filled_to, _ = keep_ref.shape
    per_block = width // (2 * halves) // 128
    held = depth + 32

    def finish(core):
        for i in range(chunks):
            cols = slice(i * CH, (i + 1) * CH)
            for rows in tiles:
                inv = twice(stat_ref[1, rows])
                xhat = (x_ref[rows, cols] - twice(stat_ref[0, rows])) * inv
                go = up_ref[rows, cols].astype(F32) * twice(stat_ref[2, rows])
                inner = h_ref[rows, cols] - twice(acc_ref[rows]) - xhat * twice(acc2_ref[rows])
                hi_ref[rows] = (go + inv * inner).astype(BF16)
            weight = dot(frames_t_ref[...], hi_ref[...])
            for half in range(CH // 128):
                tile = i * (CH // 128) + half
                block, inside = tile // per_block, (tile % per_block) * held
                lanes = slice(half * 128, half * 128 + 128)
                small = small_ref[:, tile * 128 : (tile + 1) * 128]
                target = keep_ref if block % 2 == core else send_ref
                target[block // 2, inside : inside + depth] = weight[:, lanes]
                target[block // 2, inside + depth : inside + held] = small

    pl.when(core_ref[0, 0] == 0)(lambda: finish(0))
    pl.when(core_ref[0, 0] != 0)(lambda: finish(1))
    filled = per_block * held
    if filled_to > filled:
        for half in range(halves):
            for ref in (keep_ref, send_ref):
                ref[half, filled:] = jnp.zeros((filled_to - filled, 128), F32)


def vmem(count):
    return [pl.BlockSpec(memory_space=pltpu.VMEM)] * count


def pick(index, rows):
    total = index.shape[1]
    return pl.pallas_call(
        pick_kernel,
        out_shape=jax.ShapeDtypeStruct((total, rows.shape[1]), BF16),
        in_specs=vmem(2),
        out_specs=vmem(1)[0],
        compiler_params=pltpu.CompilerParams(vmem_limit_bytes=VMEM_LIMIT),
        cost_estimate=pl.CostEstimate(
            flops=2 * total * rows.size, bytes_accessed=6 * rows.size, transcendentals=0
        ),
        name="pick_rows",
    )(index, rows)


def positions(utterances):
    steps = utterances.shape[0]
    place = jnp.arange(steps, dtype=jnp.int32) + GAP * utterances
    most = max(sum(sizes) for sizes in WIDE_K + BLOCK_K)
    lines = []
    for kind, (ranges, sizes_of) in enumerate(((WIDE_STEPS, WIDE_K), (BLOCK_STEPS, BLOCK_K))):
        for j in range(3):
            local = place - (STARTS[j] - GAP)
            low, high = (0, LENGTHS[j] + 2 * GAP) if kind == 0 else (GAP, LENGTHS[j] + GAP)
            local = jnp.where((local >= low) & (local < high), local, -1)
            inside = jnp.arange(steps)
            local = jnp.where((inside >= ranges[j][0]) & (inside < ranges[j][1]), local, -1)
            pieces = [local[a:b] for a, b in k_slices(ranges[j], sizes_of[j])]
            line = jnp.concatenate(pieces)
            lines.append(jnp.pad(line, (0, most - line.shape[0]), constant_values=-1))
    lines.extend([jnp.full((most,), -1, jnp.int32)] * 2)
    return jnp.stack(lines)


def prepare(utterances, f_hi, f_lo, back):
    shapes = [
        jax.ShapeDtypeStruct((POINTS, AHEAD_AT[-1]), BF16),
        jax.ShapeDtypeStruct((BEHIND_AT[-1], 3 * POINTS), BF16),
    ]
    return pl.pallas_call(
        prep_kernel,
        out_shape=shapes,
        in_specs=vmem(4),
        out_specs=vmem(2),
        compiler_params=pltpu.CompilerParams(vmem_limit_bytes=VMEM_LIMIT),
        cost_estimate=pl.CostEstimate(flops=3 * 10**9, bytes_accessed=8 * 10**6, transcendentals=0),
        name="prepare_transforms",
    )(positions(utterances), f_hi, f_lo, back)


def layer(core, arrived, take, params, upstream, tap_fwd, lags, ahead, behind, out_rows, halves):
    steps, width = upstream.shape
    depth = arrived.shape[1] // 2
    hbm = pl.BlockSpec(memory_space=pltpu.HBM)
    scratch = [
        pltpu.VMEM(params.shape, BF16),
        pltpu.VMEM(upstream.shape, BF16),
        pltpu.VMEM(ahead.shape, BF16),
        pltpu.VMEM(behind.shape, BF16),
        pltpu.SemaphoreType.DMA((4,)),
        pltpu.VMEM((steps, depth), BF16),
        pltpu.VMEM((depth, steps), BF16),
        pltpu.VMEM((steps, width), F32),
        pltpu.VMEM((steps, width), F32),
        pltpu.VMEM((3, steps, 128), F32),
        pltpu.VMEM((steps, 128), F32),
        pltpu.VMEM((steps, 128), F32),
        pltpu.VMEM((steps, CH), BF16),
        pltpu.VMEM((steps, CH), BF16),
        pltpu.VMEM((steps, CH), BF16),
        pltpu.VMEM((steps, CH), BF16),
        pltpu.VMEM((3, POINTS, CH), F32),
        pltpu.VMEM((3, POINTS, CH), F32),
        pltpu.VMEM((4, POINTS, CH), BF16),
        pltpu.VMEM((4, POINTS, CH), BF16),
        pltpu.VMEM((POINTS, CH), F32),
        pltpu.VMEM((steps, CH), F32),
        pltpu.VMEM((32, width), F32),
        pltpu.VMEM((1, CH), F32),
    ]
    return pl.pallas_call(
        layer_kernel,
        out_shape=[
            jax.ShapeDtypeStruct((halves, out_rows, 128), F32),
            jax.ShapeDtypeStruct((halves, out_rows, 128), F32),
            jax.ShapeDtypeStruct((1, 1), F32),
        ],
        in_specs=[pl.BlockSpec(memory_space=pltpu.SMEM)] + vmem(4) + [hbm] * 4,
        out_specs=vmem(3),
        scratch_shapes=scratch,
        compiler_params=pltpu.CompilerParams(vmem_limit_bytes=VMEM_LIMIT),
        cost_estimate=pl.CostEstimate(flops=10**10, bytes_accessed=16 * 10**6, transcendentals=10**6),
        name="layer_step",
    )(core, arrived, take, tap_fwd, lags, params, upstream, ahead, behind)


def per_device(
    dp, fsdp, cached, send_rows, take_rows, utt_index, upstream, in_proj, norm_gain, conv_kernel
):
    tap_count = conv_kernel.shape[0]
    f_hi, f_lo, back, tap_fwd, lags = [jnp.asarray(m) for m in transforms(tap_count)]
    local = jnp.concatenate([in_proj, conv_kernel, norm_gain[None, :]], axis=0)
    params = lax.all_gather(local, "fsdp", axis=1, tiled=True)
    wanted = send_rows[0, 0]
    outgoing = pick(wanted.reshape(1, -1), cached[0, 0])
    outgoing, take_own, utt_own = lax.optimization_barrier(
        (outgoing, take_rows[0, 0], utt_index[0, 0])
    )
    outgoing = outgoing.reshape(wanted.shape + outgoing.shape[1:])
    arrived = lax.all_to_all(outgoing, "dp", split_axis=0, concat_axis=0, tiled=True)
    arrived = arrived.reshape(-1, arrived.shape[2])
    take = jnp.repeat(take_own, 2)[None, :]
    ahead, behind = prepare(jnp.repeat(utt_own, 2), f_hi, f_lo, back)

    shard_cols = in_proj.shape[1]
    held = local.shape[0]
    tiles = shard_cols // 128
    part = -(-(held * tiles) // dp)
    part = -(-part // 16) * 16
    halves = fsdp // 2
    core = (lax.axis_index("fsdp") % 2).astype(jnp.int32).reshape(1, 1)
    keep, send, loss = layer(
        core, arrived, take, params, upstream[0, 0], tap_fwd, lags, ahead, behind, part * dp, halves
    )
    other = lax.ppermute(send, "fsdp", [(i, i ^ 1) for i in range(fsdp)])
    chip = (keep + other).astype(BF16).reshape(halves * dp, part, 128)
    groups = [
        [d * fsdp + 2 * y + c for y in range(halves) for d in range(dp)] for c in range(2)
    ]
    pieces = lax.all_to_all(
        chip, ("dp", "fsdp"), split_axis=0, concat_axis=0, tiled=True, axis_index_groups=groups
    )
    piece = jnp.sum(pieces.astype(F32), axis=0).astype(BF16)
    whole = lax.all_gather(piece, "dp", axis=0, tiled=True)
    whole = whole[: held * tiles].reshape(tiles, held, 128).transpose(1, 0, 2)
    whole = whole.reshape(held, shard_cols).astype(F32)
    depth = in_proj.shape[0]
    return (
        whole[:depth],
        whole[depth : depth + tap_count],
        whole[depth + tap_count],
        loss,
    )


def solution(mesh):
    placed = (
        P("dp", "fsdp", None, None),
        P("dp", "fsdp", None, None),
        P("dp", "fsdp", None),
        P("dp", "fsdp", None),
        P("dp", "fsdp", None, None),
        P(None, "fsdp"),
        P("fsdp"),
        P(None, "fsdp"),
    )
    return jax.shard_map(
        functools.partial(per_device, mesh.shape["dp"], mesh.shape["fsdp"]),
        mesh=mesh,
        in_specs=placed,
        out_specs=(P(None, "fsdp"), P(None, "fsdp"), P("fsdp"), P("dp", "fsdp")),
        check_vma=False,
    )
```

time: 284 us -> 146 us (0.51)
  waiting for transfers between devices: 113 us -> 22.6 us
  other arithmetic: 80.5 us -> 2.56 us
  Pallas kernels: 0 us -> 25.9 us
  blocking collectives: 48.7 us -> 58.6 us
  matrix products: 6.1 us -> 0 us
    psum x1 -> x0, waiting for transfers between devices: 99.5 us -> none  [per_device(): lax.psum((grad_weight, grad_taps, grad_scale[None, :]), ('dp', 'fsdp'))]
    reduce_sum x6 -> x1, other arithmetic: 77 us -> 0.12 us  [per_device(): piece = jnp.sum(pieces.astype(F32), axis=0).astype(BF16)]
    psum x1 -> x0, blocking collectives: 38.2 us -> none  [per_device(): lax.psum((grad_weight, grad_taps, grad_scale[None, :]), ('dp', 'fsdp'))]
    all_to_all x0 -> x1, blocking collectives: none -> 27.3 us  [per_device(): lax.all_to_all(chip, ('dp', 'fsdp'), split_axis=0, concat_axis=0, tiled=T...]
    pallas_call x0 -> x3, Pallas kernels: none -> 25.9 us  [the longest x1 22.1 us: layer(): pl.pallas_call(layer_kernel, out_shape=[jax.ShapeDtypeStruct((halves, out...]
    all_gather x2 -> x1, blocking collectives: 10.5 us -> 31.2 us  [per_device(): whole = lax.all_gather(piece, 'dp', axis=0, tiled=True)]
    unnamed x13 -> x31, local copies, waits for them, and re-layouts: 0.98 us -> 10.3 us
    all_to_all x1, waiting for transfers between devices: 12.8 us -> 19 us  [per_device(): lax.all_to_all(outgoing, 'dp', split_axis=0, concat_axis=0, tiled=True)]
  transfers between devices with their start and end apart: 3 -> 3, of which waited for: 2 -> 2; matrix products, arithmetic and copies ran while one was open for 3% -> 2% of each run, Pallas kernels for 0% -> 3%
where the time goes in v1:
time: 146 us; the launch traced here: 145 us
  blocking collectives  58.6 us (40%)
  Pallas kernels  25.9 us (18%)
  waiting for transfers between devices  22.6 us (15%)
  between operations  14.3 us (10%)
  local copies, waits for them, and re-layouts  13.7 us (9%)
  starting transfers between devices  7.49 us (5%)
  other arithmetic  2.56 us (2%)
    all_gather x1, blocking collectives, per_device(): whole = lax.all_gather(piece, 'dp', axis=0, tiled=True)  31.2 us
    all_to_all x1, blocking collectives, per_device(): lax.all_to_all(chip, ('dp', 'fsdp'), split_axis=0, concat_axis=0, tiled=T...  27.3 us
    pallas_call x1, Pallas kernels, layer(): pl.pallas_call(layer_kernel, out_shape=[jax.ShapeDtypeStruct((halves, out...  22.1 us
    all_to_all x1, waiting for transfers between devices, per_device(): lax.all_to_all(outgoing, 'dp', split_axis=0, concat_axis=0, tiled=True)  19 us
    unnamed x31, local copies, waits for them, and re-layouts  10.3 us
    all_to_all x1, starting transfers between devices, per_device(): lax.all_to_all(outgoing, 'dp', split_axis=0, concat_axis=0, tiled=True)  7.38 us
    ppermute x1, waiting for transfers between devices, per_device(): other = lax.ppermute(send, 'fsdp', [(i, i ^ 1) for i in range(fsdp)])  3.58 us
  transfers between devices with their start and end apart: 3, of which 2 were waited for; matrix products, arithmetic and copies ran while one was open for 2% of the time, Pallas kernels for 3%

profile of v1, /device:TPU:0, one launch (start us, length us, event | category | flops | bytes accessed | tf_op | source)
XLA Modules:
  0.0 145.2 jit_solution(6935841194590600711)
XLA Ops:
  7.2 0.0 all-gather.2.cloned.1.call-start
  7.2 0.7 broadcast_in_dim.25
  7.9 1.8 %pad_maximum_fusion = bf16[544,384]{1,0:T(8,128)(2,1)} fusion(bf16[1,384]{1,0:T(2,128)(2,1)S(1)} %broadcast_in_dim.25, bf16[31,384]{1,0:T(8,128)(2,1)} %param.20, bf16[512,384]{1,0:T(8,128)(2,1)} %param.18), kind=kLoop, calls=%fused_computation.2 | loop fusion | flops 1253376 | bytes 835584 | tf_op jit(solution)/shard_map/concatenate | solution.py:415
  9.7 0.0 all-gather.2.cloned.1.call-update
  9.7 0.8 reshape_squeeze.3.index_ref
  10.5 0.0 copy-start
  10.5 1.0 copy-done
  11.5 0.0 copy-start.12
  11.5 1.5 %pick_rows.1 = bf16[512,1024]{1,0:T(8,128)(2,1)} custom-call(s32[1,512]{1,0:T(1,128)S(1)} %reshape_squeeze.3.index_ref, bf16[256,1024]{1,0:T(8,128)(2,1)S(1)} %bitcast.21), custom_call_target="tpu_custom_call" | custom-call | flops 268435456 | bytes 1572864 | tf_op jit(solution)/shard_map/pick_rows/pallas_call | solution.py:316
  13.0 0.0 copy-start.3
  13.0 0.0 copy-start.4
  13.0 7.4 %all-to-all-start = ((bf16[8,64,1024]{2,1,0:T(8,128)(2,1)}), bf16[8,64,1024]{2,1,0:T(8,128)(2,1)S(1)}, u32[]{:S(2)}, u32[]{:S(2)}) async-start(bf16[8,64,1024]{2,1,0:T(8,128)(2,1)} %bitcast.4), calls=%async_computation | async-start | bytes 2097152 | tf_op jit(solution)/shard_map/all_to_all | solution.py:423
  20.4 0.0 copy-done.13
  20.4 0.1 broadcast_in_dim.26
  20.5 0.1 mul.8
  20.7 0.1 slice.69
  20.7 0.1 slice.68
  20.8 0.1 slice.63
  20.9 0.1 slice.64
  21.0 0.1 slice.62
  21.0 0.1 slice.61
  21.1 0.1 pad_add_fusion.2
  21.2 0.1 pad_add_fusion
  21.3 0.1 pad_add_fusion.3
  21.4 0.1 pad_add_fusion.5
  21.5 0.1 pad_add_fusion.1
  21.6 0.0 copy-done.12
  21.6 0.1 broadcast_in_dim.24
  21.7 0.1 broadcast_in_dim_reshape.3.take_ref
  21.9 0.1 stack.31.pos_ref
  21.9 0.0 copy-done.3
  21.9 0.0 copy-done.4
  22.0 0.0 copy-done.5
  22.0 0.0 copy-start.2
  22.0 0.0 copy-start.6
  22.0 0.0 copy-start.7
  22.0 2.4 %prepare_transforms.1 = (bf16[256,4480]{1,0:T(8,128)(2,1)S(1)}, bf16[1408,768]{1,0:T(8,128)(2,1)S(1)}) custom-call(s32[8,896]{1,0:T(8,128)S(1)} %stack.31.pos_ref, bf16[256,256]{1,0:T(8,128)(2,1)S(1)} %copy-done.5, bf16[256,256]{1,0:T(8,128)(2,1)S(1)} %copy-done.4, bf16[256,768]{1,0:T(8,128)(2,1)S(1)} %copy-done.3), custom_call_target="tpu_custom_call" | custom-call | flops 3000000000 | bytes 8000000 | tf_op jit(solution)/shard_map/prepare_transforms/pallas_call | solution.py:353
  24.4 0.0 copy-start.8
  24.4 1.4 copy-done.8
  25.8 0.0 copy-start.10
  25.8 1.3 copy-done.10
  27.1 19.0 %all-to-all-done = bf16[8,64,1024]{2,1,0:T(8,128)(2,1)S(1)} async-done(((bf16[8,64,1024]{2,1,0:T(8,128)(2,1)}), bf16[8,64,1024]{2,1,0:T(8,128)(2,1)S(1)}, u32[]{:S(2)}, u32[]{:S(2)}) %all-to-all-start) | async-done | bytes 1048608 | tf_op jit(solution)/shard_map/all_to_all | solution.py:423
  46.2 0.0 all-gather.2.cloned.1.call-done.params_hbm
  46.2 0.0 copy-done.2
  46.2 0.0 copy-done.6
  46.2 0.0 copy-done.7
  46.2 0.0 copy-start.1
  46.2 1.4 copy-done.1
  47.6 0.0 copy-start.9
  47.6 1.6 %copy-done.9 = bf16[256,4480]{1,0:T(8,128)(2,1)S(1)} copy-done((bf16[256,4480]{1,0:T(8,128)(2,1)S(1)}, bf16[256,4480]{1,0:T(8,128)(2,1)}, u32[]{:S(2)}) %copy-start.9) | copy-done | bytes 2293784
  49.3 1.6 %copy-done.11 = bf16[1408,768]{1,0:T(8,128)(2,1)S(1)} copy-done((bf16[1408,768]{1,0:T(8,128)(2,1)S(1)}, bf16[1408,768]{1,0:T(8,128)(2,1)}, u32[]{:S(2)}) %copy-start.11) | copy-done | bytes 2162712
  50.9 22.1 %layer_step.1 = (f32[2,1664,128]{2,1,0:T(8,128)S(1)}, f32[2,1664,128]{2,1,0:T(8,128)S(1)}, f32[1,1]{1,0:T(1,128)}) custom-call(s32[1,1]{1,0:T(1,128)} %bitcast.core_ref, bf16[512,1024]{1,0:T(8,128)(2,1)S(1)} %bitcast.20, s32[1,512]{1,0:T(1,128)S(1)} %broadcast_in_dim_reshape.3.take_ref, bf16[256,64]{1,0:T(8,128)(2,1)S(1)} %copy-done.6, ...), custom_call_target="tpu_custom_call" | custom-call | flops 10000000000 | bytes 16000000 | tf_op jit(solution)/shard_map/layer_step/pallas_call | solution.py:394
  73.0 0.1 collective-permute-start
  73.1 3.6 %collective-permute-done = f32[2,1664,128]{2,1,0:T(8,128)S(1)} collective-permute-done((f32[2,1664,128]{2,1,0:T(8,128)S(1)}, f32[2,1664,128]{2,1,0:T(8,128)S(1)}, u32[]{:S(2)}, u32[]{:S(2)}) %collective-permute-start) | collective-permute-done | bytes 1703968 | tf_op jit(solution)/shard_map/ppermute | solution.py:438
  76.6 0.2 add_convert_fusion
  76.8 27.3 %all_to_all.10 = bf16[16,208,128]{2,1,0:T(8,128)(2,1)S(1)} all-to-all(bf16[16,208,128]{2,1,0:T(8,128)(2,1)S(1)} %bitcast.23), channel_id=1, replica_groups={{0,4,8,12,16,20,24,28,2,6,10,14,18,22,26,30},{1,5,9,13,17,21,25,29,3,7,..., dimensions={0} | all-to-all | bytes 1703936 | tf_op jit(solution)/shard_map/all_to_all | solution.py:443
  104.1 0.1 reduce_sum.12
  104.3 31.2 %all_gather.7 = bf16[1664,128]{1,0:T(8,128)(2,1)S(1)} all-gather(bf16[208,128]{1,0:T(8,128)(2,1)S(1)} %reduce_sum.12), channel_id=1, replica_groups=mesh['dp'=8,'fsdp'=4] {'dp'}, dimensions={0}, use_global_device_ids=true | all-gather | bytes 479232 | tf_op jit(solution)/shard_map/all_gather | solution.py:447
  135.5 0.1 convert_bitcast_fusion
  135.6 0.6 slice_reduce_fusion
  136.2 0.1 slice.77
  136.3 0.3 copy.17
  136.5 1.1 copy.19
  137.7 0.6 copy.20
  (26 shorter events, 0.2 us)
Async XLA Ops:
  7.2 39.0 %all-gather.2.cloned.1.call-start = ((), (), s32[]{:S(2)}) async-start(), calls=%async_computation.2 | async-start | bytes 2088960 | tf_op jit(solution)/shard_map/all_gather | solution.py:416
  10.5 1.0 copy-start
  11.5 8.9 %copy-start.13 = (s32[1,1,256]{2,1,0:T(1,128)S(1)}, s32[1,1,256]{2,1,0:T(1,128)}, u32[]{:S(2)}) copy-start(s32[1,1,256]{2,1,0:T(1,128)} %param.16) | copy-start | bytes 3076
  11.5 10.1 %copy-start.12 = (s32[1,1,256]{2,1,0:T(1,128)S(1)}, s32[1,1,256]{2,1,0:T(1,128)}, u32[]{:S(2)}) copy-start(s32[1,1,256]{2,1,0:T(1,128)} %param.15) | copy-start | bytes 3076
  13.0 8.9 %copy-start.3 = (bf16[256,768]{1,0:T(8,128)(2,1)S(1)}, bf16[256,768]{1,0:T(8,128)(2,1)}, u32[]{:S(2)}) copy-start(bf16[256,768]{1,0:T(8,128)(2,1)} %constant.68.clone.back_ref) | copy-start | bytes 1179652
  13.0 8.9 %copy-start.4 = (bf16[256,256]{1,0:T(8,128)(2,1)S(1)}, bf16[256,256]{1,0:T(8,128)(2,1)}, u32[]{:S(2)}) copy-start(bf16[256,256]{1,0:T(8,128)(2,1)} %constant.67.clone.lo_ref) | copy-start | bytes 393220
  13.0 8.9 %copy-start.5 = (bf16[256,256]{1,0:T(8,128)(2,1)S(1)}, bf16[256,256]{1,0:T(8,128)(2,1)}, u32[]{:S(2)}) copy-start(bf16[256,256]{1,0:T(8,128)(2,1)} %constant.66.clone.hi_ref) | copy-start | bytes 393220
  13.0 33.2 %all-to-all-start = ((bf16[8,64,1024]{2,1,0:T(8,128)(2,1)}), bf16[8,64,1024]{2,1,0:T(8,128)(2,1)S(1)}, u32[]{:S(2)}, u32[]{:S(2)}) async-start(bf16[8,64,1024]{2,1,0:T(8,128)(2,1)} %bitcast.4), calls=%async_computation | async-start | bytes 2097152 | tf_op jit(solution)/shard_map/all_to_all | solution.py:423
  22.0 24.2 %copy-start.2 = (bf16[1,1,512,1536]{3,2,1,0:T(8,128)(2,1)S(1)}, bf16[1,1,512,1536]{3,2,1,0:T(8,128)(2,1)}, u32[]{:S(2)}) copy-start(bf16[1,1,512,1536]{3,2,1,0:T(8,128)(2,1)} %param.17) | copy-start | bytes 4718596
  22.0 24.2 %copy-start.6 = (bf16[256,64]{1,0:T(8,128)(2,1)S(1)}, bf16[256,64]{1,0:T(8,128)(2,1)}, u32[]{:S(2)}) copy-start(bf16[256,64]{1,0:T(8,128)(2,1)} %constant.69.clone.tapf_ref) | copy-start | bytes 98308
  22.0 24.2 %copy-start.7 = (bf16[32,768]{1,0:T(8,128)(2,1)S(1)}, bf16[32,768]{1,0:T(8,128)(2,1)}, u32[]{:S(2)}) copy-start(bf16[32,768]{1,0:T(8,128)(2,1)} %constant.70.clone.lag_ref) | copy-start | bytes 147460
  24.4 1.4 copy-start.8
  25.8 1.3 copy-start.10
  46.2 1.4 copy-start.1
  47.6 1.6 %copy-start.9 = (bf16[256,4480]{1,0:T(8,128)(2,1)S(1)}, bf16[256,4480]{1,0:T(8,128)(2,1)}, u32[]{:S(2)}) copy-start(bf16[256,4480]{1,0:T(8,128)(2,1)} %copy-done.8) | copy-start | bytes 6881284
  49.3 1.6 %copy-start.11 = (bf16[1408,768]{1,0:T(8,128)(2,1)S(1)}, bf16[1408,768]{1,0:T(8,128)(2,1)}, u32[]{:S(2)}) copy-start(bf16[1408,768]{1,0:T(8,128)(2,1)} %copy-done.10) | copy-start | bytes 6488068
  73.0 3.7 %collective-permute-start = (f32[2,1664,128]{2,1,0:T(8,128)S(1)}, f32[2,1664,128]{2,1,0:T(8,128)S(1)}, u32[]{:S(2)}, u32[]{:S(2)}) collective-permute-start(f32[2,1664,128]{2,1,0:T(8,128)S(1)} %get-tuple-element.18), channel_id=1, source_target_pairs={{0,1},{1,0},{2,3},{3,2},{4,5},{5,4},{6,7},{7,6},{8,9},{9,8},{10,11... | collective-permute-start | bytes 5111816 | tf_op jit(solution)/shard_map/ppermute | solution.py:438
Sparse Core Ops, SparseCore 0:
  10.1 22.9 all-gather.1

commit v2 on v1

--- a/solution.py
+++ b/solution.py
@@ -24,7 +24,8 @@
 ROWS = 64
 F32 = jnp.float32
 BF16 = jnp.bfloat16
-VMEM_LIMIT = 40 * 1024 * 1024
+VMEM_LIMIT = 60 * 1024 * 1024
+FEW = 16
 
 
 def k_slices(steps, sizes):
@@ -71,12 +72,52 @@
     return lax.dot_general(a, b, (((0,), (0,)), ((), ())), preferred_element_type=F32)
 
 
-def pick_kernel(index_ref, rows_ref, out_ref):
+def pick_kernel(ids_ref, index_ref, rows_ref, *out_refs):
     count = rows_ref.shape[0]
-    total = index_ref.shape[1]
-    number = lax.broadcasted_iota(jnp.int32, (count, total), 0)
-    choose = jnp.where(number == index_ref[...], 1.0, 0.0).astype(BF16)
-    out_ref[...] = dot_t(choose, rows_ref[...]).astype(BF16)
+    rows = rows_ref[...]
+    if len(out_refs) == 1:
+        index = index_ref[...]
+        number = lax.broadcasted_iota(jnp.int32, (count, index.shape[1]), 0)
+        choose = jnp.where(number == index, 1.0, 0.0).astype(BF16)
+        out_refs[0][...] = dot_t(choose, rows).astype(BF16)
+        return
+    slot = index_ref.shape[1]
+    number = lax.broadcasted_iota(jnp.int32, (count, slot), 0)
+    for k, out_ref in enumerate(out_refs):
+        index = index_ref[pl.ds(ids_ref[0, 2] ^ k, 1), :]
+        choose = jnp.where(number == index, 1.0, 0.0).astype(BF16)
+        out_ref[...] = dot_t(choose, rows).astype(BF16)
+
+
+def runs(first, last, part):
+    out = []
+    row = first
+    while row < last:
+        stop = min(last, (row // part + 1) * part)
+        out.append((row // part, row % part, row % part + stop - row, row - first))
+        row = stop
+    return out
+
+
+def unpack_kernel(count, ids_ref, *refs):
+    piece_refs, (proj_ref, taps_ref, gain_ref, held_ref) = refs[:count], refs[count:]
+    parts, part, _ = held_ref.shape
+    for k in range(parts):
+        piece = piece_refs[k][...] if count == parts else piece_refs[0][k * part : (k + 1) * part]
+        held_ref[k] = piece.astype(F32)
+    depth, width = proj_ref.shape
+    held = depth + 32
+    for tile in range(width // 128):
+        lanes = slice(tile * 128, tile * 128 + 128)
+        for p, start, stop, offset in runs(tile * held, tile * held + depth, part):
+            proj_ref[offset : offset + stop - start, lanes] = held_ref[p ^ ids_ref[0, 2], start:stop]
+        last = [
+            held_ref[p ^ ids_ref[0, 2], start:stop]
+            for p, start, stop, _ in runs(tile * held + depth, tile * held + held, part)
+        ]
+        last = last[0] if len(last) == 1 else jnp.concatenate(last, axis=0)
+        taps_ref[:, lanes] = last[: taps_ref.shape[0]]
+        gain_ref[:, lanes] = last[taps_ref.shape[0] : taps_ref.shape[0] + 1]
 
 
 def prep_kernel(pos_ref, hi_ref, lo_ref, back_ref, ahead_ref, behind_ref):
@@ -100,14 +141,16 @@
         behind_ref[BEHIND_AT[part] : BEHIND_AT[part + 1]] = wide[:held].astype(BF16)
 
 
-def layer_kernel(
-    core_ref, arrived_ref, take_ref, tapf_ref, lag_ref, params_hbm, up_hbm, ahead_hbm, behind_hbm,
-    keep_ref, send_ref, loss_ref,
-    params_ref, up_ref, ahead_ref, behind_ref, sems,
-    frames_ref, frames_t_ref, x_ref, h_ref, stat_ref, acc_ref, acc2_ref,
-    hi_ref, lo_ref, ghi_ref, glo_ref, spec_ref, nspec_ref, phi_ref, plo_ref,
-    coef_ref, c_ref, small_ref, lossacc_ref,
-):
+def layer_kernel(count, ids_ref, *refs):
+    arrived_refs = refs[:count]
+    (
+        take_ref, tapf_ref, lag_ref, small_in_ref, params_hbm, up_hbm, ahead_hbm, behind_hbm,
+        keep_ref, send_ref, loss_ref,
+        params_ref, up_ref, ahead_ref, behind_ref, sems,
+        frames_ref, frames_t_ref, x_ref, h_ref, stat_ref, acc_ref, acc2_ref,
+        hi_ref, lo_ref, ghi_ref, glo_ref, spec_ref, nspec_ref, phi_ref, plo_ref,
+        coef_ref, c_ref, small_ref, lossacc_ref,
+    ) = refs[count:]
     copies = [
         pltpu.make_async_copy(source, target, sems.at[k])
         for k, (source, target) in enumerate(
@@ -117,7 +160,8 @@
     for copy in copies:
         copy.start()
     steps, width = up_ref.shape
-    slots, pair_width = arrived_ref.shape
+    slots = sum(ref.shape[0] for ref in arrived_refs)
+    pair_width = arrived_refs[0].shape[1]
     depth = pair_width // 2
     chunks = width // CH
     scale = (steps * width) ** -0.5
@@ -133,7 +177,9 @@
     here = number == take
     even_hot = jnp.where(here & (odd == 0), 1.0, 0.0).astype(BF16)
     odd_hot = jnp.where(here & (odd == 1), 1.0, 0.0).astype(BF16)
-    frames = dot_t(even_hot, arrived_ref[:, :depth]) + dot_t(odd_hot, arrived_ref[:, depth:])
+    first = jnp.concatenate([ref[:, :depth] for ref in arrived_refs], axis=0)
+    second = jnp.concatenate([ref[:, depth:] for ref in arrived_refs], axis=0)
+    frames = dot_t(even_hot, first) + dot_t(odd_hot, second)
     frames_ref[...] = frames.astype(BF16)
     frames_t_ref[...] = jnp.transpose(frames).astype(BF16)
     live = dot_t(even_hot + odd_hot, jnp.ones((slots, 128), BF16))
@@ -144,7 +190,7 @@
 
     def project(i, carry):
         cols = pl.ds(pl.multiple_of(i * CH, CH), CH)
-        x = dot(frames_ref[...], params_ref[:depth, cols])
+        x = dot(frames_ref[...], params_ref[:, cols])
         x_ref[:, cols] = x
         acc_ref[...] += x[:, :128] + x[:, 128:]
         return carry
@@ -178,8 +224,8 @@
 
     def middle(i, carry):
         cols = pl.ds(pl.multiple_of(i * CH, CH), CH)
-        gain = params_ref[depth + 16 : depth + 32, cols][15:16].astype(F32)
-        taps = params_ref[depth : depth + 32, cols]
+        gain = small_in_ref[16:32, cols][15:16].astype(F32)
+        taps = small_in_ref[:, cols]
         coef_ref[...] = dot(tapf_ref[...], jnp.concatenate([taps, taps], axis=0))
         for rows in tiles:
             xhat = (x_ref[rows, cols] - twice(stat_ref[0, rows])) * twice(stat_ref[1, rows])
@@ -275,7 +321,7 @@
         acc_ref[rows] = jnp.broadcast_to(m1, (ROWS, 128))
         acc2_ref[rows] = jnp.broadcast_to(m2, (ROWS, 128))
 
-    halves, filled_to, _ = keep_ref.shape
+    halves, parts, part, _ = keep_ref.shape
     per_block = width // (2 * halves) // 128
     held = depth + 32
 
@@ -295,35 +341,65 @@
                 lanes = slice(half * 128, half * 128 + 128)
                 small = small_ref[:, tile * 128 : (tile + 1) * 128]
                 target = keep_ref if block % 2 == core else send_ref
-                target[block // 2, inside : inside + depth] = weight[:, lanes]
-                target[block // 2, inside + depth : inside + held] = small
-
-    pl.when(core_ref[0, 0] == 0)(lambda: finish(0))
-    pl.when(core_ref[0, 0] != 0)(lambda: finish(1))
-    filled = per_block * held
-    if filled_to > filled:
-        for half in range(halves):
+                side = (block // 2) ^ ids_ref[0, 1]
+                for p, start, stop, offset in runs(inside, inside + depth, part):
+                    value = weight[offset : offset + stop - start, lanes]
+                    target[side, p ^ ids_ref[0, 2], start:stop] = value
+                for p, start, stop, offset in runs(inside + depth, inside + held, part):
+                    value = small[offset : offset + stop - start]
+                    target[side, p ^ ids_ref[0, 2], start:stop] = value
+
+    pl.when(ids_ref[0, 0] == 0)(lambda: finish(0))
+    pl.when(ids_ref[0, 0] != 0)(lambda: finish(1))
+    for p, start, stop, _ in runs(per_block * held, parts * part, part):
+        for side in range(halves):
             for ref in (keep_ref, send_ref):
-                ref[half, filled:] = jnp.zeros((filled_to - filled, 128), F32)
+                ref[side, p ^ ids_ref[0, 2], start:stop] = jnp.zeros((stop - start, 128), F32)
 
 
 def vmem(count):
     return [pl.BlockSpec(memory_space=pltpu.VMEM)] * count
 
 
-def pick(index, rows):
-    total = index.shape[1]
+SCALARS = pl.BlockSpec(memory_space=pltpu.SMEM)
+
+
+def pick(ids, index, rows):
+    dp, slot = index.shape
+    width = rows.shape[1]
+    if dp > FEW:
+        index = index.reshape(1, -1)
+        shapes = [jax.ShapeDtypeStruct((dp * slot, width), BF16)]
+    else:
+        shapes = [jax.ShapeDtypeStruct((slot, width), BF16)] * dp
     return pl.pallas_call(
         pick_kernel,
-        out_shape=jax.ShapeDtypeStruct((total, rows.shape[1]), BF16),
-        in_specs=vmem(2),
-        out_specs=vmem(1)[0],
+        out_shape=shapes,
+        in_specs=[SCALARS] + vmem(2),
+        out_specs=vmem(len(shapes)),
         compiler_params=pltpu.CompilerParams(vmem_limit_bytes=VMEM_LIMIT),
         cost_estimate=pl.CostEstimate(
-            flops=2 * total * rows.size, bytes_accessed=6 * rows.size, transcendentals=0
+            flops=2 * dp * slot * rows.size, bytes_accessed=6 * rows.size, transcendentals=0
         ),
         name="pick_rows",
-    )(index, rows)
+    )(ids, index, rows)
+
+
+def unpack(ids, pieces, parts, part, depth, tap_count, width):
+    return pl.pallas_call(
+        functools.partial(unpack_kernel, len(pieces)),
+        out_shape=[
+            jax.ShapeDtypeStruct((depth, width), F32),
+            jax.ShapeDtypeStruct((tap_count, width), F32),
+            jax.ShapeDtypeStruct((1, width), F32),
+        ],
+        in_specs=[SCALARS] + vmem(len(pieces)),
+        out_specs=vmem(3),
+        scratch_shapes=[pltpu.VMEM((parts, part, 128), F32)],
+        compiler_params=pltpu.CompilerParams(vmem_limit_bytes=VMEM_LIMIT),
+        cost_estimate=pl.CostEstimate(flops=10**6, bytes_accessed=12 * 10**5, transcendentals=0),
+        name="unpack_gradients",
+    )(ids, *pieces)
 
 
 def positions(utterances):
@@ -361,9 +437,11 @@
     )(positions(utterances), f_hi, f_lo, back)
 
 
-def layer(core, arrived, take, params, upstream, tap_fwd, lags, ahead, behind, out_rows, halves):
+def layer(
+    ids, arrived, take, small, params, upstream, tap_fwd, lags, ahead, behind, parts, part, halves
+):
     steps, width = upstream.shape
-    depth = arrived.shape[1] // 2
+    depth = arrived[0].shape[1] // 2
     hbm = pl.BlockSpec(memory_space=pltpu.HBM)
     scratch = [
         pltpu.VMEM(params.shape, BF16),
@@ -392,19 +470,19 @@
         pltpu.VMEM((1, CH), F32),
     ]
     return pl.pallas_call(
-        layer_kernel,
+        functools.partial(layer_kernel, len(arrived)),
         out_shape=[
-            jax.ShapeDtypeStruct((halves, out_rows, 128), F32),
-            jax.ShapeDtypeStruct((halves, out_rows, 128), F32),
+            jax.ShapeDtypeStruct((halves, parts, part, 128), F32),
+            jax.ShapeDtypeStruct((halves, parts, part, 128), F32),
             jax.ShapeDtypeStruct((1, 1), F32),
         ],
-        in_specs=[pl.BlockSpec(memory_space=pltpu.SMEM)] + vmem(4) + [hbm] * 4,
+        in_specs=[SCALARS] + vmem(len(arrived) + 4) + [hbm] * 4,
         out_specs=vmem(3),
         scratch_shapes=scratch,
         compiler_params=pltpu.CompilerParams(vmem_limit_bytes=VMEM_LIMIT),
         cost_estimate=pl.CostEstimate(flops=10**10, bytes_accessed=16 * 10**6, transcendentals=10**6),
         name="layer_step",
-    )(core, arrived, take, tap_fwd, lags, params, upstream, ahead, behind)
+    )(ids, *arrived, take, tap_fwd, lags, small, params, upstream, ahead, behind)
 
 
 def per_device(
@@ -412,48 +490,75 @@
 ):
     tap_count = conv_kernel.shape[0]
     f_hi, f_lo, back, tap_fwd, lags = [jnp.asarray(m) for m in transforms(tap_count)]
-    local = jnp.concatenate([in_proj, conv_kernel, norm_gain[None, :]], axis=0)
-    params = lax.all_gather(local, "fsdp", axis=1, tiled=True)
+    params = lax.all_gather(in_proj, "fsdp", axis=1, tiled=True)
+    few = dp <= FEW
+    place = lax.axis_index("fsdp")
+    ours = lax.axis_index("dp") if few else 0
+    ids = jnp.stack([place % 2, place // 2, ours]).astype(jnp.int32)[None, :]
     wanted = send_rows[0, 0]
-    outgoing = pick(wanted.reshape(1, -1), cached[0, 0])
-    outgoing, take_own, utt_own = lax.optimization_barrier(
-        (outgoing, take_rows[0, 0], utt_index[0, 0])
+    outgoing = pick(ids, wanted, cached[0, 0])
+    outgoing, take_own, utt_own, taps_own, gain_own = lax.optimization_barrier(
+        (outgoing, take_rows[0, 0], utt_index[0, 0], conv_kernel, norm_gain)
     )
-    outgoing = outgoing.reshape(wanted.shape + outgoing.shape[1:])
-    arrived = lax.all_to_all(outgoing, "dp", split_axis=0, concat_axis=0, tiled=True)
-    arrived = arrived.reshape(-1, arrived.shape[2])
+
+    def swap(value, k):
+        return lax.ppermute(value, "dp", [(i, i ^ k) for i in range(dp)])
+
+    far_first = [k for k in range(dp // 2, dp)] + [k for k in range(dp // 2 - 1, 0, -1)]
+    if few:
+        got = {k: swap(outgoing[k], k) for k in far_first}
+        arrived = [outgoing[0]] + [got[k] for k in range(1, dp)]
+        take_own = jnp.where(take_own >= 0, take_own ^ (ours * wanted.shape[1]), -1)
+    else:
+        sent = outgoing[0].reshape(wanted.shape + outgoing[0].shape[1:])
+        back_in = lax.all_to_all(sent, "dp", split_axis=0, concat_axis=0, tiled=True)
+        arrived = [back_in.reshape(-1, back_in.shape[2])]
+    small = lax.all_gather(
+        jnp.concatenate([taps_own, gain_own[None, :]], axis=0), "fsdp", axis=1, tiled=True
+    )
     take = jnp.repeat(take_own, 2)[None, :]
     ahead, behind = prepare(jnp.repeat(utt_own, 2), f_hi, f_lo, back)
 
-    shard_cols = in_proj.shape[1]
-    held = local.shape[0]
+    depth, shard_cols = in_proj.shape
+    held = depth + 32
     tiles = shard_cols // 128
     part = -(-(held * tiles) // dp)
     part = -(-part // 16) * 16
     halves = fsdp // 2
-    core = (lax.axis_index("fsdp") % 2).astype(jnp.int32).reshape(1, 1)
     keep, send, loss = layer(
-        core, arrived, take, params, upstream[0, 0], tap_fwd, lags, ahead, behind, part * dp, halves
+        ids, arrived, take, small, params, upstream[0, 0], tap_fwd, lags, ahead, behind,
+        dp, part, halves,
     )
     other = lax.ppermute(send, "fsdp", [(i, i ^ 1) for i in range(fsdp)])
-    chip = (keep + other).astype(BF16).reshape(halves * dp, part, 128)
-    groups = [
-        [d * fsdp + 2 * y + c for y in range(halves) for d in range(dp)] for c in range(2)
-    ]
-    pieces = lax.all_to_all(
-        chip, ("dp", "fsdp"), split_axis=0, concat_axis=0, tiled=True, axis_index_groups=groups
-    )
-    piece = jnp.sum(pieces.astype(F32), axis=0).astype(BF16)
-    whole = lax.all_gather(piece, "dp", axis=0, tiled=True)
-    whole = whole[: held * tiles].reshape(tiles, held, 128).transpose(1, 0, 2)
-    whole = whole.reshape(held, shard_cols).astype(F32)
-    depth = in_proj.shape[0]
-    return (
-        whole[:depth],
-        whole[depth : depth + tap_count],
-        whole[depth + tap_count],
-        loss,
-    )
+    half = dp // 2
+    across = [(i, i ^ 2) for i in range(fsdp)]
+    sums = {}
+    for low, high in ((half, dp), (0, half)):
+        theirs = (keep[1, low:high] + other[1, low:high]).astype(BF16)
+        theirs = lax.ppermute(theirs, "fsdp", across)
+        mine = keep[0, low:high] + other[0, low:high]
+        sums[low] = mine + theirs.astype(F32)
+    if few:
+        got = {}
+        for k in far_first:
+            low = half if k >= half else 0
+            got[k] = swap(sums[low][k - low].astype(BF16), k)
+        total = sums[0][0]
+        for k in range(1, dp):
+            total = total + got[k].astype(F32)
+        piece = total.astype(BF16)
+        far = {k: swap(piece, k) for k in range(dp - 2, 0, -2)}
+        pieces = {0: piece, 1: swap(piece, 1), **far}
+        for k in far:
+            pieces[k + 1] = swap(far[k], 1)
+        pieces = [pieces[k] for k in range(dp)]
+    else:
+        chip = jnp.concatenate([sums[0], sums[half]], axis=0).astype(BF16)
+        shared = lax.all_to_all(chip, "dp", split_axis=0, concat_axis=0, tiled=True)
+        piece = jnp.sum(shared.astype(F32), axis=0).astype(BF16)
+        pieces = [lax.all_gather(piece, "dp", axis=0, tiled=True)]
+    proj, taps, gain = unpack(ids, pieces, dp, part, depth, tap_count, shard_cols)
+    return (proj, taps, gain[0], loss)
 
 
 def solution(mesh):

time: 146 us -> 124 us (0.85)
  blocking collectives: 58.6 us -> 5.83 us
  starting transfers between devices: 7.49 us -> 35.3 us
  local copies, waits for them, and re-layouts: 13.7 us -> 3.54 us
  Pallas kernels: 25.9 us -> 34.4 us
  waiting for transfers between devices: 22.6 us -> 26.2 us
  other arithmetic: 2.56 us -> 4.44 us
    ppermute x0 -> x23, starting transfers between devices: none -> 35.2 us  [the longest x21 33.1 us: swap(): return lax.ppermute(value, 'dp', [(i, i ^ k) for i in range(dp)])]
    all_to_all x1 -> x0, blocking collectives: 27.3 us -> none  [per_device(): lax.all_to_all(chip, ('dp', 'fsdp'), split_axis=0, concat_axis=0, tiled=T...]
    all_gather x1, blocking collectives: 31.2 us -> 5.83 us  [per_device(): lax.all_gather(jnp.concatenate([taps_own, gain_own[None, :]], axis=0), 'f...]
    ppermute x0 -> x23, waiting for transfers between devices: none -> 21.7 us  [the longest x21 11.9 us: swap(): return lax.ppermute(value, 'dp', [(i, i ^ k) for i in range(dp)])]
    all_to_all x1 -> x0, waiting for transfers between devices: 19 us -> none  [per_device(): lax.all_to_all(outgoing, 'dp', split_axis=0, concat_axis=0, tiled=True)]
    unnamed x31 -> x40, local copies, waits for them, and re-layouts: 10.3 us -> 1.3 us
    all_to_all x1 -> x0, starting transfers between devices: 7.38 us -> none  [per_device(): lax.all_to_all(outgoing, 'dp', split_axis=0, concat_axis=0, tiled=True)]
    pallas_call x2 -> x3, Pallas kernels: 23.6 us -> 28.8 us  [the longest x1 24.2 us: layer(): pl.pallas_call(functools.partial(layer_kernel, len(arrived)), out_shape=[...]
  transfers between devices with their start and end apart: 3 -> 25, of which waited for: 2 -> 11; matrix products, arithmetic and copies ran while one was open for 2% -> 3% of each run, Pallas kernels for 3% -> 7%
where the time goes in v2:
time: 124 us
  starting transfers between devices  35.3 us (28%)
  Pallas kernels  34.4 us (28%)
  waiting for transfers between devices  26.2 us (21%)
  between operations  14.4 us (12%)
  blocking collectives  5.83 us (5%)
  other arithmetic  4.44 us (4%)
  local copies, waits for them, and re-layouts  3.54 us (3%)
    ppermute x21, starting transfers between devices, swap(): return lax.ppermute(value, 'dp', [(i, i ^ k) for i in range(dp)])  33.1 us
    pallas_call x1, Pallas kernels, layer(): pl.pallas_call(functools.partial(layer_kernel, len(arrived)), out_shape=[...  24.2 us
    ppermute x21, waiting for transfers between devices, swap(): return lax.ppermute(value, 'dp', [(i, i ^ k) for i in range(dp)])  11.9 us
    ppermute x2, waiting for transfers between devices, per_device(): theirs = lax.ppermute(theirs, 'fsdp', across)  9.83 us
    all_gather x1, blocking collectives, per_device(): lax.all_gather(jnp.concatenate([taps_own, gain_own[None, :]], axis=0), 'f...  5.83 us
    pallas_call x1, Pallas kernels, prepare(): pl.pallas_call(prep_kernel, out_shape=shapes, in_specs=vmem(4), out_specs...  5.59 us
    ppermute x1, waiting for transfers between devices, per_device(): other = lax.ppermute(send, 'fsdp', [(i, i ^ 1) for i in range(fsdp)])  3.8 us
    pallas_call x1, Pallas kernels, pick(): pl.pallas_call(pick_kernel, out_shape=shapes, in_specs=[SCALARS] + vmem(2...  2.61 us
  transfers between devices with their start and end apart: 25, of which 11 were waited for; matrix products, arithmetic and copies ran while one was open for 3% of the time, Pallas kernels for 7%

profile of v2, /device:TPU:0, one launch (start us, length us, event | category | flops | bytes accessed | tf_op | source)
XLA Modules:
  0.0 124.1 jit_solution(8503063578548770913)
XLA Ops:
  7.2 0.0 all-gather.2.cloned.1.call-start
  7.2 0.7 all-gather.2.cloned.1.call-update
  7.9 0.7 add_bitcast_fusion.ids_ref
  8.6 2.6 %pick_rows.1 = (bf16[64,1024]{1,0:T(8,128)(2,1)}, bf16[64,1024]{1,0:T(8,128)(2,1)}, bf16[64,1024]{1,0:T(8,128)(2,1)}, bf16[64,1024]{1,0:T(8,128)(2,1)}, bf16[64,...) custom-call(s32[1,3]{1,0:T(1,128)} %add_bitcast_fusion.ids_ref, ...), custom_call_target="tpu_custom_call" | custom-call | flops 268435456 | bytes 1572864 | tf_op jit(solution)/shard_map/pick_rows/pallas_call | solution.py:375
  11.2 2.9 %collective-permute-start = (bf16[64,1024]{1,0:T(8,128)(2,1)}, bf16[64,1024]{1,0:T(8,128)(2,1)S(1)}, u32[]{:S(2)}, u32[]{:S(2)}) collective-permute-start(bf16[64,1024]{1,0:T(8,128)(2,1)} %get-tuple-element.41), channel_id=1, source_target_pairs={{0,4},{4,0},{8,12},{12,8},{16,20},{20,16},{24,28},{28,24},{1,5},{5... | collective-permute-start | bytes 393224 | tf_op jit(solution)/shard_map/ppermute | solution.py:505
  14.1 1.6 %collective-permute-start.1 = (bf16[64,1024]{1,0:T(8,128)(2,1)}, bf16[64,1024]{1,0:T(8,128)(2,1)S(1)}, u32[]{:S(2)}, u32[]{:S(2)}) collective-permute-start(bf16[64,1024]{1,0:T(8,128)(2,1)} %get-tuple-element.42), channel_id=1, source_target_pairs={{0,8},{4,12},{8,0},{12,4},{16,24},{20,28},{24,16},{28,20},{1,9},{5... | collective-permute-start | bytes 393224 | tf_op jit(solution)/shard_map/ppermute | solution.py:505
  15.7 0.0 collective-permute-start.2
  15.7 3.0 %collective-permute-start.3 = (bf16[64,1024]{1,0:T(8,128)(2,1)}, bf16[64,1024]{1,0:T(8,128)(2,1)S(1)}, u32[]{:S(2)}, u32[]{:S(2)}) collective-permute-start(bf16[64,1024]{1,0:T(8,128)(2,1)} %get-tuple-element.44), channel_id=1, source_target_pairs={{0,16},{4,20},{8,24},{12,28},{16,0},{20,4},{24,8},{28,12},{1,17},{... | collective-permute-start | bytes 393224 | tf_op jit(solution)/shard_map/ppermute | solution.py:505
  18.7 1.3 %collective-permute-start.4 = (bf16[64,1024]{1,0:T(8,128)(2,1)}, bf16[64,1024]{1,0:T(8,128)(2,1)S(1)}, u32[]{:S(2)}, u32[]{:S(2)}) collective-permute-start(bf16[64,1024]{1,0:T(8,128)(2,1)} %get-tuple-element.45), channel_id=1, source_target_pairs={{0,20},{4,16},{8,28},{12,24},{16,4},{20,0},{24,12},{28,8},{1,21},{... | collective-permute-start | bytes 393224 | tf_op jit(solution)/shard_map/ppermute | solution.py:505
  20.0 0.7 compare_select_fusion
  20.7 0.1 broadcast_in_dim.35
  20.8 0.1 mul.12
  21.0 0.1 slice.105
  21.0 0.1 slice.104
  21.1 0.1 slice.99
  21.2 0.1 slice.100
  21.3 0.1 slice.98
  21.3 0.1 slice.97
  21.4 0.1 pad_add_fusion.2
  21.5 0.1 pad_add_fusion
  21.6 0.1 pad_add_fusion.3
  21.7 0.1 pad_add_fusion.5
  21.8 0.1 pad_add_fusion.1
  21.9 0.7 stack.47.pos_ref
  22.6 5.6 %prepare_transforms.1 = (bf16[256,4480]{1,0:T(8,128)(2,1)}, bf16[1408,768]{1,0:T(8,128)(2,1)}) custom-call(s32[8,896]{1,0:T(8,128)} %stack.47.pos_ref, bf16[256,256]{1,0:T(8,128)(2,1)} %constant.81.clone.hi_ref, bf16[256,256]{1,0:T(8,128)(2,1)} %constant.82.clone.lo_ref, bf16[256,768]{1,0:T(8,128)(2,1)} %constant.83.clone.back_ref), custom_call_target="tpu_custom_call" | custom-call | flops 3000000000 | bytes 8000000 | tf_op jit(solution)/shard_map/prepare_transforms/pallas_call | solution.py:429
  28.2 0.1 broadcast_in_dim.33
  28.3 0.7 broadcast_in_dim_reshape.3.refs_8_
  29.0 3.7 %collective-permute-start.5 = (bf16[64,1024]{1,0:T(8,128)(2,1)S(1)}, bf16[64,1024]{1,0:T(8,128)(2,1)S(1)}, u32[]{:S(2)}, u32[]{:S(2)}) collective-permute-start(bf16[64,1024]{1,0:T(8,128)(2,1)S(1)} %copy-done.17), channel_id=1, source_target_pairs={{0,24},{4,28},{8,16},{12,20},{16,8},{20,12},{24,0},{28,4},{1,25},{... | collective-permute-start | bytes 393224 | tf_op jit(solution)/shard_map/ppermute | solution.py:505
  32.7 0.1 collective-permute-start.6
  32.8 5.8 %all_gather.6.refs_11_ = bf16[32,1536]{1,0:T(8,128)(2,1)} all-gather(bf16[32,384]{1,0:T(8,128)(2,1)S(1)} %pad_maximum_fusion), channel_id=1, replica_groups=mesh['dp'=8,'fsdp'=4] {'fsdp'}, dimensions={1}, use_global_device_ids=true | all-gather | bytes 122880 | tf_op jit(solution)/shard_map/all_gather | solution.py:516
  38.6 0.0 collective-permute-done.2.refs_3_
  38.7 1.8 %collective-permute-done.6.refs_7_ = bf16[64,1024]{1,0:T(8,128)(2,1)S(1)} collective-permute-done((bf16[64,1024]{1,0:T(8,128)(2,1)S(1)}, bf16[64,1024]{1,0:T(8,128)(2,1)S(1)}, u32[]{:S(2)}, u32[]{:S(2)}) %collective-permute-start.6) | collective-permute-done | bytes 131104 | tf_op jit(solution)/shard_map/ppermute | solution.py:505
  40.6 0.6 copy-done.19
  41.2 24.2 %layer_step.1 = (f32[2,8,208,128]{3,2,1,0:T(8,128)}, f32[2,8,208,128]{3,2,1,0:T(8,128)}, f32[1,1]{1,0:T(1,128)}) custom-call(s32[1,3]{1,0:T(1,128)} %add_bitcast_fusion.ids_ref, bf16[64,1024]{1,0:T(8,128)(2,1)} %get-tuple-element.40.refs_0_, bf16[64,1024]{1,0:T(8,128)(2,1)} %copy-done.11, bf16[64,1024]{1,0:T(8,128)(2,1)} %copy-done.12, ...), custom_call_target="tpu_custom_call" | custom-call | flops 10000000000 | bytes 16000000 | tf_op jit(solution)/shard_map/layer_step/pallas_call | solution.py:472
  65.4 0.1 collective-permute-start.7
  65.5 3.8 %collective-permute-done.7 = f32[2,8,208,128]{3,2,1,0:T(8,128)S(1)} collective-permute-done((f32[2,8,208,128]{3,2,1,0:T(8,128)}, f32[2,8,208,128]{3,2,1,0:T(8,128)S(1)}, u32[]{:S(2)}, u32[]{:S(2)}) %collective-permute-start.7) | collective-permute-done | bytes 1703968 | tf_op jit(solution)/shard_map/ppermute | solution.py:532
  69.3 1.2 fusion.8
  70.5 1.6 %collective-permute-start.12 = (bf16[4,208,128]{2,1,0:T(8,128)(2,1)S(1)}, bf16[4,208,128]{2,1,0:T(8,128)(2,1)S(1)}, u32[]{:S(2)}, u32[]{:S(2)}) collective-permute-start(bf16[4,208,128]{2,1,0:T(8,128)(2,1)S(1)} %get-tuple-element.63), channel_id=1, source_target_pairs={{0,2},{1,3},{2,0},{3,1},{4,6},{5,7},{6,4},{7,5},{8,10},{9,11},{10,... | collective-permute-start | bytes 638984 | tf_op jit(solution)/shard_map/ppermute | solution.py:538
  72.1 0.5 collective-permute-start.8
  72.6 6.1 %collective-permute-done.12 = bf16[4,208,128]{2,1,0:T(8,128)(2,1)S(1)} collective-permute-done((bf16[4,208,128]{2,1,0:T(8,128)(2,1)S(1)}, bf16[4,208,128]{2,1,0:T(8,128)(2,1)S(1)}, u32[]{:S(2)}, u32[]{:S(2)}) %collective-permute-start.12) | collective-permute-done | bytes 213024 | tf_op jit(solution)/shard_map/ppermute | solution.py:538
  78.6 3.8 %collective-permute-done.8 = bf16[4,208,128]{2,1,0:T(8,128)(2,1)S(1)} collective-permute-done((bf16[4,208,128]{2,1,0:T(8,128)(2,1)S(1)}, bf16[4,208,128]{2,1,0:T(8,128)(2,1)S(1)}, u32[]{:S(2)}, u32[]{:S(2)}) %collective-permute-start.8) | collective-permute-done | bytes 213024 | tf_op jit(solution)/shard_map/ppermute | solution.py:538
  82.4 0.1 fusion.21
  82.6 0.6 collective-permute-start.9
  83.1 3.8 %collective-permute-start.11 = (bf16[208,128]{1,0:T(8,128)(2,1)S(1)}, bf16[208,128]{1,0:T(8,128)(2,1)S(1)}, u32[]{:S(2)}, u32[]{:S(2)}) collective-permute-start(bf16[208,128]{1,0:T(8,128)(2,1)S(1)} %get-tuple-element.66), channel_id=1, source_target_pairs={{0,12},{4,8},{8,4},{12,0},{16,28},{20,24},{24,20},{28,16},{1,13},{... | collective-permute-start | bytes 159752 | tf_op jit(solution)/shard_map/ppermute | solution.py:505
  87.0 3.6 %collective-permute-start.13 = (bf16[208,128]{1,0:T(8,128)(2,1)S(1)}, bf16[208,128]{1,0:T(8,128)(2,1)S(1)}, u32[]{:S(2)}, u32[]{:S(2)}) collective-permute-start(bf16[208,128]{1,0:T(8,128)(2,1)S(1)} %get-tuple-element.68), channel_id=1, source_target_pairs={{0,16},{4,20},{8,24},{12,28},{16,0},{20,4},{24,8},{28,12},{1,17},{... | collective-permute-start | bytes 159752 | tf_op jit(solution)/shard_map/ppermute | solution.py:505
  90.6 1.2 collective-permute-start.16
  91.9 2.6 %collective-permute-start.15 = (bf16[208,128]{1,0:T(8,128)(2,1)S(1)}, bf16[208,128]{1,0:T(8,128)(2,1)S(1)}, u32[]{:S(2)}, u32[]{:S(2)}) collective-permute-start(bf16[208,128]{1,0:T(8,128)(2,1)S(1)} %get-tuple-element.70), channel_id=1, source_target_pairs={{0,24},{4,28},{8,16},{12,20},{16,8},{20,12},{24,0},{28,4},{1,25},{... | collective-permute-start | bytes 159752 | tf_op jit(solution)/shard_map/ppermute | solution.py:505
  94.5 3.1 %collective-permute-done.16 = bf16[208,128]{1,0:T(8,128)(2,1)S(1)} collective-permute-done((bf16[208,128]{1,0:T(8,128)(2,1)S(1)}, bf16[208,128]{1,0:T(8,128)(2,1)S(1)}, u32[]{:S(2)}, u32[]{:S(2)}) %collective-permute-start.16) | collective-permute-done | bytes 53280 | tf_op jit(solution)/shard_map/ppermute | solution.py:505
  97.6 0.3 collective-permute-done.15
  97.9 3.0 %collective-permute-done.14 = bf16[208,128]{1,0:T(8,128)(2,1)S(1)} collective-permute-done((bf16[208,128]{1,0:T(8,128)(2,1)S(1)}, bf16[208,128]{1,0:T(8,128)(2,1)S(1)}, u32[]{:S(2)}, u32[]{:S(2)}) %collective-permute-start.14) | collective-permute-done | bytes 53280 | tf_op jit(solution)/shard_map/ppermute | solution.py:505
  100.9 0.1 fusion.16.refs_0_
  101.0 1.6 %collective-permute-start.22 = (bf16[208,128]{1,0:T(8,128)(2,1)S(1)}, bf16[208,128]{1,0:T(8,128)(2,1)S(1)}, u32[]{:S(2)}, u32[]{:S(2)}) collective-permute-start(bf16[208,128]{1,0:T(8,128)(2,1)S(1)} %fusion.16.refs_0_), channel_id=1, source_target_pairs={{0,24},{4,28},{8,16},{12,20},{16,8},{20,12},{24,0},{28,4},{1,25},{... | collective-permute-start | bytes 159752 | tf_op jit(solution)/shard_map/ppermute | solution.py:505
  102.6 2.8 %collective-permute-start.18 = (bf16[208,128]{1,0:T(8,128)(2,1)S(1)}, bf16[208,128]{1,0:T(8,128)(2,1)S(1)}, u32[]{:S(2)}, u32[]{:S(2)}) collective-permute-start(bf16[208,128]{1,0:T(8,128)(2,1)S(1)} %fusion.16.refs_0_), channel_id=1, source_target_pairs={{0,8},{4,12},{8,0},{12,4},{16,24},{20,28},{24,16},{28,20},{1,9},{5... | collective-permute-start | bytes 159752 | tf_op jit(solution)/shard_map/ppermute | solution.py:505
  105.4 1.1 collective-permute-start.17
  106.5 0.4 collective-permute-done.22.refs_6_
  107.0 1.1 collective-permute-start.23
  108.1 1.1 collective-permute-start.21
  109.2 0.9 collective-permute-start.19
  110.1 0.9 collective-permute-done.23.refs_7_
  111.1 1.1 collective-permute-done.21.refs_5_
  112.2 1.1 collective-permute-done.19.refs_3_
  113.4 0.6 copy-done.8
  114.0 2.0 %unpack_gradients.1 = (f32[512,384]{1,0:T(8,128)}, f32[31,384]{1,0:T(8,128)}, f32[1,384]{1,0:T(1,128)}) custom-call(s32[1,3]{1,0:T(1,128)} %add_bitcast_fusion.ids_ref, bf16[208,128]{1,0:T(8,128)(2,1)} %copy-done.1, bf16[208,128]{1,0:T(8,128)(2,1)} %copy-done.5, bf16[208,128]{1,0:T(8,128)(2,1)} %copy-done.4, bf16[208,128]{1,0:T(8,128)(2,1)} %copy-done.8, ...), custom_call_target="tpu_custom_call" | custom-call | flops 1000000 | bytes 1200000 | tf_op jit(solution)/shard_map/unpack_gradients/pallas_call | solution.py:389
  116.0 1.3 %reduce = f32[384]{0:T(512)} reduce(f32[1,384]{1,0:T(1,128)} %get-tuple-element.58, f32[]{:T(128)} %constant.101), dimensions={0}, to_apply=%get-tuple-element.58.reduce_sub_computation | reduce | bytes 3076 | tf_op jit(solution)/shard_map/unpack_gradients/pallas_call | solution.py:389
  (76 shorter events, 0.3 us)
Async XLA Ops:
  7.2 33.3 %all-gather.2.cloned.1.call-start = ((), (), s32[]{:S(2)}) async-start(), calls=%async_computation | async-start | bytes 1966080 | tf_op jit(solution)/shard_map/all_gather | solution.py:493
  11.2 17.8 %collective-permute-start = (bf16[64,1024]{1,0:T(8,128)(2,1)}, bf16[64,1024]{1,0:T(8,128)(2,1)S(1)}, u32[]{:S(2)}, u32[]{:S(2)}) collective-permute-start(bf16[64,1024]{1,0:T(8,128)(2,1)} %get-tuple-element.41), channel_id=1, source_target_pairs={{0,4},{4,0},{8,12},{12,8},{16,20},{20,16},{24,28},{28,24},{1,5},{5... | collective-permute-start | bytes 393224 | tf_op jit(solution)/shard_map/ppermute | solution.py:505
  14.1 18.5 %collective-permute-start.1 = (bf16[64,1024]{1,0:T(8,128)(2,1)}, bf16[64,1024]{1,0:T(8,128)(2,1)S(1)}, u32[]{:S(2)}, u32[]{:S(2)}) collective-permute-start(bf16[64,1024]{1,0:T(8,128)(2,1)} %get-tuple-element.42), channel_id=1, source_target_pairs={{0,8},{4,12},{8,0},{12,4},{16,24},{20,28},{24,16},{28,20},{1,9},{5... | collective-permute-start | bytes 393224 | tf_op jit(solution)/shard_map/ppermute | solution.py:505
  15.7 22.9 %collective-permute-start.2 = (bf16[64,1024]{1,0:T(8,128)(2,1)}, bf16[64,1024]{1,0:T(8,128)(2,1)S(1)}, u32[]{:S(2)}, u32[]{:S(2)}) collective-permute-start(bf16[64,1024]{1,0:T(8,128)(2,1)} %get-tuple-element.43), channel_id=1, source_target_pairs={{0,12},{4,8},{8,4},{12,0},{16,28},{20,24},{24,20},{28,16},{1,13},{... | collective-permute-start | bytes 393224 | tf_op jit(solution)/shard_map/ppermute | solution.py:505
  15.7 22.9 %collective-permute-start.3 = (bf16[64,1024]{1,0:T(8,128)(2,1)}, bf16[64,1024]{1,0:T(8,128)(2,1)S(1)}, u32[]{:S(2)}, u32[]{:S(2)}) collective-permute-start(bf16[64,1024]{1,0:T(8,128)(2,1)} %get-tuple-element.44), channel_id=1, source_target_pairs={{0,16},{4,20},{8,24},{12,28},{16,0},{20,4},{24,8},{28,12},{1,17},{... | collective-permute-start | bytes 393224 | tf_op jit(solution)/shard_map/ppermute | solution.py:505
  18.7 19.9 %collective-permute-start.4 = (bf16[64,1024]{1,0:T(8,128)(2,1)}, bf16[64,1024]{1,0:T(8,128)(2,1)S(1)}, u32[]{:S(2)}, u32[]{:S(2)}) collective-permute-start(bf16[64,1024]{1,0:T(8,128)(2,1)} %get-tuple-element.45), channel_id=1, source_target_pairs={{0,20},{4,16},{8,28},{12,24},{16,4},{20,0},{24,12},{28,8},{1,21},{... | collective-permute-start | bytes 393224 | tf_op jit(solution)/shard_map/ppermute | solution.py:505
  22.6 5.6 %copy-start.10 = (bf16[384]{0:T(512)(128)(2,1)S(1)}, bf16[384]{0:T(512)(128)(2,1)}, u32[]{:S(2)}) copy-start(bf16[384]{0:T(512)(128)(2,1)} %param.19) | copy-start | bytes 2308
  22.6 6.4 %copy-start.17 = (bf16[64,1024]{1,0:T(8,128)(2,1)S(1)}, bf16[64,1024]{1,0:T(8,128)(2,1)}, u32[]{:S(2)}) copy-start(bf16[64,1024]{1,0:T(8,128)(2,1)} %get-tuple-element.46) | copy-start | bytes 393220
  22.6 10.1 %copy-start.15 = (bf16[64,1024]{1,0:T(8,128)(2,1)S(1)}, bf16[64,1024]{1,0:T(8,128)(2,1)}, u32[]{:S(2)}) copy-start(bf16[64,1024]{1,0:T(8,128)(2,1)} %get-tuple-element.47) | copy-start | bytes 393220
  22.6 10.2 %copy-start.9 = (bf16[31,384]{1,0:T(8,128)(2,1)S(1)}, bf16[31,384]{1,0:T(8,128)(2,1)}, u32[]{:S(2)}) copy-start(bf16[31,384]{1,0:T(8,128)(2,1)} %param.20) | copy-start | bytes 71428
  29.0 11.5 %copy-start.11 = (bf16[64,1024]{1,0:T(8,128)(2,1)}, bf16[64,1024]{1,0:T(8,128)(2,1)S(1)}, u32[]{:S(2)}) copy-start(bf16[64,1024]{1,0:T(8,128)(2,1)S(1)} %collective-permute-done.refs_1_) | copy-start | bytes 393220
  29.0 9.6 %collective-permute-start.5 = (bf16[64,1024]{1,0:T(8,128)(2,1)S(1)}, bf16[64,1024]{1,0:T(8,128)(2,1)S(1)}, u32[]{:S(2)}, u32[]{:S(2)}) collective-permute-start(bf16[64,1024]{1,0:T(8,128)(2,1)S(1)} %copy-done.17), channel_id=1, source_target_pairs={{0,24},{4,28},{8,16},{12,20},{16,8},{20,12},{24,0},{28,4},{1,25},{... | collective-permute-start | bytes 393224 | tf_op jit(solution)/shard_map/ppermute | solution.py:505
  32.7 7.8 %copy-start.12 = (bf16[64,1024]{1,0:T(8,128)(2,1)}, bf16[64,1024]{1,0:T(8,128)(2,1)S(1)}, u32[]{:S(2)}) copy-start(bf16[64,1024]{1,0:T(8,128)(2,1)S(1)} %collective-permute-done.1.refs_2_) | copy-start | bytes 393220
  32.7 7.8 %collective-permute-start.6 = (bf16[64,1024]{1,0:T(8,128)(2,1)S(1)}, bf16[64,1024]{1,0:T(8,128)(2,1)S(1)}, u32[]{:S(2)}, u32[]{:S(2)}) collective-permute-start(bf16[64,1024]{1,0:T(8,128)(2,1)S(1)} %copy-done.15), channel_id=1, source_target_pairs={{0,28},{4,24},{8,20},{12,16},{16,12},{20,8},{24,4},{28,0},{1,29},{... | collective-permute-start | bytes 393224 | tf_op jit(solution)/shard_map/ppermute | solution.py:505
  38.6 1.9 %copy-start.13 = (bf16[64,1024]{1,0:T(8,128)(2,1)}, bf16[64,1024]{1,0:T(8,128)(2,1)S(1)}, u32[]{:S(2)}) copy-start(bf16[64,1024]{1,0:T(8,128)(2,1)S(1)} %collective-permute-done.2.refs_3_) | copy-start | bytes 393220
  38.6 1.9 %copy-start.14 = (bf16[64,1024]{1,0:T(8,128)(2,1)}, bf16[64,1024]{1,0:T(8,128)(2,1)S(1)}, u32[]{:S(2)}) copy-start(bf16[64,1024]{1,0:T(8,128)(2,1)S(1)} %collective-permute-done.3.refs_4_) | copy-start | bytes 393220
  38.6 1.9 %copy-start.16 = (bf16[64,1024]{1,0:T(8,128)(2,1)}, bf16[64,1024]{1,0:T(8,128)(2,1)S(1)}, u32[]{:S(2)}) copy-start(bf16[64,1024]{1,0:T(8,128)(2,1)S(1)} %collective-permute-done.4.refs_5_) | copy-start | bytes 393220
  38.7 1.9 %copy-start.18 = (bf16[64,1024]{1,0:T(8,128)(2,1)}, bf16[64,1024]{1,0:T(8,128)(2,1)S(1)}, u32[]{:S(2)}) copy-start(bf16[64,1024]{1,0:T(8,128)(2,1)S(1)} %collective-permute-done.5.refs_6_) | copy-start | bytes 393220
  40.5 0.7 copy-start.19
  65.4 17.0 %copy-start = (f32[2,8,208,128]{3,2,1,0:T(8,128)S(1)}, f32[2,8,208,128]{3,2,1,0:T(8,128)}, u32[]{:S(2)}) copy-start(f32[2,8,208,128]{3,2,1,0:T(8,128)} %get-tuple-element.54) | copy-start | bytes 5111812
  65.4 3.9 %collective-permute-start.7 = (f32[2,8,208,128]{3,2,1,0:T(8,128)}, f32[2,8,208,128]{3,2,1,0:T(8,128)S(1)}, u32[]{:S(2)}, u32[]{:S(2)}) collective-permute-start(f32[2,8,208,128]{3,2,1,0:T(8,128)} %get-tuple-element.55), channel_id=1, source_target_pairs={{0,1},{1,0},{2,3},{3,2},{4,5},{5,4},{6,7},{7,6},{8,9},{9,8},{10,11... | collective-permute-start | bytes 5111816 | tf_op jit(solution)/shard_map/ppermute | solution.py:532
  70.5 8.2 %collective-permute-start.12 = (bf16[4,208,128]{2,1,0:T(8,128)(2,1)S(1)}, bf16[4,208,128]{2,1,0:T(8,128)(2,1)S(1)}, u32[]{:S(2)}, u32[]{:S(2)}) collective-permute-start(bf16[4,208,128]{2,1,0:T(8,128)(2,1)S(1)} %get-tuple-element.63), channel_id=1, source_target_pairs={{0,2},{1,3},{2,0},{3,1},{4,6},{5,7},{6,4},{7,5},{8,10},{9,11},{10,... | collective-permute-start | bytes 638984 | tf_op jit(solution)/shard_map/ppermute | solution.py:538
  72.1 10.3 %collective-permute-start.8 = (bf16[4,208,128]{2,1,0:T(8,128)(2,1)S(1)}, bf16[4,208,128]{2,1,0:T(8,128)(2,1)S(1)}, u32[]{:S(2)}, u32[]{:S(2)}) collective-permute-start(bf16[4,208,128]{2,1,0:T(8,128)(2,1)S(1)} %get-tuple-element.64), channel_id=1, source_target_pairs={{0,2},{1,3},{2,0},{3,1},{4,6},{5,7},{6,4},{7,5},{8,10},{9,11},{10,... | collective-permute-start | bytes 638984 | tf_op jit(solution)/shard_map/ppermute | solution.py:538
  82.6 9.3 %collective-permute-start.9 = (bf16[208,128]{1,0:T(8,128)(2,1)S(1)}, bf16[208,128]{1,0:T(8,128)(2,1)S(1)}, u32[]{:S(2)}, u32[]{:S(2)}) collective-permute-start(bf16[208,128]{1,0:T(8,128)(2,1)S(1)} %get-tuple-element.65), channel_id=1, source_target_pairs={{0,4},{4,0},{8,12},{12,8},{16,20},{20,16},{24,28},{28,24},{1,5},{5... | collective-permute-start | bytes 159752 | tf_op jit(solution)/shard_map/ppermute | solution.py:505
  83.1 11.3 %collective-permute-start.11 = (bf16[208,128]{1,0:T(8,128)(2,1)S(1)}, bf16[208,128]{1,0:T(8,128)(2,1)S(1)}, u32[]{:S(2)}, u32[]{:S(2)}) collective-permute-start(bf16[208,128]{1,0:T(8,128)(2,1)S(1)} %get-tuple-element.66), channel_id=1, source_target_pairs={{0,12},{4,8},{8,4},{12,0},{16,28},{20,24},{24,20},{28,16},{1,13},{... | collective-permute-start | bytes 159752 | tf_op jit(solution)/shard_map/ppermute | solution.py:505
  87.0 7.5 %collective-permute-start.10 = (bf16[208,128]{1,0:T(8,128)(2,1)S(1)}, bf16[208,128]{1,0:T(8,128)(2,1)S(1)}, u32[]{:S(2)}, u32[]{:S(2)}) collective-permute-start(bf16[208,128]{1,0:T(8,128)(2,1)S(1)} %get-tuple-element.67), channel_id=1, source_target_pairs={{0,8},{4,12},{8,0},{12,4},{16,24},{20,28},{24,16},{28,20},{1,9},{5... | collective-permute-start | bytes 159752 | tf_op jit(solution)/shard_map/ppermute | solution.py:505
  87.0 7.5 %collective-permute-start.13 = (bf16[208,128]{1,0:T(8,128)(2,1)S(1)}, bf16[208,128]{1,0:T(8,128)(2,1)S(1)}, u32[]{:S(2)}, u32[]{:S(2)}) collective-permute-start(bf16[208,128]{1,0:T(8,128)(2,1)S(1)} %get-tuple-element.68), channel_id=1, source_target_pairs={{0,16},{4,20},{8,24},{12,28},{16,0},{20,4},{24,8},{28,12},{1,17},{... | collective-permute-start | bytes 159752 | tf_op jit(solution)/shard_map/ppermute | solution.py:505
  90.6 6.9 %collective-permute-start.16 = (bf16[208,128]{1,0:T(8,128)(2,1)S(1)}, bf16[208,128]{1,0:T(8,128)(2,1)S(1)}, u32[]{:S(2)}, u32[]{:S(2)}) collective-permute-start(bf16[208,128]{1,0:T(8,128)(2,1)S(1)} %get-tuple-element.69), channel_id=1, source_target_pairs={{0,28},{4,24},{8,20},{12,16},{16,12},{20,8},{24,4},{28,0},{1,29},{... | collective-permute-start | bytes 159752 | tf_op jit(solution)/shard_map/ppermute | solution.py:505
  91.9 6.0 %collective-permute-start.15 = (bf16[208,128]{1,0:T(8,128)(2,1)S(1)}, bf16[208,128]{1,0:T(8,128)(2,1)S(1)}, u32[]{:S(2)}, u32[]{:S(2)}) collective-permute-start(bf16[208,128]{1,0:T(8,128)(2,1)S(1)} %get-tuple-element.70), channel_id=1, source_target_pairs={{0,24},{4,28},{8,16},{12,20},{16,8},{20,12},{24,0},{28,4},{1,25},{... | collective-permute-start | bytes 159752 | tf_op jit(solution)/shard_map/ppermute | solution.py:505
  94.5 6.4 %collective-permute-start.14 = (bf16[208,128]{1,0:T(8,128)(2,1)S(1)}, bf16[208,128]{1,0:T(8,128)(2,1)S(1)}, u32[]{:S(2)}, u32[]{:S(2)}) collective-permute-start(bf16[208,128]{1,0:T(8,128)(2,1)S(1)} %get-tuple-element.71), channel_id=1, source_target_pairs={{0,20},{4,16},{8,28},{12,24},{16,4},{20,0},{24,12},{28,8},{1,21},{... | collective-permute-start | bytes 159752 | tf_op jit(solution)/shard_map/ppermute | solution.py:505
  101.0 12.4 %copy-start.1 = (bf16[208,128]{1,0:T(8,128)(2,1)}, bf16[208,128]{1,0:T(8,128)(2,1)S(1)}, u32[]{:S(2)}) copy-start(bf16[208,128]{1,0:T(8,128)(2,1)S(1)} %fusion.16.refs_0_) | copy-start | bytes 159748
  101.0 6.0 %collective-permute-start.22 = (bf16[208,128]{1,0:T(8,128)(2,1)S(1)}, bf16[208,128]{1,0:T(8,128)(2,1)S(1)}, u32[]{:S(2)}, u32[]{:S(2)}) collective-permute-start(bf16[208,128]{1,0:T(8,128)(2,1)S(1)} %fusion.16.refs_0_), channel_id=1, source_target_pairs={{0,24},{4,28},{8,16},{12,20},{16,8},{20,12},{24,0},{28,4},{1,25},{... | collective-permute-start | bytes 159752 | tf_op jit(solution)/shard_map/ppermute | solution.py:505
  102.6 5.5 %collective-permute-start.20 = (bf16[208,128]{1,0:T(8,128)(2,1)S(1)}, bf16[208,128]{1,0:T(8,128)(2,1)S(1)}, u32[]{:S(2)}, u32[]{:S(2)}) collective-permute-start(bf16[208,128]{1,0:T(8,128)(2,1)S(1)} %fusion.16.refs_0_), channel_id=1, source_target_pairs={{0,16},{4,20},{8,24},{12,28},{16,0},{20,4},{24,8},{28,12},{1,17},{... | collective-permute-start | bytes 159752 | tf_op jit(solution)/shard_map/ppermute | solution.py:505
  102.6 6.6 %collective-permute-start.18 = (bf16[208,128]{1,0:T(8,128)(2,1)S(1)}, bf16[208,128]{1,0:T(8,128)(2,1)S(1)}, u32[]{:S(2)}, u32[]{:S(2)}) collective-permute-start(bf16[208,128]{1,0:T(8,128)(2,1)S(1)} %fusion.16.refs_0_), channel_id=1, source_target_pairs={{0,8},{4,12},{8,0},{12,4},{16,24},{20,28},{24,16},{28,20},{1,9},{5... | collective-permute-start | bytes 159752 | tf_op jit(solution)/shard_map/ppermute | solution.py:505
  105.4 4.7 %collective-permute-start.17 = (bf16[208,128]{1,0:T(8,128)(2,1)S(1)}, bf16[208,128]{1,0:T(8,128)(2,1)S(1)}, u32[]{:S(2)}, u32[]{:S(2)}) collective-permute-start(bf16[208,128]{1,0:T(8,128)(2,1)S(1)} %fusion.16.refs_0_), channel_id=1, source_target_pairs={{0,4},{4,0},{8,12},{12,8},{16,20},{20,16},{24,28},{28,24},{1,5},{5... | collective-permute-start | bytes 159752 | tf_op jit(solution)/shard_map/ppermute | solution.py:505
  107.0 6.4 %copy-start.2 = (bf16[208,128]{1,0:T(8,128)(2,1)}, bf16[208,128]{1,0:T(8,128)(2,1)S(1)}, u32[]{:S(2)}) copy-start(bf16[208,128]{1,0:T(8,128)(2,1)S(1)} %collective-permute-done.22.refs_6_) | copy-start | bytes 159748
  107.0 4.1 %collective-permute-start.23 = (bf16[208,128]{1,0:T(8,128)(2,1)S(1)}, bf16[208,128]{1,0:T(8,128)(2,1)S(1)}, u32[]{:S(2)}, u32[]{:S(2)}) collective-permute-start(bf16[208,128]{1,0:T(8,128)(2,1)S(1)} %collective-permute-done.22.refs_6_), channel_id=1, source_target_pairs={{0,4},{4,0},{8,12},{12,8},{16,20},{20,16},{24,28},{28,24},{1,5},{5... | collective-permute-start | bytes 159752 | tf_op jit(solution)/shard_map/ppermute | solution.py:505
  108.1 5.2 %copy-start.3 = (bf16[208,128]{1,0:T(8,128)(2,1)}, bf16[208,128]{1,0:T(8,128)(2,1)S(1)}, u32[]{:S(2)}) copy-start(bf16[208,128]{1,0:T(8,128)(2,1)S(1)} %collective-permute-done.20.refs_4_) | copy-start | bytes 159748
  108.1 4.1 %collective-permute-start.21 = (bf16[208,128]{1,0:T(8,128)(2,1)S(1)}, bf16[208,128]{1,0:T(8,128)(2,1)S(1)}, u32[]{:S(2)}, u32[]{:S(2)}) collective-permute-start(bf16[208,128]{1,0:T(8,128)(2,1)S(1)} %collective-permute-done.20.refs_4_), channel_id=1, source_target_pairs={{0,4},{4,0},{8,12},{12,8},{16,20},{20,16},{24,28},{28,24},{1,5},{5... | collective-permute-start | bytes 159752 | tf_op jit(solution)/shard_map/ppermute | solution.py:505
  109.2 4.2 %copy-start.4 = (bf16[208,128]{1,0:T(8,128)(2,1)}, bf16[208,128]{1,0:T(8,128)(2,1)S(1)}, u32[]{:S(2)}) copy-start(bf16[208,128]{1,0:T(8,128)(2,1)S(1)} %collective-permute-done.18.refs_2_) | copy-start | bytes 159748
  109.2 4.1 %collective-permute-start.19 = (bf16[208,128]{1,0:T(8,128)(2,1)S(1)}, bf16[208,128]{1,0:T(8,128)(2,1)S(1)}, u32[]{:S(2)}, u32[]{:S(2)}) collective-permute-start(bf16[208,128]{1,0:T(8,128)(2,1)S(1)} %collective-permute-done.18.refs_2_), channel_id=1, source_target_pairs={{0,4},{4,0},{8,12},{12,8},{16,20},{20,16},{24,28},{28,24},{1,5},{5... | collective-permute-start | bytes 159752 | tf_op jit(solution)/shard_map/ppermute | solution.py:505
  110.1 3.2 %copy-start.5 = (bf16[208,128]{1,0:T(8,128)(2,1)}, bf16[208,128]{1,0:T(8,128)(2,1)S(1)}, u32[]{:S(2)}) copy-start(bf16[208,128]{1,0:T(8,128)(2,1)S(1)} %collective-permute-done.17.refs_1_) | copy-start | bytes 159748
  111.1 2.3 %copy-start.6 = (bf16[208,128]{1,0:T(8,128)(2,1)}, bf16[208,128]{1,0:T(8,128)(2,1)S(1)}, u32[]{:S(2)}) copy-start(bf16[208,128]{1,0:T(8,128)(2,1)S(1)} %collective-permute-done.23.refs_7_) | copy-start | bytes 159748
  112.2 1.1 copy-start.7
  113.4 0.6 copy-start.8
Sparse Core Ops, SparseCore 0:
  9.6 22.3 all-gather.1

commit v3 on v2

--- a/solution.py
+++ b/solution.py
@@ -72,7 +72,13 @@
     return lax.dot_general(a, b, (((0,), (0,)), ((), ())), preferred_element_type=F32)
 
 
-def pick_kernel(ids_ref, index_ref, rows_ref, *out_refs):
+def pick_kernel(ours_ref, index_ref, rows_ref, proj_ref, taps_ref, gain_ref, packed_ref, *refs):
+    out_refs, tail_ref = refs[:-1], refs[-1]
+    depth, tap_count = proj_ref.shape[0], taps_ref.shape[0]
+    packed_ref[:depth] = proj_ref[...]
+    tail_ref[:tap_count] = taps_ref[...].astype(F32)
+    tail_ref[tap_count:] = gain_ref[...].astype(F32)
+    packed_ref[depth:] = tail_ref[...].astype(BF16)
     count = rows_ref.shape[0]
     rows = rows_ref[...]
     if len(out_refs) == 1:
@@ -84,7 +90,7 @@
     slot = index_ref.shape[1]
     number = lax.broadcasted_iota(jnp.int32, (count, slot), 0)
     for k, out_ref in enumerate(out_refs):
-        index = index_ref[pl.ds(ids_ref[0, 2] ^ k, 1), :]
+        index = index_ref[pl.ds(ours_ref[0, 0] ^ k, 1), :]
         choose = jnp.where(number == index, 1.0, 0.0).astype(BF16)
         out_ref[...] = dot_t(choose, rows).astype(BF16)
 
@@ -99,7 +105,7 @@
     return out
 
 
-def unpack_kernel(count, ids_ref, *refs):
+def unpack_kernel(count, ours_ref, *refs):
     piece_refs, (proj_ref, taps_ref, gain_ref, held_ref) = refs[:count], refs[count:]
     parts, part, _ = held_ref.shape
     for k in range(parts):
@@ -110,14 +116,14 @@
     for tile in range(width // 128):
         lanes = slice(tile * 128, tile * 128 + 128)
         for p, start, stop, offset in runs(tile * held, tile * held + depth, part):
-            proj_ref[offset : offset + stop - start, lanes] = held_ref[p ^ ids_ref[0, 2], start:stop]
+            proj_ref[offset : offset + stop - start, lanes] = held_ref[p ^ ours_ref[0, 0], start:stop]
         last = [
-            held_ref[p ^ ids_ref[0, 2], start:stop]
+            held_ref[p ^ ours_ref[0, 0], start:stop]
             for p, start, stop, _ in runs(tile * held + depth, tile * held + held, part)
         ]
         last = last[0] if len(last) == 1 else jnp.concatenate(last, axis=0)
         taps_ref[:, lanes] = last[: taps_ref.shape[0]]
-        gain_ref[:, lanes] = last[taps_ref.shape[0] : taps_ref.shape[0] + 1]
+        gain_ref[lanes] = last[taps_ref.shape[0] : taps_ref.shape[0] + 1].reshape(128)
 
 
 def prep_kernel(pos_ref, hi_ref, lo_ref, back_ref, ahead_ref, behind_ref):
@@ -141,10 +147,10 @@
         behind_ref[BEHIND_AT[part] : BEHIND_AT[part + 1]] = wide[:held].astype(BF16)
 
 
-def layer_kernel(count, ids_ref, *refs):
+def layer_kernel(count, core_ref, side_ref, ours_ref, *refs):
     arrived_refs = refs[:count]
     (
-        take_ref, tapf_ref, lag_ref, small_in_ref, params_hbm, up_hbm, ahead_hbm, behind_hbm,
+        take_ref, tapf_ref, lag_ref, params_hbm, up_hbm, ahead_hbm, behind_hbm,
         keep_ref, send_ref, loss_ref,
         params_ref, up_ref, ahead_ref, behind_ref, sems,
         frames_ref, frames_t_ref, x_ref, h_ref, stat_ref, acc_ref, acc2_ref,
@@ -190,7 +196,7 @@
 
     def project(i, carry):
         cols = pl.ds(pl.multiple_of(i * CH, CH), CH)
-        x = dot(frames_ref[...], params_ref[:, cols])
+        x = dot(frames_ref[...], params_ref[:depth, cols])
         x_ref[:, cols] = x
         acc_ref[...] += x[:, :128] + x[:, 128:]
         return carry
@@ -222,86 +228,106 @@
         (a, b), (c, d), (e, f) = slices
         return jnp.concatenate([hi[a:b], hi[c:d], lo[e:f]], axis=0)
 
-    def middle(i, carry):
+    def chunk(i, b):
+        hi_b, lo_b, ghi_b, glo_b = hi_ref.at[b], lo_ref.at[b], ghi_ref.at[b], glo_ref.at[b]
+        spec_b, nspec_b, phi_b, plo_b = spec_ref.at[b], nspec_ref.at[b], phi_ref.at[b], plo_ref.at[b]
+        coef_b, c_b = coef_ref.at[b], c_ref.at[b]
         cols = pl.ds(pl.multiple_of(i * CH, CH), CH)
-        gain = small_in_ref[16:32, cols][15:16].astype(F32)
-        taps = small_in_ref[:, cols]
-        coef_ref[...] = dot(tapf_ref[...], jnp.concatenate([taps, taps], axis=0))
-        for rows in tiles:
+        gain = params_ref[depth + 16 : depth + 32, cols][15:16].astype(F32)
+        taps = params_ref[depth : depth + 32, cols]
+        coef_b[...] = dot(tapf_ref[...], jnp.concatenate([taps, taps], axis=0))
+        for t, rows in enumerate(tiles):
             xhat = (x_ref[rows, cols] - twice(stat_ref[0, rows])) * twice(stat_ref[1, rows])
             hi, lo = split(xhat * gain)
-            hi_ref[rows] = hi
-            lo_ref[rows] = lo
+            hi_b[rows] = hi
+            lo_b[rows] = lo
+            if t in (2, 5):
+                yield
+        yield
         for j in range(3):
-            nspec_ref[j] = dot(ahead_ref[:, block_of[j]], stack(hi_ref, lo_ref, k_slices(BLOCK_STEPS[j], BLOCK_K[j])))
+            nspec_b[j] = dot(ahead_ref[:, block_of[j]], stack(hi_b, lo_b, k_slices(BLOCK_STEPS[j], BLOCK_K[j])))
+            yield
         for j in range(3):
             for f in range(0, FREQS, 32):
                 lower, upper = slice(f, f + 32), slice(FREQS + f, FREQS + f + 32)
-                re, im = nspec_ref[j, lower], nspec_ref[j, upper]
-                cre, cim = coef_ref[lower], coef_ref[upper]
+                re, im = nspec_b[j, lower], nspec_b[j, upper]
+                cre, cim = coef_b[lower], coef_b[upper]
                 hi, lo = split(re * cre - im * cim)
-                phi_ref[j, lower] = hi
-                plo_ref[j, lower] = lo
+                phi_b[j, lower] = hi
+                plo_b[j, lower] = lo
                 hi, lo = split(re * cim + im * cre)
-                phi_ref[j, upper] = hi
-                plo_ref[j, upper] = lo
-        parts = [
-            dot(behind_ref[back_wide[j]], jnp.concatenate([phi_ref[j], phi_ref[j], plo_ref[j]], axis=0))
-            for j in range(3)
-        ]
-        c_ref[0:112] = parts[0][0:112]
-        c_ref[112:224] = parts[0][112:224] + parts[1][0:112]
-        c_ref[224:288] = parts[1][112:176]
-        c_ref[288:400] = parts[1][176:288] + parts[2][0:112]
-        c_ref[400:512] = parts[2][112:224]
+                phi_b[j, upper] = hi
+                plo_b[j, upper] = lo
+            yield
+        parts = []
+        for j in range(3):
+            held_j = jnp.concatenate([phi_b[j], phi_b[j], plo_b[j]], axis=0)
+            parts.append(dot(behind_ref[back_wide[j]], held_j))
+            if j == 1:
+                c_b[0:112] = parts[0][0:112]
+                c_b[112:224] = parts[0][112:224] + parts[1][0:112]
+                c_b[224:288] = parts[1][112:176]
+            if j == 2:
+                c_b[288:400] = parts[1][176:288] + parts[2][0:112]
+                c_b[400:512] = parts[2][112:224]
+            yield
         loss = jnp.zeros((1, CH), F32)
-        for rows in tiles:
-            conv = c_ref[rows]
+        for t, rows in enumerate(tiles):
+            conv = c_b[rows]
             sig = jax.nn.sigmoid(conv)
             go = up_ref[rows, cols].astype(F32) * twice(stat_ref[2, rows])
             out = x_ref[rows, cols] + conv * sig
             loss = loss + jnp.sum(out * go, axis=0, keepdims=True)
             hi, lo = split(go * (sig * (1.0 + conv * (1.0 - sig))))
-            ghi_ref[rows] = hi
-            glo_ref[rows] = lo
+            ghi_b[rows] = hi
+            glo_b[rows] = lo
+            if t in (2, 5):
+                yield
         lossacc_ref[...] += loss
+        yield
         for j in range(3):
-            spec_ref[j] = dot(ahead_ref[:, wide_of[j]], stack(ghi_ref, glo_ref, k_slices(WIDE_STEPS[j], WIDE_K[j])))
+            spec_b[j] = dot(ahead_ref[:, wide_of[j]], stack(ghi_b, glo_b, k_slices(WIDE_STEPS[j], WIDE_K[j])))
+            yield
         for f in range(0, FREQS, 32):
             lower, upper = slice(f, f + 32), slice(FREQS + f, FREQS + f + 32)
-            cre, cim = coef_ref[lower], coef_ref[upper]
+            cre, cim = coef_b[lower], coef_b[upper]
             zre = jnp.zeros((32, CH), F32)
             zim = jnp.zeros((32, CH), F32)
             for j in range(3):
-                nre, nim = nspec_ref[j, lower], nspec_ref[j, upper]
-                re, im = spec_ref[j, lower], spec_ref[j, upper]
+                nre, nim = nspec_b[j, lower], nspec_b[j, upper]
+                re, im = spec_b[j, lower], spec_b[j, upper]
                 zre = zre + (nre * re + nim * im)
                 zim = zim + (nim * re - nre * im)
                 hi, lo = split(re * cre + im * cim)
-                phi_ref[j, lower] = hi
-                plo_ref[j, lower] = lo
+                phi_b[j, lower] = hi
+                plo_b[j, lower] = lo
                 hi, lo = split(im * cre - re * cim)
-                phi_ref[j, upper] = hi
-                plo_ref[j, upper] = lo
+                phi_b[j, upper] = hi
+                plo_b[j, upper] = lo
             hi, lo = split(zre)
-            phi_ref[3, lower] = hi
-            plo_ref[3, lower] = lo
+            phi_b[3, lower] = hi
+            plo_b[3, lower] = lo
             hi, lo = split(zim)
-            phi_ref[3, upper] = hi
-            plo_ref[3, upper] = lo
-        tap_grad = dot(lag_ref[...], jnp.concatenate([phi_ref[3], phi_ref[3], plo_ref[3]], axis=0))
-        parts = [
-            dot(behind_ref[back_block[j]], jnp.concatenate([phi_ref[j], phi_ref[j], plo_ref[j]], axis=0))
-            for j in range(3)
-        ]
-        c_ref[0:128] = parts[0][0:128]
-        c_ref[128:208] = parts[0][128:208] + parts[1][0:80]
-        c_ref[208:304] = parts[1][80:176]
-        c_ref[304:384] = parts[1][176:256] + parts[2][0:80]
-        c_ref[384:512] = parts[2][80:208]
+            phi_b[3, upper] = hi
+            plo_b[3, upper] = lo
+            if f != 32:
+                yield
+        parts = []
+        for j in range(3):
+            held_j = jnp.concatenate([phi_b[j], phi_b[j], plo_b[j]], axis=0)
+            parts.append(dot(behind_ref[back_block[j]], held_j))
+            if j == 1:
+                c_b[0:128] = parts[0][0:128]
+                c_b[128:208] = parts[0][128:208] + parts[1][0:80]
+                c_b[208:304] = parts[1][80:176]
+            if j == 2:
+                c_b[304:384] = parts[1][176:256] + parts[2][0:80]
+                c_b[384:512] = parts[2][80:208]
+            yield
+        tap_grad = dot(lag_ref[...], jnp.concatenate([phi_b[3], phi_b[3], plo_b[3]], axis=0))
         gain_grad = jnp.zeros((1, CH), F32)
-        for rows in tiles:
-            gn = c_ref[rows]
+        for t, rows in enumerate(tiles):
+            gn = c_b[rows]
             xhat = (x_ref[rows, cols] - twice(stat_ref[0, rows])) * twice(stat_ref[1, rows])
             gain_grad = gain_grad + jnp.sum(gn * xhat, axis=0, keepdims=True)
             h = gn * gain
@@ -309,11 +335,21 @@
             h_ref[rows, cols] = h
             acc_ref[rows] += h[:, :128] + h[:, 128:]
             acc2_ref[rows] += hx[:, :128] + hx[:, 128:]
+            if t in (2, 5):
+                yield
         last = lax.broadcasted_iota(jnp.int32, (32, CH), 0) == 31
         small_ref[:, cols] = jnp.where(last, gain_grad, tap_grad)
+
+    def middle(i, carry):
+        lead, follow = chunk(2 * i, 0), chunk(2 * i + 1, 1)
+        for _ in range(3):
+            next(lead)
+        running = [lead, follow]
+        while running:
+            running = [g for g in running if next(g, running) is not running]
         return carry
 
-    lax.fori_loop(0, chunks, middle, 0)
+    lax.fori_loop(0, chunks // 2, middle, 0)
     loss_ref[...] = jnp.sum(lossacc_ref[...], axis=1, keepdims=True)
     for rows in tiles:
         m1 = jnp.sum(acc_ref[rows], axis=1, keepdims=True) * (1.0 / width)
@@ -325,36 +361,41 @@
     per_block = width // (2 * halves) // 128
     held = depth + 32
 
+    def grad_rows(i):
+        cols = slice(i * CH, (i + 1) * CH)
+        for rows in tiles:
+            inv = twice(stat_ref[1, rows])
+            xhat = (x_ref[rows, cols] - twice(stat_ref[0, rows])) * inv
+            go = up_ref[rows, cols].astype(F32) * twice(stat_ref[2, rows])
+            inner = h_ref[rows, cols] - twice(acc_ref[rows]) - xhat * twice(acc2_ref[rows])
+            hi_ref[i % 2, rows] = (go + inv * inner).astype(BF16)
+
     def finish(core):
+        grad_rows(0)
         for i in range(chunks):
-            cols = slice(i * CH, (i + 1) * CH)
-            for rows in tiles:
-                inv = twice(stat_ref[1, rows])
-                xhat = (x_ref[rows, cols] - twice(stat_ref[0, rows])) * inv
-                go = up_ref[rows, cols].astype(F32) * twice(stat_ref[2, rows])
-                inner = h_ref[rows, cols] - twice(acc_ref[rows]) - xhat * twice(acc2_ref[rows])
-                hi_ref[rows] = (go + inv * inner).astype(BF16)
-            weight = dot(frames_t_ref[...], hi_ref[...])
+            if i + 1 < chunks:
+                grad_rows(i + 1)
+            weight = dot(frames_t_ref[...], hi_ref[i % 2])
             for half in range(CH // 128):
                 tile = i * (CH // 128) + half
                 block, inside = tile // per_block, (tile % per_block) * held
                 lanes = slice(half * 128, half * 128 + 128)
                 small = small_ref[:, tile * 128 : (tile + 1) * 128]
                 target = keep_ref if block % 2 == core else send_ref
-                side = (block // 2) ^ ids_ref[0, 1]
+                side = (block // 2) ^ side_ref[0, 0]
                 for p, start, stop, offset in runs(inside, inside + depth, part):
                     value = weight[offset : offset + stop - start, lanes]
-                    target[side, p ^ ids_ref[0, 2], start:stop] = value
+                    target[side, p ^ ours_ref[0, 0], start:stop] = value
                 for p, start, stop, offset in runs(inside + depth, inside + held, part):
                     value = small[offset : offset + stop - start]
-                    target[side, p ^ ids_ref[0, 2], start:stop] = value
-
-    pl.when(ids_ref[0, 0] == 0)(lambda: finish(0))
-    pl.when(ids_ref[0, 0] != 0)(lambda: finish(1))
+                    target[side, p ^ ours_ref[0, 0], start:stop] = value
+
+    pl.when(core_ref[0, 0] == 0)(lambda: finish(0))
+    pl.when(core_ref[0, 0] != 0)(lambda: finish(1))
     for p, start, stop, _ in runs(per_block * held, parts * part, part):
         for side in range(halves):
             for ref in (keep_ref, send_ref):
-                ref[side, p ^ ids_ref[0, 2], start:stop] = jnp.zeros((stop - start, 128), F32)
+                ref[side, p ^ ours_ref[0, 0], start:stop] = jnp.zeros((stop - start, 128), F32)
 
 
 def vmem(count):
@@ -364,7 +405,7 @@
 SCALARS = pl.BlockSpec(memory_space=pltpu.SMEM)
 
 
-def pick(ids, index, rows):
+def pick(ours, index, rows, proj, taps, gain):
     dp, slot = index.shape
     width = rows.shape[1]
     if dp > FEW:
@@ -374,24 +415,25 @@
         shapes = [jax.ShapeDtypeStruct((slot, width), BF16)] * dp
     return pl.pallas_call(
         pick_kernel,
-        out_shape=shapes,
-        in_specs=[SCALARS] + vmem(2),
-        out_specs=vmem(len(shapes)),
+        out_shape=[jax.ShapeDtypeStruct((proj.shape[0] + 32, proj.shape[1]), BF16)] + shapes,
+        in_specs=[SCALARS] + vmem(5),
+        out_specs=vmem(1 + len(shapes)),
+        scratch_shapes=[pltpu.VMEM((32, proj.shape[1]), F32)],
         compiler_params=pltpu.CompilerParams(vmem_limit_bytes=VMEM_LIMIT),
         cost_estimate=pl.CostEstimate(
             flops=2 * dp * slot * rows.size, bytes_accessed=6 * rows.size, transcendentals=0
         ),
         name="pick_rows",
-    )(ids, index, rows)
-
-
-def unpack(ids, pieces, parts, part, depth, tap_count, width):
+    )(ours, index, rows, proj, taps, gain)
+
+
+def unpack(ours, pieces, parts, part, depth, tap_count, width):
     return pl.pallas_call(
         functools.partial(unpack_kernel, len(pieces)),
         out_shape=[
             jax.ShapeDtypeStruct((depth, width), F32),
             jax.ShapeDtypeStruct((tap_count, width), F32),
-            jax.ShapeDtypeStruct((1, width), F32),
+            jax.ShapeDtypeStruct((width,), F32),
         ],
         in_specs=[SCALARS] + vmem(len(pieces)),
         out_specs=vmem(3),
@@ -399,7 +441,7 @@
         compiler_params=pltpu.CompilerParams(vmem_limit_bytes=VMEM_LIMIT),
         cost_estimate=pl.CostEstimate(flops=10**6, bytes_accessed=12 * 10**5, transcendentals=0),
         name="unpack_gradients",
-    )(ids, *pieces)
+    )(ours, *pieces)
 
 
 def positions(utterances):
@@ -438,7 +480,7 @@
 
 
 def layer(
-    ids, arrived, take, small, params, upstream, tap_fwd, lags, ahead, behind, parts, part, halves
+    ids, arrived, take, params, upstream, tap_fwd, lags, ahead, behind, parts, part, halves
 ):
     steps, width = upstream.shape
     depth = arrived[0].shape[1] // 2
@@ -456,16 +498,16 @@
         pltpu.VMEM((3, steps, 128), F32),
         pltpu.VMEM((steps, 128), F32),
         pltpu.VMEM((steps, 128), F32),
-        pltpu.VMEM((steps, CH), BF16),
-        pltpu.VMEM((steps, CH), BF16),
-        pltpu.VMEM((steps, CH), BF16),
-        pltpu.VMEM((steps, CH), BF16),
-        pltpu.VMEM((3, POINTS, CH), F32),
-        pltpu.VMEM((3, POINTS, CH), F32),
-        pltpu.VMEM((4, POINTS, CH), BF16),
-        pltpu.VMEM((4, POINTS, CH), BF16),
-        pltpu.VMEM((POINTS, CH), F32),
-        pltpu.VMEM((steps, CH), F32),
+        pltpu.VMEM((2, steps, CH), BF16),
+        pltpu.VMEM((2, steps, CH), BF16),
+        pltpu.VMEM((2, steps, CH), BF16),
+        pltpu.VMEM((2, steps, CH), BF16),
+        pltpu.VMEM((2, 3, POINTS, CH), F32),
+        pltpu.VMEM((2, 3, POINTS, CH), F32),
+        pltpu.VMEM((2, 4, POINTS, CH), BF16),
+        pltpu.VMEM((2, 4, POINTS, CH), BF16),
+        pltpu.VMEM((2, POINTS, CH), F32),
+        pltpu.VMEM((2, steps, CH), F32),
         pltpu.VMEM((32, width), F32),
         pltpu.VMEM((1, CH), F32),
     ]
@@ -476,13 +518,13 @@
             jax.ShapeDtypeStruct((halves, parts, part, 128), F32),
             jax.ShapeDtypeStruct((1, 1), F32),
         ],
-        in_specs=[SCALARS] + vmem(len(arrived) + 4) + [hbm] * 4,
+        in_specs=[SCALARS] * 3 + vmem(len(arrived) + 3) + [hbm] * 4,
         out_specs=vmem(3),
         scratch_shapes=scratch,
         compiler_params=pltpu.CompilerParams(vmem_limit_bytes=VMEM_LIMIT),
         cost_estimate=pl.CostEstimate(flops=10**10, bytes_accessed=16 * 10**6, transcendentals=10**6),
         name="layer_step",
-    )(ids, *arrived, take, tap_fwd, lags, small, params, upstream, ahead, behind)
+    )(*ids, *arrived, take, tap_fwd, lags, params, upstream, ahead, behind)
 
 
 def per_device(
@@ -490,15 +532,15 @@
 ):
     tap_count = conv_kernel.shape[0]
     f_hi, f_lo, back, tap_fwd, lags = [jnp.asarray(m) for m in transforms(tap_count)]
-    params = lax.all_gather(in_proj, "fsdp", axis=1, tiled=True)
     few = dp <= FEW
     place = lax.axis_index("fsdp")
-    ours = lax.axis_index("dp") if few else 0
-    ids = jnp.stack([place % 2, place // 2, ours]).astype(jnp.int32)[None, :]
+    ours = lax.axis_index("dp") if few else jnp.zeros((), jnp.int32)
+    ids = [v.astype(jnp.int32).reshape(1, 1) for v in (place % 2, place // 2, ours)]
     wanted = send_rows[0, 0]
-    outgoing = pick(ids, wanted, cached[0, 0])
-    outgoing, take_own, utt_own, taps_own, gain_own = lax.optimization_barrier(
-        (outgoing, take_rows[0, 0], utt_index[0, 0], conv_kernel, norm_gain)
+    packed, *outgoing = pick(ids[2], wanted, cached[0, 0], in_proj, conv_kernel, norm_gain[None, :])
+    params = lax.all_gather(packed, "fsdp", axis=1, tiled=True)
+    outgoing, take_own, utt_own = lax.optimization_barrier(
+        (outgoing, take_rows[0, 0], utt_index[0, 0])
     )
 
     def swap(value, k):
@@ -513,9 +555,6 @@
         sent = outgoing[0].reshape(wanted.shape + outgoing[0].shape[1:])
         back_in = lax.all_to_all(sent, "dp", split_axis=0, concat_axis=0, tiled=True)
         arrived = [back_in.reshape(-1, back_in.shape[2])]
-    small = lax.all_gather(
-        jnp.concatenate([taps_own, gain_own[None, :]], axis=0), "fsdp", axis=1, tiled=True
-    )
     take = jnp.repeat(take_own, 2)[None, :]
     ahead, behind = prepare(jnp.repeat(utt_own, 2), f_hi, f_lo, back)
 
@@ -526,24 +565,25 @@
     part = -(-part // 16) * 16
     halves = fsdp // 2
     keep, send, loss = layer(
-        ids, arrived, take, small, params, upstream[0, 0], tap_fwd, lags, ahead, behind,
+        ids, arrived, take, params, upstream[0, 0], tap_fwd, lags, ahead, behind,
         dp, part, halves,
     )
     other = lax.ppermute(send, "fsdp", [(i, i ^ 1) for i in range(fsdp)])
     half = dp // 2
     across = [(i, i ^ 2) for i in range(fsdp)]
-    sums = {}
-    for low, high in ((half, dp), (0, half)):
-        theirs = (keep[1, low:high] + other[1, low:high]).astype(BF16)
-        theirs = lax.ppermute(theirs, "fsdp", across)
-        mine = keep[0, low:high] + other[0, low:high]
-        sums[low] = mine + theirs.astype(F32)
+    spans = ((half, dp), (0, half))
+    sent = [(keep[1, low:high] + other[1, low:high]).astype(BF16) for low, high in spans]
+    far_in, near_in = [lax.ppermute(v, "fsdp", across) for v in sent]
+    far_sum = keep[0, half:] + other[0, half:] + far_in.astype(F32)
+    far_out = far_sum.astype(BF16)
+    near_in, far_out = lax.optimization_barrier((near_in, far_out))
+    near_sum = keep[0, :half] + other[0, :half] + near_in.astype(F32)
+    near_out = near_sum.astype(BF16)
     if few:
         got = {}
         for k in far_first:
-            low = half if k >= half else 0
-            got[k] = swap(sums[low][k - low].astype(BF16), k)
-        total = sums[0][0]
+            got[k] = swap(far_out[k - half] if k >= half else near_out[k], k)
+        total = near_sum[0]
         for k in range(1, dp):
             total = total + got[k].astype(F32)
         piece = total.astype(BF16)
@@ -553,12 +593,12 @@
             pieces[k + 1] = swap(far[k], 1)
         pieces = [pieces[k] for k in range(dp)]
     else:
-        chip = jnp.concatenate([sums[0], sums[half]], axis=0).astype(BF16)
+        chip = jnp.concatenate([near_out, far_out], axis=0)
         shared = lax.all_to_all(chip, "dp", split_axis=0, concat_axis=0, tiled=True)
         piece = jnp.sum(shared.astype(F32), axis=0).astype(BF16)
         pieces = [lax.all_gather(piece, "dp", axis=0, tiled=True)]
-    proj, taps, gain = unpack(ids, pieces, dp, part, depth, tap_count, shard_cols)
-    return (proj, taps, gain[0], loss)
+    proj, taps, gain = unpack(ids[2], pieces, dp, part, depth, tap_count, shard_cols)
+    return (proj, taps, gain, loss)
 
 
 def solution(mesh):

time: 124 us -> 119 us (0.960)
  blocking collectives: 5.83 us -> 0 us
  Pallas kernels: 34.4 us -> 30 us
  waiting for transfers between devices: 26.2 us -> 30.5 us
  other arithmetic: 4.44 us -> 2.51 us
    all_gather x1 -> x0, blocking collectives: 5.83 us -> none  [per_device(): lax.all_gather(jnp.concatenate([taps_own, gain_own[None, :]], axis=0), 'f...]
    ppermute x21, waiting for transfers between devices: 11.9 us -> 16.9 us  [swap(): return lax.ppermute(value, 'dp', [(i, i ^ k) for i in range(dp)])]
    pallas_call x1, Pallas kernels: 24.2 us -> 19.5 us  [layer(): pl.pallas_call(functools.partial(layer_kernel, len(arrived)), out_shape=[...]
    pallas_call x1 -> x0, other arithmetic: 1.26 us -> none  [unpack(): pl.pallas_call(functools.partial(unpack_kernel, len(pieces)), out_shape=[...]
    broadcast_in_dim x1, local copies, waits for them, and re-layouts: 0.01 us -> 1.24 us  [per_device(): norm_gain[None, :]]
  transfers between devices with their start and end apart: 25 -> 25, of which waited for: 11 -> 11; matrix products, arithmetic and copies ran while one was open for 3% -> 3% of each run, Pallas kernels for 7% -> 5%
where the time goes in v3:
time: 119 us; the launch traced here: 118 us
  starting transfers between devices  36.3 us (31%)
  waiting for transfers between devices  30.5 us (26%)
  Pallas kernels  30 us (25%)
  between operations  14.3 us (12%)
  local copies, waits for them, and re-layouts  4.77 us (4%)
  other arithmetic  2.51 us (2%)
    ppermute x21, starting transfers between devices, swap(): return lax.ppermute(value, 'dp', [(i, i ^ k) for i in range(dp)])  34.1 us
    pallas_call x1, Pallas kernels, layer(): pl.pallas_call(functools.partial(layer_kernel, len(arrived)), out_shape=[...  19.5 us
    ppermute x21, waiting for transfers between devices, swap(): return lax.ppermute(value, 'dp', [(i, i ^ k) for i in range(dp)])  16.9 us
    ppermute x2, waiting for transfers between devices, per_device(): far_in, near_in = [lax.ppermute(v, 'fsdp', across) for v in sent]  9.75 us
    pallas_call x1, Pallas kernels, prepare(): pl.pallas_call(prep_kernel, out_shape=shapes, in_specs=vmem(4), out_specs...  5.59 us
    ppermute x1, waiting for transfers between devices, per_device(): other = lax.ppermute(send, 'fsdp', [(i, i ^ 1) for i in range(fsdp)])  3.8 us
    pallas_call x1, Pallas kernels, pick(): pl.pallas_call(pick_kernel, out_shape=[jax.ShapeDtypeStruct((proj.shape[0...  2.93 us
  transfers between devices with their start and end apart: 25, of which 11 were waited for; matrix products, arithmetic and copies ran while one was open for 3% of the time, Pallas kernels for 5%

profile of v3, /device:TPU:0, one launch (start us, length us, event | category | flops | bytes accessed | tf_op | source)
XLA Modules:
  0.0 118.4 jit_solution(908778776058413365)
XLA Ops:
  7.2 0.0 all-gather.2.cloned.1.call-start
  7.2 1.2 %broadcast_in_dim.28.gain_ref = bf16[1,384]{1,0:T(2,128)(2,1)} reshape(bf16[384]{0:T(512)(128)(2,1)} %param.19) | data formatting | bytes 1536 | tf_op jit(solution)/shard_map/broadcast_in_dim | solution.py:540
  8.5 2.9 %pick_rows.1 = (bf16[544,384]{1,0:T(8,128)(2,1)}, bf16[64,1024]{1,0:T(8,128)(2,1)}, bf16[64,1024]{1,0:T(8,128)(2,1)}, bf16[64,1024]{1,0:T(8,128)(2,1)}, bf16[64,...) custom-call(s32[1,1]{1,0:T(1,128)} %bitcast.ours_ref, ...), custom_call_target="tpu_custom_call" | custom-call | flops 268435456 | bytes 1572864 | tf_op jit(solution)/shard_map/pick_rows/pallas_call | solution.py:416
  11.4 0.0 all-gather.2.cloned.1.call-update
  11.4 3.0 %collective-permute-start = (bf16[64,1024]{1,0:T(8,128)(2,1)}, bf16[64,1024]{1,0:T(8,128)(2,1)S(1)}, u32[]{:S(2)}, u32[]{:S(2)}) collective-permute-start(bf16[64,1024]{1,0:T(8,128)(2,1)} %get-tuple-element.42), channel_id=1, source_target_pairs={{0,4},{4,0},{8,12},{12,8},{16,20},{20,16},{24,28},{28,24},{1,5},{5... | collective-permute-start | bytes 393224 | tf_op jit(solution)/shard_map/ppermute | solution.py:547
  14.4 1.6 %collective-permute-start.1 = (bf16[64,1024]{1,0:T(8,128)(2,1)}, bf16[64,1024]{1,0:T(8,128)(2,1)S(1)}, u32[]{:S(2)}, u32[]{:S(2)}) collective-permute-start(bf16[64,1024]{1,0:T(8,128)(2,1)} %get-tuple-element.43), channel_id=1, source_target_pairs={{0,8},{4,12},{8,0},{12,4},{16,24},{20,28},{24,16},{28,20},{1,9},{5... | collective-permute-start | bytes 393224 | tf_op jit(solution)/shard_map/ppermute | solution.py:547
  16.0 3.0 %collective-permute-start.3 = (bf16[64,1024]{1,0:T(8,128)(2,1)}, bf16[64,1024]{1,0:T(8,128)(2,1)S(1)}, u32[]{:S(2)}, u32[]{:S(2)}) collective-permute-start(bf16[64,1024]{1,0:T(8,128)(2,1)} %get-tuple-element.45), channel_id=1, source_target_pairs={{0,16},{4,20},{8,24},{12,28},{16,0},{20,4},{24,8},{28,12},{1,17},{... | collective-permute-start | bytes 393224 | tf_op jit(solution)/shard_map/ppermute | solution.py:547
  19.0 1.3 %collective-permute-start.4 = (bf16[64,1024]{1,0:T(8,128)(2,1)}, bf16[64,1024]{1,0:T(8,128)(2,1)S(1)}, u32[]{:S(2)}, u32[]{:S(2)}) collective-permute-start(bf16[64,1024]{1,0:T(8,128)(2,1)} %get-tuple-element.46), channel_id=1, source_target_pairs={{0,20},{4,16},{8,28},{12,24},{16,4},{20,0},{24,12},{28,8},{1,21},{... | collective-permute-start | bytes 393224 | tf_op jit(solution)/shard_map/ppermute | solution.py:547
  20.3 0.7 broadcast_multiply_fusion
  21.0 0.1 broadcast_in_dim.31
  21.1 0.1 mul.12
  21.2 0.1 slice.98
  21.3 0.1 slice.97
  21.4 0.1 slice.92
  21.4 0.1 slice.93
  21.5 0.1 slice.91
  21.6 0.1 slice.90
  21.7 0.1 pad_add_fusion.2
  21.8 0.1 pad_add_fusion
  21.8 0.1 pad_add_fusion.3
  21.9 0.1 pad_add_fusion.5
  22.0 0.1 pad_add_fusion.1
  22.2 0.7 stack.31.pos_ref
  22.8 5.6 %prepare_transforms.1 = (bf16[256,4480]{1,0:T(8,128)(2,1)}, bf16[1408,768]{1,0:T(8,128)(2,1)}) custom-call(s32[8,896]{1,0:T(8,128)} %stack.31.pos_ref, bf16[256,256]{1,0:T(8,128)(2,1)} %constant.81.clone.hi_ref, bf16[256,256]{1,0:T(8,128)(2,1)} %constant.82.clone.lo_ref, bf16[256,768]{1,0:T(8,128)(2,1)} %constant.83.clone.back_ref), custom_call_target="tpu_custom_call" | custom-call | flops 3000000000 | bytes 8000000 | tf_op jit(solution)/shard_map/prepare_transforms/pallas_call | solution.py:471
  28.4 3.7 %collective-permute-start.5 = (bf16[64,1024]{1,0:T(8,128)(2,1)S(1)}, bf16[64,1024]{1,0:T(8,128)(2,1)S(1)}, u32[]{:S(2)}, u32[]{:S(2)}) collective-permute-start(bf16[64,1024]{1,0:T(8,128)(2,1)S(1)} %copy-done.13), channel_id=1, source_target_pairs={{0,24},{4,28},{8,16},{12,20},{16,8},{20,12},{24,0},{28,4},{1,25},{... | collective-permute-start | bytes 393224 | tf_op jit(solution)/shard_map/ppermute | solution.py:547
  32.1 0.0 collective-permute-done.1.refs_2_
  32.1 0.1 collective-permute-start.6
  32.2 0.1 broadcast_in_dim.30
  32.3 0.7 broadcast_in_dim_reshape.3.refs_8_
  33.1 0.0 collective-permute-done.2.refs_3_
  33.1 0.0 collective-permute-done.3.refs_4_
  33.1 4.1 %collective-permute-done.4.refs_5_ = bf16[64,1024]{1,0:T(8,128)(2,1)S(1)} collective-permute-done((bf16[64,1024]{1,0:T(8,128)(2,1)}, bf16[64,1024]{1,0:T(8,128)(2,1)S(1)}, u32[]{:S(2)}, u32[]{:S(2)}) %collective-permute-start.4) | collective-permute-done | bytes 131104 | tf_op jit(solution)/shard_map/ppermute | solution.py:547
  37.2 2.7 %collective-permute-done.6.refs_7_ = bf16[64,1024]{1,0:T(8,128)(2,1)S(1)} collective-permute-done((bf16[64,1024]{1,0:T(8,128)(2,1)S(1)}, bf16[64,1024]{1,0:T(8,128)(2,1)S(1)}, u32[]{:S(2)}, u32[]{:S(2)}) %collective-permute-start.6) | collective-permute-done | bytes 131104 | tf_op jit(solution)/shard_map/ppermute | solution.py:547
  40.0 0.6 copy-done.18
  40.6 19.5 %layer_step.1 = (f32[2,8,208,128]{3,2,1,0:T(8,128)}, f32[2,8,208,128]{3,2,1,0:T(8,128)}, f32[1,1]{1,0:T(1,128)}) custom-call(s32[1,1]{1,0:T(1,128)} %bitcast.1.core_ref, s32[1,1]{1,0:T(1,128)} %bitcast.2.side_ref, s32[1,1]{1,0:T(1,128)} %bitcast.ours_ref, bf16[64,1024]{1,0:T(8,128)(2,1)} %get-tuple-element.41.refs_0_, bf16[64,1024]{1,0:T(8,128)(2,1)} %copy-done.10, ...), custom_call_target="tpu_custom_call" | custom-call | flops 10000000000 | bytes 16000000 | tf_op jit(solution)/shard_map/layer_step/pallas_call | solution.py:514
  60.1 0.1 collective-permute-start.7
  60.2 3.8 %collective-permute-done.7 = f32[2,8,208,128]{3,2,1,0:T(8,128)S(1)} collective-permute-done((f32[2,8,208,128]{3,2,1,0:T(8,128)}, f32[2,8,208,128]{3,2,1,0:T(8,128)S(1)}, u32[]{:S(2)}, u32[]{:S(2)}) %collective-permute-start.7) | collective-permute-done | bytes 1703968 | tf_op jit(solution)/shard_map/ppermute | solution.py:571
  64.0 1.2 %fusion.8 = (bf16[4,208,128]{2,1,0:T(8,128)(2,1)S(1)}, bf16[4,208,128]{2,1,0:T(8,128)(2,1)S(1)}) fusion(f32[2,8,208,128]{3,2,1,0:T(8,128)S(1)} %collective-permute-done.7, f32[2,8,208,128]{3,2,1,0:T(8,128)} %get-tuple-element.54), kind=kLoop, calls=%fused_computation.12 | loop fusion | flops 425984 | bytes 2129920 | tf_op jit(solution)/shard_map/convert_element_type | solution.py:575
  65.2 1.6 %collective-permute-start.9 = (bf16[4,208,128]{2,1,0:T(8,128)(2,1)S(1)}, bf16[4,208,128]{2,1,0:T(8,128)(2,1)S(1)}, u32[]{:S(2)}, u32[]{:S(2)}) collective-permute-start(bf16[4,208,128]{2,1,0:T(8,128)(2,1)S(1)} %get-tuple-element.64), channel_id=1, source_target_pairs={{0,2},{1,3},{2,0},{3,1},{4,6},{5,7},{6,4},{7,5},{8,10},{9,11},{10,... | collective-permute-start | bytes 638984 | tf_op jit(solution)/shard_map/ppermute | solution.py:576
  66.8 0.5 collective-permute-start.8
  67.3 6.1 %collective-permute-done.9 = bf16[4,208,128]{2,1,0:T(8,128)(2,1)S(1)} collective-permute-done((bf16[4,208,128]{2,1,0:T(8,128)(2,1)S(1)}, bf16[4,208,128]{2,1,0:T(8,128)(2,1)S(1)}, u32[]{:S(2)}, u32[]{:S(2)}) %collective-permute-start.9) | collective-permute-done | bytes 213024 | tf_op jit(solution)/shard_map/ppermute | solution.py:576
  73.4 0.1 fusion.3
  73.5 3.7 %collective-permute-done.8 = bf16[4,208,128]{2,1,0:T(8,128)(2,1)S(1)} collective-permute-done((bf16[4,208,128]{2,1,0:T(8,128)(2,1)S(1)}, bf16[4,208,128]{2,1,0:T(8,128)(2,1)S(1)}, u32[]{:S(2)}, u32[]{:S(2)}) %collective-permute-start.8) | collective-permute-done | bytes 213024 | tf_op jit(solution)/shard_map/ppermute | solution.py:576
  77.1 0.1 fusion.21
  77.2 0.6 collective-permute-start.10
  77.9 4.6 %collective-permute-start.12 = (bf16[208,128]{1,0:T(8,128)(2,1)S(1)}, bf16[208,128]{1,0:T(8,128)(2,1)S(1)}, u32[]{:S(2)}, u32[]{:S(2)}) collective-permute-start(bf16[208,128]{1,0:T(8,128)(2,1)S(1)} %get-tuple-element.67), channel_id=1, source_target_pairs={{0,12},{4,8},{8,4},{12,0},{16,28},{20,24},{24,20},{28,16},{1,13},{... | collective-permute-start | bytes 159752 | tf_op jit(solution)/shard_map/ppermute | solution.py:547
  82.5 3.6 %collective-permute-start.13 = (bf16[208,128]{1,0:T(8,128)(2,1)S(1)}, bf16[208,128]{1,0:T(8,128)(2,1)S(1)}, u32[]{:S(2)}, u32[]{:S(2)}) collective-permute-start(bf16[208,128]{1,0:T(8,128)(2,1)S(1)} %get-tuple-element.69), channel_id=1, source_target_pairs={{0,16},{4,20},{8,24},{12,28},{16,0},{20,4},{24,8},{28,12},{1,17},{... | collective-permute-start | bytes 159752 | tf_op jit(solution)/shard_map/ppermute | solution.py:547
  86.2 0.6 collective-permute-start.16
  86.8 3.2 %collective-permute-start.15 = (bf16[208,128]{1,0:T(8,128)(2,1)S(1)}, bf16[208,128]{1,0:T(8,128)(2,1)S(1)}, u32[]{:S(2)}, u32[]{:S(2)}) collective-permute-start(bf16[208,128]{1,0:T(8,128)(2,1)S(1)} %get-tuple-element.71), channel_id=1, source_target_pairs={{0,24},{4,28},{8,16},{12,20},{16,8},{20,12},{24,0},{28,4},{1,25},{... | collective-permute-start | bytes 159752 | tf_op jit(solution)/shard_map/ppermute | solution.py:547
  90.0 3.1 %collective-permute-done.16 = bf16[208,128]{1,0:T(8,128)(2,1)S(1)} collective-permute-done((bf16[208,128]{1,0:T(8,128)(2,1)S(1)}, bf16[208,128]{1,0:T(8,128)(2,1)S(1)}, u32[]{:S(2)}, u32[]{:S(2)}) %collective-permute-start.16) | collective-permute-done | bytes 53280 | tf_op jit(solution)/shard_map/ppermute | solution.py:547
  93.1 3.3 %collective-permute-done.14 = bf16[208,128]{1,0:T(8,128)(2,1)S(1)} collective-permute-done((bf16[208,128]{1,0:T(8,128)(2,1)S(1)}, bf16[208,128]{1,0:T(8,128)(2,1)S(1)}, u32[]{:S(2)}, u32[]{:S(2)}) %collective-permute-start.14) | collective-permute-done | bytes 53280 | tf_op jit(solution)/shard_map/ppermute | solution.py:547
  96.4 0.1 fusion.16.refs_0_
  96.5 1.4 %collective-permute-start.22 = (bf16[208,128]{1,0:T(8,128)(2,1)S(1)}, bf16[208,128]{1,0:T(8,128)(2,1)S(1)}, u32[]{:S(2)}, u32[]{:S(2)}) collective-permute-start(bf16[208,128]{1,0:T(8,128)(2,1)S(1)} %fusion.16.refs_0_), channel_id=1, source_target_pairs={{0,24},{4,28},{8,16},{12,20},{16,8},{20,12},{24,0},{28,4},{1,25},{... | collective-permute-start | bytes 159752 | tf_op jit(solution)/shard_map/ppermute | solution.py:547
  97.9 3.1 %collective-permute-start.18 = (bf16[208,128]{1,0:T(8,128)(2,1)S(1)}, bf16[208,128]{1,0:T(8,128)(2,1)S(1)}, u32[]{:S(2)}, u32[]{:S(2)}) collective-permute-start(bf16[208,128]{1,0:T(8,128)(2,1)S(1)} %fusion.16.refs_0_), channel_id=1, source_target_pairs={{0,8},{4,12},{8,0},{12,4},{16,24},{20,28},{24,16},{28,20},{1,9},{5... | collective-permute-start | bytes 159752 | tf_op jit(solution)/shard_map/ppermute | solution.py:547
  100.9 1.1 collective-permute-start.17
  102.0 0.5 collective-permute-done.22.refs_6_
  102.5 1.1 collective-permute-start.23
  103.6 1.1 collective-permute-start.21
  104.7 0.9 collective-permute-start.19
  105.7 1.0 collective-permute-done.23.refs_7_
  106.6 1.1 collective-permute-done.21.refs_5_
  107.8 1.1 collective-permute-done.19.refs_3_
  108.9 0.6 copy-done.8
  109.5 2.0 %unpack_gradients.1 = (f32[512,384]{1,0:T(8,128)}, f32[31,384]{1,0:T(8,128)}, f32[384]{0:T(512)}) custom-call(s32[1,1]{1,0:T(1,128)} %bitcast.ours_ref, bf16[208,128]{1,0:T(8,128)(2,1)} %copy-done.1, bf16[208,128]{1,0:T(8,128)(2,1)} %copy-done.5, bf16[208,128]{1,0:T(8,128)(2,1)} %copy-done.4, bf16[208,128]{1,0:T(8,128)(2,1)} %copy-done.8, ...), custom_call_target="tpu_custom_call" | custom-call | flops 1000000 | bytes 1200000 | tf_op jit(solution)/shard_map/unpack_gradients/pallas_call | solution.py:431
  (72 shorter events, 0.2 us)
Async XLA Ops:
  7.2 32.8 %all-gather.2.cloned.1.call-start = ((), (), s32[]{:S(2)}) async-start(), calls=%async_computation | async-start | bytes 2088960 | tf_op jit(solution)/shard_map/all_gather | solution.py:541
  11.4 17.0 %collective-permute-start = (bf16[64,1024]{1,0:T(8,128)(2,1)}, bf16[64,1024]{1,0:T(8,128)(2,1)S(1)}, u32[]{:S(2)}, u32[]{:S(2)}) collective-permute-start(bf16[64,1024]{1,0:T(8,128)(2,1)} %get-tuple-element.42), channel_id=1, source_target_pairs={{0,4},{4,0},{8,12},{12,8},{16,20},{20,16},{24,28},{28,24},{1,5},{5... | collective-permute-start | bytes 393224 | tf_op jit(solution)/shard_map/ppermute | solution.py:547
  14.4 17.7 %collective-permute-start.1 = (bf16[64,1024]{1,0:T(8,128)(2,1)}, bf16[64,1024]{1,0:T(8,128)(2,1)S(1)}, u32[]{:S(2)}, u32[]{:S(2)}) collective-permute-start(bf16[64,1024]{1,0:T(8,128)(2,1)} %get-tuple-element.43), channel_id=1, source_target_pairs={{0,8},{4,12},{8,0},{12,4},{16,24},{20,28},{24,16},{28,20},{1,9},{5... | collective-permute-start | bytes 393224 | tf_op jit(solution)/shard_map/ppermute | solution.py:547
  16.0 17.1 %collective-permute-start.2 = (bf16[64,1024]{1,0:T(8,128)(2,1)}, bf16[64,1024]{1,0:T(8,128)(2,1)S(1)}, u32[]{:S(2)}, u32[]{:S(2)}) collective-permute-start(bf16[64,1024]{1,0:T(8,128)(2,1)} %get-tuple-element.44), channel_id=1, source_target_pairs={{0,12},{4,8},{8,4},{12,0},{16,28},{20,24},{24,20},{28,16},{1,13},{... | collective-permute-start | bytes 393224 | tf_op jit(solution)/shard_map/ppermute | solution.py:547
  16.0 17.1 %collective-permute-start.3 = (bf16[64,1024]{1,0:T(8,128)(2,1)}, bf16[64,1024]{1,0:T(8,128)(2,1)S(1)}, u32[]{:S(2)}, u32[]{:S(2)}) collective-permute-start(bf16[64,1024]{1,0:T(8,128)(2,1)} %get-tuple-element.45), channel_id=1, source_target_pairs={{0,16},{4,20},{8,24},{12,28},{16,0},{20,4},{24,8},{28,12},{1,17},{... | collective-permute-start | bytes 393224 | tf_op jit(solution)/shard_map/ppermute | solution.py:547
  19.0 18.2 %collective-permute-start.4 = (bf16[64,1024]{1,0:T(8,128)(2,1)}, bf16[64,1024]{1,0:T(8,128)(2,1)S(1)}, u32[]{:S(2)}, u32[]{:S(2)}) collective-permute-start(bf16[64,1024]{1,0:T(8,128)(2,1)} %get-tuple-element.46), channel_id=1, source_target_pairs={{0,20},{4,16},{8,28},{12,24},{16,4},{20,0},{24,12},{28,8},{1,21},{... | collective-permute-start | bytes 393224 | tf_op jit(solution)/shard_map/ppermute | solution.py:547
  22.8 5.6 %copy-start.13 = (bf16[64,1024]{1,0:T(8,128)(2,1)S(1)}, bf16[64,1024]{1,0:T(8,128)(2,1)}, u32[]{:S(2)}) copy-start(bf16[64,1024]{1,0:T(8,128)(2,1)} %get-tuple-element.47) | copy-start | bytes 393220
  22.8 9.3 %copy-start.11 = (bf16[64,1024]{1,0:T(8,128)(2,1)S(1)}, bf16[64,1024]{1,0:T(8,128)(2,1)}, u32[]{:S(2)}) copy-start(bf16[64,1024]{1,0:T(8,128)(2,1)} %get-tuple-element.48) | copy-start | bytes 393220
  22.8 9.4 %copy-start.9 = (s32[1,1,256]{2,1,0:T(1,128)S(1)}, s32[1,1,256]{2,1,0:T(1,128)}, u32[]{:S(2)}) copy-start(s32[1,1,256]{2,1,0:T(1,128)} %param.15) | copy-start | bytes 3076
  28.4 11.5 %copy-start.10 = (bf16[64,1024]{1,0:T(8,128)(2,1)}, bf16[64,1024]{1,0:T(8,128)(2,1)S(1)}, u32[]{:S(2)}) copy-start(bf16[64,1024]{1,0:T(8,128)(2,1)S(1)} %collective-permute-done.refs_1_) | copy-start | bytes 393220
  28.4 8.8 %collective-permute-start.5 = (bf16[64,1024]{1,0:T(8,128)(2,1)S(1)}, bf16[64,1024]{1,0:T(8,128)(2,1)S(1)}, u32[]{:S(2)}, u32[]{:S(2)}) collective-permute-start(bf16[64,1024]{1,0:T(8,128)(2,1)S(1)} %copy-done.13), channel_id=1, source_target_pairs={{0,24},{4,28},{8,16},{12,20},{16,8},{20,12},{24,0},{28,4},{1,25},{... | collective-permute-start | bytes 393224 | tf_op jit(solution)/shard_map/ppermute | solution.py:547
  32.1 7.8 %copy-start.12 = (bf16[64,1024]{1,0:T(8,128)(2,1)}, bf16[64,1024]{1,0:T(8,128)(2,1)S(1)}, u32[]{:S(2)}) copy-start(bf16[64,1024]{1,0:T(8,128)(2,1)S(1)} %collective-permute-done.1.refs_2_) | copy-start | bytes 393220
  32.1 7.8 %collective-permute-start.6 = (bf16[64,1024]{1,0:T(8,128)(2,1)S(1)}, bf16[64,1024]{1,0:T(8,128)(2,1)S(1)}, u32[]{:S(2)}, u32[]{:S(2)}) collective-permute-start(bf16[64,1024]{1,0:T(8,128)(2,1)S(1)} %copy-done.11), channel_id=1, source_target_pairs={{0,28},{4,24},{8,20},{12,16},{16,12},{20,8},{24,4},{28,0},{1,29},{... | collective-permute-start | bytes 393224 | tf_op jit(solution)/shard_map/ppermute | solution.py:547
  33.1 6.9 %copy-start.14 = (bf16[64,1024]{1,0:T(8,128)(2,1)}, bf16[64,1024]{1,0:T(8,128)(2,1)S(1)}, u32[]{:S(2)}) copy-start(bf16[64,1024]{1,0:T(8,128)(2,1)S(1)} %collective-permute-done.2.refs_3_) | copy-start | bytes 393220
  33.1 6.9 %copy-start.15 = (bf16[64,1024]{1,0:T(8,128)(2,1)}, bf16[64,1024]{1,0:T(8,128)(2,1)S(1)}, u32[]{:S(2)}) copy-start(bf16[64,1024]{1,0:T(8,128)(2,1)S(1)} %collective-permute-done.3.refs_4_) | copy-start | bytes 393220
  37.2 2.8 %copy-start.16 = (bf16[64,1024]{1,0:T(8,128)(2,1)}, bf16[64,1024]{1,0:T(8,128)(2,1)S(1)}, u32[]{:S(2)}) copy-start(bf16[64,1024]{1,0:T(8,128)(2,1)S(1)} %collective-permute-done.4.refs_5_) | copy-start | bytes 393220
  37.2 2.8 %copy-start.17 = (bf16[64,1024]{1,0:T(8,128)(2,1)}, bf16[64,1024]{1,0:T(8,128)(2,1)S(1)}, u32[]{:S(2)}) copy-start(bf16[64,1024]{1,0:T(8,128)(2,1)S(1)} %collective-permute-done.5.refs_6_) | copy-start | bytes 393220
  39.9 0.7 copy-start.18
  60.1 13.3 %copy-start = (f32[2,8,208,128]{3,2,1,0:T(8,128)S(1)}, f32[2,8,208,128]{3,2,1,0:T(8,128)}, u32[]{:S(2)}) copy-start(f32[2,8,208,128]{3,2,1,0:T(8,128)} %get-tuple-element.54) | copy-start | bytes 5111812
  60.1 3.9 %collective-permute-start.7 = (f32[2,8,208,128]{3,2,1,0:T(8,128)}, f32[2,8,208,128]{3,2,1,0:T(8,128)S(1)}, u32[]{:S(2)}, u32[]{:S(2)}) collective-permute-start(f32[2,8,208,128]{3,2,1,0:T(8,128)} %get-tuple-element.55), channel_id=1, source_target_pairs={{0,1},{1,0},{2,3},{3,2},{4,5},{5,4},{6,7},{7,6},{8,9},{9,8},{10,11... | collective-permute-start | bytes 5111816 | tf_op jit(solution)/shard_map/ppermute | solution.py:571
  65.2 8.2 %collective-permute-start.9 = (bf16[4,208,128]{2,1,0:T(8,128)(2,1)S(1)}, bf16[4,208,128]{2,1,0:T(8,128)(2,1)S(1)}, u32[]{:S(2)}, u32[]{:S(2)}) collective-permute-start(bf16[4,208,128]{2,1,0:T(8,128)(2,1)S(1)} %get-tuple-element.64), channel_id=1, source_target_pairs={{0,2},{1,3},{2,0},{3,1},{4,6},{5,7},{6,4},{7,5},{8,10},{9,11},{10,... | collective-permute-start | bytes 638984 | tf_op jit(solution)/shard_map/ppermute | solution.py:576
  66.8 10.3 %collective-permute-start.8 = (bf16[4,208,128]{2,1,0:T(8,128)(2,1)S(1)}, bf16[4,208,128]{2,1,0:T(8,128)(2,1)S(1)}, u32[]{:S(2)}, u32[]{:S(2)}) collective-permute-start(bf16[4,208,128]{2,1,0:T(8,128)(2,1)S(1)} %get-tuple-element.65), channel_id=1, source_target_pairs={{0,2},{1,3},{2,0},{3,1},{4,6},{5,7},{6,4},{7,5},{8,10},{9,11},{10,... | collective-permute-start | bytes 638984 | tf_op jit(solution)/shard_map/ppermute | solution.py:576
  77.2 9.6 %collective-permute-start.10 = (bf16[208,128]{1,0:T(8,128)(2,1)S(1)}, bf16[208,128]{1,0:T(8,128)(2,1)S(1)}, u32[]{:S(2)}, u32[]{:S(2)}) collective-permute-start(bf16[208,128]{1,0:T(8,128)(2,1)S(1)} %get-tuple-element.66), channel_id=1, source_target_pairs={{0,4},{4,0},{8,12},{12,8},{16,20},{20,16},{24,28},{28,24},{1,5},{5... | collective-permute-start | bytes 159752 | tf_op jit(solution)/shard_map/ppermute | solution.py:547
  77.9 12.1 %collective-permute-start.12 = (bf16[208,128]{1,0:T(8,128)(2,1)S(1)}, bf16[208,128]{1,0:T(8,128)(2,1)S(1)}, u32[]{:S(2)}, u32[]{:S(2)}) collective-permute-start(bf16[208,128]{1,0:T(8,128)(2,1)S(1)} %get-tuple-element.67), channel_id=1, source_target_pairs={{0,12},{4,8},{8,4},{12,0},{16,28},{20,24},{24,20},{28,16},{1,13},{... | collective-permute-start | bytes 159752 | tf_op jit(solution)/shard_map/ppermute | solution.py:547
  82.5 7.5 %collective-permute-start.11 = (bf16[208,128]{1,0:T(8,128)(2,1)S(1)}, bf16[208,128]{1,0:T(8,128)(2,1)S(1)}, u32[]{:S(2)}, u32[]{:S(2)}) collective-permute-start(bf16[208,128]{1,0:T(8,128)(2,1)S(1)} %get-tuple-element.68), channel_id=1, source_target_pairs={{0,8},{4,12},{8,0},{12,4},{16,24},{20,28},{24,16},{28,20},{1,9},{5... | collective-permute-start | bytes 159752 | tf_op jit(solution)/shard_map/ppermute | solution.py:547
  82.5 7.5 %collective-permute-start.13 = (bf16[208,128]{1,0:T(8,128)(2,1)S(1)}, bf16[208,128]{1,0:T(8,128)(2,1)S(1)}, u32[]{:S(2)}, u32[]{:S(2)}) collective-permute-start(bf16[208,128]{1,0:T(8,128)(2,1)S(1)} %get-tuple-element.69), channel_id=1, source_target_pairs={{0,16},{4,20},{8,24},{12,28},{16,0},{20,4},{24,8},{28,12},{1,17},{... | collective-permute-start | bytes 159752 | tf_op jit(solution)/shard_map/ppermute | solution.py:547
  86.2 6.9 %collective-permute-start.16 = (bf16[208,128]{1,0:T(8,128)(2,1)S(1)}, bf16[208,128]{1,0:T(8,128)(2,1)S(1)}, u32[]{:S(2)}, u32[]{:S(2)}) collective-permute-start(bf16[208,128]{1,0:T(8,128)(2,1)S(1)} %get-tuple-element.70), channel_id=1, source_target_pairs={{0,28},{4,24},{8,20},{12,16},{16,12},{20,8},{24,4},{28,0},{1,29},{... | collective-permute-start | bytes 159752 | tf_op jit(solution)/shard_map/ppermute | solution.py:547
  86.8 6.3 %collective-permute-start.15 = (bf16[208,128]{1,0:T(8,128)(2,1)S(1)}, bf16[208,128]{1,0:T(8,128)(2,1)S(1)}, u32[]{:S(2)}, u32[]{:S(2)}) collective-permute-start(bf16[208,128]{1,0:T(8,128)(2,1)S(1)} %get-tuple-element.71), channel_id=1, source_target_pairs={{0,24},{4,28},{8,16},{12,20},{16,8},{20,12},{24,0},{28,4},{1,25},{... | collective-permute-start | bytes 159752 | tf_op jit(solution)/shard_map/ppermute | solution.py:547
  90.0 6.4 %collective-permute-start.14 = (bf16[208,128]{1,0:T(8,128)(2,1)S(1)}, bf16[208,128]{1,0:T(8,128)(2,1)S(1)}, u32[]{:S(2)}, u32[]{:S(2)}) collective-permute-start(bf16[208,128]{1,0:T(8,128)(2,1)S(1)} %get-tuple-element.72), channel_id=1, source_target_pairs={{0,20},{4,16},{8,28},{12,24},{16,4},{20,0},{24,12},{28,8},{1,21},{... | collective-permute-start | bytes 159752 | tf_op jit(solution)/shard_map/ppermute | solution.py:547
  96.5 12.4 %copy-start.1 = (bf16[208,128]{1,0:T(8,128)(2,1)}, bf16[208,128]{1,0:T(8,128)(2,1)S(1)}, u32[]{:S(2)}) copy-start(bf16[208,128]{1,0:T(8,128)(2,1)S(1)} %fusion.16.refs_0_) | copy-start | bytes 159748
  96.5 6.0 %collective-permute-start.22 = (bf16[208,128]{1,0:T(8,128)(2,1)S(1)}, bf16[208,128]{1,0:T(8,128)(2,1)S(1)}, u32[]{:S(2)}, u32[]{:S(2)}) collective-permute-start(bf16[208,128]{1,0:T(8,128)(2,1)S(1)} %fusion.16.refs_0_), channel_id=1, source_target_pairs={{0,24},{4,28},{8,16},{12,20},{16,8},{20,12},{24,0},{28,4},{1,25},{... | collective-permute-start | bytes 159752 | tf_op jit(solution)/shard_map/ppermute | solution.py:547
  97.8 5.8 %collective-permute-start.20 = (bf16[208,128]{1,0:T(8,128)(2,1)S(1)}, bf16[208,128]{1,0:T(8,128)(2,1)S(1)}, u32[]{:S(2)}, u32[]{:S(2)}) collective-permute-start(bf16[208,128]{1,0:T(8,128)(2,1)S(1)} %fusion.16.refs_0_), channel_id=1, source_target_pairs={{0,16},{4,20},{8,24},{12,28},{16,0},{20,4},{24,8},{28,12},{1,17},{... | collective-permute-start | bytes 159752 | tf_op jit(solution)/shard_map/ppermute | solution.py:547
  97.9 6.9 %collective-permute-start.18 = (bf16[208,128]{1,0:T(8,128)(2,1)S(1)}, bf16[208,128]{1,0:T(8,128)(2,1)S(1)}, u32[]{:S(2)}, u32[]{:S(2)}) collective-permute-start(bf16[208,128]{1,0:T(8,128)(2,1)S(1)} %fusion.16.refs_0_), channel_id=1, source_target_pairs={{0,8},{4,12},{8,0},{12,4},{16,24},{20,28},{24,16},{28,20},{1,9},{5... | collective-permute-start | bytes 159752 | tf_op jit(solution)/shard_map/ppermute | solution.py:547
  100.9 4.7 %collective-permute-start.17 = (bf16[208,128]{1,0:T(8,128)(2,1)S(1)}, bf16[208,128]{1,0:T(8,128)(2,1)S(1)}, u32[]{:S(2)}, u32[]{:S(2)}) collective-permute-start(bf16[208,128]{1,0:T(8,128)(2,1)S(1)} %fusion.16.refs_0_), channel_id=1, source_target_pairs={{0,4},{4,0},{8,12},{12,8},{16,20},{20,16},{24,28},{28,24},{1,5},{5... | collective-permute-start | bytes 159752 | tf_op jit(solution)/shard_map/ppermute | solution.py:547
  102.5 6.4 %copy-start.2 = (bf16[208,128]{1,0:T(8,128)(2,1)}, bf16[208,128]{1,0:T(8,128)(2,1)S(1)}, u32[]{:S(2)}) copy-start(bf16[208,128]{1,0:T(8,128)(2,1)S(1)} %collective-permute-done.22.refs_6_) | copy-start | bytes 159748
  102.5 4.1 %collective-permute-start.23 = (bf16[208,128]{1,0:T(8,128)(2,1)S(1)}, bf16[208,128]{1,0:T(8,128)(2,1)S(1)}, u32[]{:S(2)}, u32[]{:S(2)}) collective-permute-start(bf16[208,128]{1,0:T(8,128)(2,1)S(1)} %collective-permute-done.22.refs_6_), channel_id=1, source_target_pairs={{0,4},{4,0},{8,12},{12,8},{16,20},{20,16},{24,28},{28,24},{1,5},{5... | collective-permute-start | bytes 159752 | tf_op jit(solution)/shard_map/ppermute | solution.py:547
  103.6 5.2 %copy-start.3 = (bf16[208,128]{1,0:T(8,128)(2,1)}, bf16[208,128]{1,0:T(8,128)(2,1)S(1)}, u32[]{:S(2)}) copy-start(bf16[208,128]{1,0:T(8,128)(2,1)S(1)} %collective-permute-done.20.refs_4_) | copy-start | bytes 159748
  103.6 4.1 %collective-permute-start.21 = (bf16[208,128]{1,0:T(8,128)(2,1)S(1)}, bf16[208,128]{1,0:T(8,128)(2,1)S(1)}, u32[]{:S(2)}, u32[]{:S(2)}) collective-permute-start(bf16[208,128]{1,0:T(8,128)(2,1)S(1)} %collective-permute-done.20.refs_4_), channel_id=1, source_target_pairs={{0,4},{4,0},{8,12},{12,8},{16,20},{20,16},{24,28},{28,24},{1,5},{5... | collective-permute-start | bytes 159752 | tf_op jit(solution)/shard_map/ppermute | solution.py:547
  104.7 4.2 %copy-start.4 = (bf16[208,128]{1,0:T(8,128)(2,1)}, bf16[208,128]{1,0:T(8,128)(2,1)S(1)}, u32[]{:S(2)}) copy-start(bf16[208,128]{1,0:T(8,128)(2,1)S(1)} %collective-permute-done.18.refs_2_) | copy-start | bytes 159748
  104.7 4.1 %collective-permute-start.19 = (bf16[208,128]{1,0:T(8,128)(2,1)S(1)}, bf16[208,128]{1,0:T(8,128)(2,1)S(1)}, u32[]{:S(2)}, u32[]{:S(2)}) collective-permute-start(bf16[208,128]{1,0:T(8,128)(2,1)S(1)} %collective-permute-done.18.refs_2_), channel_id=1, source_target_pairs={{0,4},{4,0},{8,12},{12,8},{16,20},{20,16},{24,28},{28,24},{1,5},{5... | collective-permute-start | bytes 159752 | tf_op jit(solution)/shard_map/ppermute | solution.py:547
  105.7 3.2 %copy-start.5 = (bf16[208,128]{1,0:T(8,128)(2,1)}, bf16[208,128]{1,0:T(8,128)(2,1)S(1)}, u32[]{:S(2)}) copy-start(bf16[208,128]{1,0:T(8,128)(2,1)S(1)} %collective-permute-done.17.refs_1_) | copy-start | bytes 159748
  106.6 2.3 %copy-start.6 = (bf16[208,128]{1,0:T(8,128)(2,1)}, bf16[208,128]{1,0:T(8,128)(2,1)S(1)}, u32[]{:S(2)}) copy-start(bf16[208,128]{1,0:T(8,128)(2,1)S(1)} %collective-permute-done.23.refs_7_) | copy-start | bytes 159748
  107.8 1.1 copy-start.7
  108.9 0.6 copy-start.8
Sparse Core Ops, SparseCore 0:
  11.5 22.8 all-gather.1

commit v4 on v3

--- a/solution.py
+++ b/solution.py
@@ -77,7 +77,7 @@
     depth, tap_count = proj_ref.shape[0], taps_ref.shape[0]
     packed_ref[:depth] = proj_ref[...]
     tail_ref[:tap_count] = taps_ref[...].astype(F32)
-    tail_ref[tap_count:] = gain_ref[...].astype(F32)
+    tail_ref[tap_count:] = gain_ref[...].astype(F32)[None, :]
     packed_ref[depth:] = tail_ref[...].astype(BF16)
     count = rows_ref.shape[0]
     rows = rows_ref[...]
@@ -232,7 +232,7 @@
         hi_b, lo_b, ghi_b, glo_b = hi_ref.at[b], lo_ref.at[b], ghi_ref.at[b], glo_ref.at[b]
         spec_b, nspec_b, phi_b, plo_b = spec_ref.at[b], nspec_ref.at[b], phi_ref.at[b], plo_ref.at[b]
         coef_b, c_b = coef_ref.at[b], c_ref.at[b]
-        cols = pl.ds(pl.multiple_of(i * CH, CH), CH)
+        cols = slice(i * CH, (i + 1) * CH)
         gain = params_ref[depth + 16 : depth + 32, cols][15:16].astype(F32)
         taps = params_ref[depth : depth + 32, cols]
         coef_b[...] = dot(tapf_ref[...], jnp.concatenate([taps, taps], axis=0))
@@ -339,17 +339,18 @@
                 yield
         last = lax.broadcasted_iota(jnp.int32, (32, CH), 0) == 31
         small_ref[:, cols] = jnp.where(last, gain_grad, tap_grad)
-
-    def middle(i, carry):
-        lead, follow = chunk(2 * i, 0), chunk(2 * i + 1, 1)
-        for _ in range(3):
-            next(lead)
-        running = [lead, follow]
-        while running:
-            running = [g for g in running if next(g, running) is not running]
-        return carry
-
-    lax.fori_loop(0, chunks // 2, middle, 0)
+        for _ in range(4):
+            yield
+
+    waiting = [chunk(i, i % 2) for i in range(chunks)]
+    running = [waiting.pop(0)]
+    for _ in range(15):
+        next(running[0])
+    while running:
+        if waiting and len(running) < 2:
+            running.append(waiting.pop(0))
+        running = [g for g in running if next(g, waiting) is not waiting]
+
     loss_ref[...] = jnp.sum(lossacc_ref[...], axis=1, keepdims=True)
     for rows in tiles:
         m1 = jnp.sum(acc_ref[rows], axis=1, keepdims=True) * (1.0 / width)
@@ -537,7 +538,7 @@
     ours = lax.axis_index("dp") if few else jnp.zeros((), jnp.int32)
     ids = [v.astype(jnp.int32).reshape(1, 1) for v in (place % 2, place // 2, ours)]
     wanted = send_rows[0, 0]
-    packed, *outgoing = pick(ids[2], wanted, cached[0, 0], in_proj, conv_kernel, norm_gain[None, :])
+    packed, *outgoing = pick(ids[2], wanted, cached[0, 0], in_proj, conv_kernel, norm_gain)
     params = lax.all_gather(packed, "fsdp", axis=1, tiled=True)
     outgoing, take_own, utt_own = lax.optimization_barrier(
         (outgoing, take_rows[0, 0], utt_index[0, 0])
@@ -576,7 +577,7 @@
     far_in, near_in = [lax.ppermute(v, "fsdp", across) for v in sent]
     far_sum = keep[0, half:] + other[0, half:] + far_in.astype(F32)
     far_out = far_sum.astype(BF16)
-    near_in, far_out = lax.optimization_barrier((near_in, far_out))
+    near_in, _ = lax.optimization_barrier((near_in, far_out))
     near_sum = keep[0, :half] + other[0, :half] + near_in.astype(F32)
     near_out = near_sum.astype(BF16)
     if few:

time: 119 us -> 113 us (0.950)
  waiting for transfers between devices: 30.5 us -> 26.5 us
  local copies, waits for them, and re-layouts: 4.77 us -> 3.55 us
    ppermute x2, waiting for transfers between devices: 9.75 us -> 6.07 us  [per_device(): far_in, near_in = [lax.ppermute(v, 'fsdp', across) for v in sent]]
    broadcast_in_dim x1 -> x0, local copies, waits for them, and re-layouts: 1.24 us -> none  [per_device(): norm_gain[None, :]]
where the time goes in v4:
time: 113 us
  starting transfers between devices  35.2 us (31%)
  Pallas kernels  30.7 us (27%)
  waiting for transfers between devices  26.5 us (23%)
  between operations  14.3 us (13%)
  local copies, waits for them, and re-layouts  3.55 us (3%)
  other arithmetic  2.51 us (2%)
    ppermute x21, starting transfers between devices, swap(): return lax.ppermute(value, 'dp', [(i, i ^ k) for i in range(dp)])  33 us
    pallas_call x1, Pallas kernels, layer(): pl.pallas_call(functools.partial(layer_kernel, len(arrived)), out_shape=[...  20.2 us
    ppermute x21, waiting for transfers between devices, swap(): return lax.ppermute(value, 'dp', [(i, i ^ k) for i in range(dp)])  16.6 us
    ppermute x2, waiting for transfers between devices, per_device(): far_in, near_in = [lax.ppermute(v, 'fsdp', across) for v in sent]  6.07 us
    pallas_call x1, Pallas kernels, prepare(): pl.pallas_call(prep_kernel, out_shape=shapes, in_specs=vmem(4), out_specs...  5.59 us
    ppermute x1, waiting for transfers between devices, per_device(): other = lax.ppermute(send, 'fsdp', [(i, i ^ 1) for i in range(fsdp)])  3.8 us
    pallas_call x1, Pallas kernels, pick(): pl.pallas_call(pick_kernel, out_shape=[jax.ShapeDtypeStruct((proj.shape[0...  2.94 us
  transfers between devices with their start and end apart: 25, of which 11 were waited for; matrix products, arithmetic and copies ran while one was open for 3% of the time, Pallas kernels for 5%

profile of v4, /device:TPU:0, one launch (start us, length us, event | category | flops | bytes accessed | tf_op | source)
XLA Modules:
  0.0 112.7 jit_solution(4497887575716843883)
XLA Ops:
  7.2 0.0 all-gather.2.cloned.1.call-start
  7.2 2.9 %pick_rows.1 = (bf16[544,384]{1,0:T(8,128)(2,1)}, bf16[64,1024]{1,0:T(8,128)(2,1)}, bf16[64,1024]{1,0:T(8,128)(2,1)}, bf16[64,1024]{1,0:T(8,128)(2,1)}, bf16[64,...) custom-call(s32[1,1]{1,0:T(1,128)} %bitcast.ours_ref, ...), custom_call_target="tpu_custom_call" | custom-call | flops 268435456 | bytes 1572864 | tf_op jit(solution)/shard_map/pick_rows/pallas_call | solution.py:417
  10.2 0.0 all-gather.2.cloned.1.call-update
  10.2 3.0 %collective-permute-start = (bf16[64,1024]{1,0:T(8,128)(2,1)}, bf16[64,1024]{1,0:T(8,128)(2,1)S(1)}, u32[]{:S(2)}, u32[]{:S(2)}) collective-permute-start(bf16[64,1024]{1,0:T(8,128)(2,1)} %get-tuple-element.41), channel_id=1, source_target_pairs={{0,4},{4,0},{8,12},{12,8},{16,20},{20,16},{24,28},{28,24},{1,5},{5... | collective-permute-start | bytes 393224 | tf_op jit(solution)/shard_map/ppermute | solution.py:548
  13.2 1.6 %collective-permute-start.1 = (bf16[64,1024]{1,0:T(8,128)(2,1)}, bf16[64,1024]{1,0:T(8,128)(2,1)S(1)}, u32[]{:S(2)}, u32[]{:S(2)}) collective-permute-start(bf16[64,1024]{1,0:T(8,128)(2,1)} %get-tuple-element.42), channel_id=1, source_target_pairs={{0,8},{4,12},{8,0},{12,4},{16,24},{20,28},{24,16},{28,20},{1,9},{5... | collective-permute-start | bytes 393224 | tf_op jit(solution)/shard_map/ppermute | solution.py:548
  14.8 0.0 collective-permute-start.2
  14.8 3.0 %collective-permute-start.3 = (bf16[64,1024]{1,0:T(8,128)(2,1)}, bf16[64,1024]{1,0:T(8,128)(2,1)S(1)}, u32[]{:S(2)}, u32[]{:S(2)}) collective-permute-start(bf16[64,1024]{1,0:T(8,128)(2,1)} %get-tuple-element.44), channel_id=1, source_target_pairs={{0,16},{4,20},{8,24},{12,28},{16,0},{20,4},{24,8},{28,12},{1,17},{... | collective-permute-start | bytes 393224 | tf_op jit(solution)/shard_map/ppermute | solution.py:548
  17.8 1.3 %collective-permute-start.4 = (bf16[64,1024]{1,0:T(8,128)(2,1)}, bf16[64,1024]{1,0:T(8,128)(2,1)S(1)}, u32[]{:S(2)}, u32[]{:S(2)}) collective-permute-start(bf16[64,1024]{1,0:T(8,128)(2,1)} %get-tuple-element.45), channel_id=1, source_target_pairs={{0,20},{4,16},{8,28},{12,24},{16,4},{20,0},{24,12},{28,8},{1,21},{... | collective-permute-start | bytes 393224 | tf_op jit(solution)/shard_map/ppermute | solution.py:548
  19.0 0.7 broadcast_multiply_fusion
  19.7 0.1 broadcast_in_dim.27
  19.8 0.1 mul.12
  20.0 0.1 slice.98
  20.1 0.1 slice.97
  20.1 0.1 slice.92
  20.2 0.1 slice.93
  20.3 0.1 slice.91
  20.3 0.1 slice.90
  20.4 0.1 pad_add_fusion.2
  20.5 0.1 pad_add_fusion
  20.6 0.1 pad_add_fusion.3
  20.7 0.1 pad_add_fusion.5
  20.8 0.1 pad_add_fusion.1
  20.9 0.7 stack.31.pos_ref
  21.6 5.6 %prepare_transforms.1 = (bf16[256,4480]{1,0:T(8,128)(2,1)}, bf16[1408,768]{1,0:T(8,128)(2,1)}) custom-call(s32[8,896]{1,0:T(8,128)} %stack.31.pos_ref, bf16[256,256]{1,0:T(8,128)(2,1)} %constant.81.clone.hi_ref, bf16[256,256]{1,0:T(8,128)(2,1)} %constant.82.clone.lo_ref, bf16[256,768]{1,0:T(8,128)(2,1)} %constant.83.clone.back_ref), custom_call_target="tpu_custom_call" | custom-call | flops 3000000000 | bytes 8000000 | tf_op jit(solution)/shard_map/prepare_transforms/pallas_call | solution.py:472
  27.2 0.0 collective-permute-done.refs_1_
  27.2 3.7 %collective-permute-start.5 = (bf16[64,1024]{1,0:T(8,128)(2,1)S(1)}, bf16[64,1024]{1,0:T(8,128)(2,1)S(1)}, u32[]{:S(2)}, u32[]{:S(2)}) collective-permute-start(bf16[64,1024]{1,0:T(8,128)(2,1)S(1)} %copy-done.13), channel_id=1, source_target_pairs={{0,24},{4,28},{8,16},{12,20},{16,8},{20,12},{24,0},{28,4},{1,25},{... | collective-permute-start | bytes 393224 | tf_op jit(solution)/shard_map/ppermute | solution.py:548
  30.9 0.0 collective-permute-done.1.refs_2_
  30.9 0.1 collective-permute-start.6
  31.0 0.1 broadcast_in_dim.26
  31.1 0.7 broadcast_in_dim_reshape.3.refs_8_
  31.8 4.1 %collective-permute-done.4.refs_5_ = bf16[64,1024]{1,0:T(8,128)(2,1)S(1)} collective-permute-done((bf16[64,1024]{1,0:T(8,128)(2,1)}, bf16[64,1024]{1,0:T(8,128)(2,1)S(1)}, u32[]{:S(2)}, u32[]{:S(2)}) %collective-permute-start.4) | collective-permute-done | bytes 131104 | tf_op jit(solution)/shard_map/ppermute | solution.py:548
  36.0 2.7 %collective-permute-done.6.refs_7_ = bf16[64,1024]{1,0:T(8,128)(2,1)S(1)} collective-permute-done((bf16[64,1024]{1,0:T(8,128)(2,1)S(1)}, bf16[64,1024]{1,0:T(8,128)(2,1)S(1)}, u32[]{:S(2)}, u32[]{:S(2)}) %collective-permute-start.6) | collective-permute-done | bytes 131104 | tf_op jit(solution)/shard_map/ppermute | solution.py:548
  38.7 0.6 copy-done.18
  39.3 20.2 %layer_step.1 = (f32[2,8,208,128]{3,2,1,0:T(8,128)}, f32[2,8,208,128]{3,2,1,0:T(8,128)}, f32[1,1]{1,0:T(1,128)}) custom-call(s32[1,1]{1,0:T(1,128)} %bitcast.1.core_ref, s32[1,1]{1,0:T(1,128)} %bitcast.2.side_ref, s32[1,1]{1,0:T(1,128)} %bitcast.ours_ref, bf16[64,1024]{1,0:T(8,128)(2,1)} %get-tuple-element.40.refs_0_, bf16[64,1024]{1,0:T(8,128)(2,1)} %copy-done.10, ...), custom_call_target="tpu_custom_call" | custom-call | flops 10000000000 | bytes 16000000 | tf_op jit(solution)/shard_map/layer_step/pallas_call | solution.py:515
  59.6 0.1 collective-permute-start.7
  59.6 3.8 %collective-permute-done.7 = f32[2,8,208,128]{3,2,1,0:T(8,128)S(1)} collective-permute-done((f32[2,8,208,128]{3,2,1,0:T(8,128)}, f32[2,8,208,128]{3,2,1,0:T(8,128)S(1)}, u32[]{:S(2)}, u32[]{:S(2)}) %collective-permute-start.7) | collective-permute-done | bytes 1703968 | tf_op jit(solution)/shard_map/ppermute | solution.py:572
  63.4 1.2 %fusion.8 = (bf16[4,208,128]{2,1,0:T(8,128)(2,1)S(1)}, bf16[4,208,128]{2,1,0:T(8,128)(2,1)S(1)}) fusion(f32[2,8,208,128]{3,2,1,0:T(8,128)S(1)} %collective-permute-done.7, f32[2,8,208,128]{3,2,1,0:T(8,128)} %get-tuple-element.53), kind=kLoop, calls=%fused_computation.12 | loop fusion | flops 425984 | bytes 2129920 | tf_op jit(solution)/shard_map/convert_element_type | solution.py:576
  64.7 1.6 %collective-permute-start.9 = (bf16[4,208,128]{2,1,0:T(8,128)(2,1)S(1)}, bf16[4,208,128]{2,1,0:T(8,128)(2,1)S(1)}, u32[]{:S(2)}, u32[]{:S(2)}) collective-permute-start(bf16[4,208,128]{2,1,0:T(8,128)(2,1)S(1)} %get-tuple-element.62), channel_id=1, source_target_pairs={{0,2},{1,3},{2,0},{3,1},{4,6},{5,7},{6,4},{7,5},{8,10},{9,11},{10,... | collective-permute-start | bytes 638984 | tf_op jit(solution)/shard_map/ppermute | solution.py:577
  66.3 0.5 collective-permute-start.8
  66.8 6.1 %collective-permute-done.9 = bf16[4,208,128]{2,1,0:T(8,128)(2,1)S(1)} collective-permute-done((bf16[4,208,128]{2,1,0:T(8,128)(2,1)S(1)}, bf16[4,208,128]{2,1,0:T(8,128)(2,1)S(1)}, u32[]{:S(2)}, u32[]{:S(2)}) %collective-permute-start.9) | collective-permute-done | bytes 213024 | tf_op jit(solution)/shard_map/ppermute | solution.py:577
  72.8 0.1 fusion.3
  72.9 5.4 %collective-permute-start.13 = (bf16[208,128]{1,0:T(8,128)(2,1)S(1)}, bf16[208,128]{1,0:T(8,128)(2,1)S(1)}, u32[]{:S(2)}, u32[]{:S(2)}) collective-permute-start(bf16[208,128]{1,0:T(8,128)(2,1)S(1)} %get-tuple-element.67), channel_id=1, source_target_pairs={{0,16},{4,20},{8,24},{12,28},{16,0},{20,4},{24,8},{28,12},{1,17},{... | collective-permute-start | bytes 159752 | tf_op jit(solution)/shard_map/ppermute | solution.py:548
  78.3 0.6 collective-permute-start.16
  78.9 3.2 %collective-permute-start.15 = (bf16[208,128]{1,0:T(8,128)(2,1)S(1)}, bf16[208,128]{1,0:T(8,128)(2,1)S(1)}, u32[]{:S(2)}, u32[]{:S(2)}) collective-permute-start(bf16[208,128]{1,0:T(8,128)(2,1)S(1)} %get-tuple-element.69), channel_id=1, source_target_pairs={{0,24},{4,28},{8,16},{12,20},{16,8},{20,12},{24,0},{28,4},{1,25},{... | collective-permute-start | bytes 159752 | tf_op jit(solution)/shard_map/ppermute | solution.py:548
  82.1 0.1 fusion.21
  82.2 1.5 %collective-permute-start.10 = (bf16[208,128]{1,0:T(8,128)(2,1)S(1)}, bf16[208,128]{1,0:T(8,128)(2,1)S(1)}, u32[]{:S(2)}, u32[]{:S(2)}) collective-permute-start(bf16[208,128]{1,0:T(8,128)(2,1)S(1)} %get-tuple-element.64), channel_id=1, source_target_pairs={{0,4},{4,0},{8,12},{12,8},{16,20},{20,16},{24,28},{28,24},{1,5},{5... | collective-permute-start | bytes 159752 | tf_op jit(solution)/shard_map/ppermute | solution.py:548
  83.7 2.3 %collective-permute-start.12 = (bf16[208,128]{1,0:T(8,128)(2,1)S(1)}, bf16[208,128]{1,0:T(8,128)(2,1)S(1)}, u32[]{:S(2)}, u32[]{:S(2)}) collective-permute-start(bf16[208,128]{1,0:T(8,128)(2,1)S(1)} %get-tuple-element.65), channel_id=1, source_target_pairs={{0,12},{4,8},{8,4},{12,0},{16,28},{20,24},{24,20},{28,16},{1,13},{... | collective-permute-start | bytes 159752 | tf_op jit(solution)/shard_map/ppermute | solution.py:548
  86.0 2.0 %collective-permute-done.14 = bf16[208,128]{1,0:T(8,128)(2,1)S(1)} collective-permute-done((bf16[208,128]{1,0:T(8,128)(2,1)S(1)}, bf16[208,128]{1,0:T(8,128)(2,1)S(1)}, u32[]{:S(2)}, u32[]{:S(2)}) %collective-permute-start.14) | collective-permute-done | bytes 53280 | tf_op jit(solution)/shard_map/ppermute | solution.py:548
  88.1 0.7 collective-permute-done.12
  88.8 1.4 %collective-permute-done.11 = bf16[208,128]{1,0:T(8,128)(2,1)S(1)} collective-permute-done((bf16[208,128]{1,0:T(8,128)(2,1)S(1)}, bf16[208,128]{1,0:T(8,128)(2,1)S(1)}, u32[]{:S(2)}, u32[]{:S(2)}) %collective-permute-start.11) | collective-permute-done | bytes 53280 | tf_op jit(solution)/shard_map/ppermute | solution.py:548
  90.2 0.1 fusion.16.refs_0_
  90.2 3.0 %collective-permute-start.22 = (bf16[208,128]{1,0:T(8,128)(2,1)S(1)}, bf16[208,128]{1,0:T(8,128)(2,1)S(1)}, u32[]{:S(2)}, u32[]{:S(2)}) collective-permute-start(bf16[208,128]{1,0:T(8,128)(2,1)S(1)} %fusion.16.refs_0_), channel_id=1, source_target_pairs={{0,24},{4,28},{8,16},{12,20},{16,8},{20,12},{24,0},{28,4},{1,25},{... | collective-permute-start | bytes 159752 | tf_op jit(solution)/shard_map/ppermute | solution.py:548
  93.3 1.4 %collective-permute-start.18 = (bf16[208,128]{1,0:T(8,128)(2,1)S(1)}, bf16[208,128]{1,0:T(8,128)(2,1)S(1)}, u32[]{:S(2)}, u32[]{:S(2)}) collective-permute-start(bf16[208,128]{1,0:T(8,128)(2,1)S(1)} %fusion.16.refs_0_), channel_id=1, source_target_pairs={{0,8},{4,12},{8,0},{12,4},{16,24},{20,28},{24,16},{28,20},{1,9},{5... | collective-permute-start | bytes 159752 | tf_op jit(solution)/shard_map/ppermute | solution.py:548
  94.7 0.4 collective-permute-start.17
  95.1 1.2 %collective-permute-done.22.refs_6_ = bf16[208,128]{1,0:T(8,128)(2,1)S(1)} collective-permute-done((bf16[208,128]{1,0:T(8,128)(2,1)S(1)}, bf16[208,128]{1,0:T(8,128)(2,1)S(1)}, u32[]{:S(2)}, u32[]{:S(2)}) %collective-permute-start.22) | collective-permute-done | bytes 53280 | tf_op jit(solution)/shard_map/ppermute | solution.py:548
  96.2 0.5 collective-permute-start.23
  96.7 1.8 %collective-permute-done.20.refs_4_ = bf16[208,128]{1,0:T(8,128)(2,1)S(1)} collective-permute-done((bf16[208,128]{1,0:T(8,128)(2,1)S(1)}, bf16[208,128]{1,0:T(8,128)(2,1)S(1)}, u32[]{:S(2)}, u32[]{:S(2)}) %collective-permute-start.20) | collective-permute-done | bytes 53280 | tf_op jit(solution)/shard_map/ppermute | solution.py:548
  98.5 0.4 collective-permute-start.21
  98.9 1.6 %collective-permute-start.19 = (bf16[208,128]{1,0:T(8,128)(2,1)S(1)}, bf16[208,128]{1,0:T(8,128)(2,1)S(1)}, u32[]{:S(2)}, u32[]{:S(2)}) collective-permute-start(bf16[208,128]{1,0:T(8,128)(2,1)S(1)} %collective-permute-done.18.refs_2_), channel_id=1, source_target_pairs={{0,4},{4,0},{8,12},{12,8},{16,20},{20,16},{24,28},{28,24},{1,5},{5... | collective-permute-start | bytes 159752 | tf_op jit(solution)/shard_map/ppermute | solution.py:548
  100.5 2.1 %collective-permute-done.21.refs_5_ = bf16[208,128]{1,0:T(8,128)(2,1)S(1)} collective-permute-done((bf16[208,128]{1,0:T(8,128)(2,1)S(1)}, bf16[208,128]{1,0:T(8,128)(2,1)S(1)}, u32[]{:S(2)}, u32[]{:S(2)}) %collective-permute-start.21) | collective-permute-done | bytes 53280 | tf_op jit(solution)/shard_map/ppermute | solution.py:548
  102.6 0.6 collective-permute-done.19.refs_3_
  103.2 0.0 copy-done.7
  103.3 0.6 copy-done.8
  103.9 2.0 %unpack_gradients.1 = (f32[512,384]{1,0:T(8,128)}, f32[31,384]{1,0:T(8,128)}, f32[384]{0:T(512)}) custom-call(s32[1,1]{1,0:T(1,128)} %bitcast.ours_ref, bf16[208,128]{1,0:T(8,128)(2,1)} %copy-done.1, bf16[208,128]{1,0:T(8,128)(2,1)} %copy-done.5, bf16[208,128]{1,0:T(8,128)(2,1)} %copy-done.4, bf16[208,128]{1,0:T(8,128)(2,1)} %copy-done.8, ...), custom_call_target="tpu_custom_call" | custom-call | flops 1000000 | bytes 1200000 | tf_op jit(solution)/shard_map/unpack_gradients/pallas_call | solution.py:432
  (71 shorter events, 0.2 us)
Async XLA Ops:
  7.2 31.5 %all-gather.2.cloned.1.call-start = ((), (), s32[]{:S(2)}) async-start(), calls=%async_computation | async-start | bytes 2088960 | tf_op jit(solution)/shard_map/all_gather | solution.py:542
  10.2 17.0 %collective-permute-start = (bf16[64,1024]{1,0:T(8,128)(2,1)}, bf16[64,1024]{1,0:T(8,128)(2,1)S(1)}, u32[]{:S(2)}, u32[]{:S(2)}) collective-permute-start(bf16[64,1024]{1,0:T(8,128)(2,1)} %get-tuple-element.41), channel_id=1, source_target_pairs={{0,4},{4,0},{8,12},{12,8},{16,20},{20,16},{24,28},{28,24},{1,5},{5... | collective-permute-start | bytes 393224 | tf_op jit(solution)/shard_map/ppermute | solution.py:548
  13.2 17.7 %collective-permute-start.1 = (bf16[64,1024]{1,0:T(8,128)(2,1)}, bf16[64,1024]{1,0:T(8,128)(2,1)S(1)}, u32[]{:S(2)}, u32[]{:S(2)}) collective-permute-start(bf16[64,1024]{1,0:T(8,128)(2,1)} %get-tuple-element.42), channel_id=1, source_target_pairs={{0,8},{4,12},{8,0},{12,4},{16,24},{20,28},{24,16},{28,20},{1,9},{5... | collective-permute-start | bytes 393224 | tf_op jit(solution)/shard_map/ppermute | solution.py:548
  14.8 17.1 %collective-permute-start.2 = (bf16[64,1024]{1,0:T(8,128)(2,1)}, bf16[64,1024]{1,0:T(8,128)(2,1)S(1)}, u32[]{:S(2)}, u32[]{:S(2)}) collective-permute-start(bf16[64,1024]{1,0:T(8,128)(2,1)} %get-tuple-element.43), channel_id=1, source_target_pairs={{0,12},{4,8},{8,4},{12,0},{16,28},{20,24},{24,20},{28,16},{1,13},{... | collective-permute-start | bytes 393224 | tf_op jit(solution)/shard_map/ppermute | solution.py:548
  14.8 17.1 %collective-permute-start.3 = (bf16[64,1024]{1,0:T(8,128)(2,1)}, bf16[64,1024]{1,0:T(8,128)(2,1)S(1)}, u32[]{:S(2)}, u32[]{:S(2)}) collective-permute-start(bf16[64,1024]{1,0:T(8,128)(2,1)} %get-tuple-element.44), channel_id=1, source_target_pairs={{0,16},{4,20},{8,24},{12,28},{16,0},{20,4},{24,8},{28,12},{1,17},{... | collective-permute-start | bytes 393224 | tf_op jit(solution)/shard_map/ppermute | solution.py:548
  17.8 18.2 %collective-permute-start.4 = (bf16[64,1024]{1,0:T(8,128)(2,1)}, bf16[64,1024]{1,0:T(8,128)(2,1)S(1)}, u32[]{:S(2)}, u32[]{:S(2)}) collective-permute-start(bf16[64,1024]{1,0:T(8,128)(2,1)} %get-tuple-element.45), channel_id=1, source_target_pairs={{0,20},{4,16},{8,28},{12,24},{16,4},{20,0},{24,12},{28,8},{1,21},{... | collective-permute-start | bytes 393224 | tf_op jit(solution)/shard_map/ppermute | solution.py:548
  21.6 5.6 %copy-start.13 = (bf16[64,1024]{1,0:T(8,128)(2,1)S(1)}, bf16[64,1024]{1,0:T(8,128)(2,1)}, u32[]{:S(2)}) copy-start(bf16[64,1024]{1,0:T(8,128)(2,1)} %get-tuple-element.46) | copy-start | bytes 393220
  21.6 9.3 %copy-start.11 = (bf16[64,1024]{1,0:T(8,128)(2,1)S(1)}, bf16[64,1024]{1,0:T(8,128)(2,1)}, u32[]{:S(2)}) copy-start(bf16[64,1024]{1,0:T(8,128)(2,1)} %get-tuple-element.47) | copy-start | bytes 393220
  21.6 9.4 %copy-start.9 = (s32[1,1,256]{2,1,0:T(1,128)S(1)}, s32[1,1,256]{2,1,0:T(1,128)}, u32[]{:S(2)}) copy-start(s32[1,1,256]{2,1,0:T(1,128)} %param.15) | copy-start | bytes 3076
  27.2 11.5 %copy-start.10 = (bf16[64,1024]{1,0:T(8,128)(2,1)}, bf16[64,1024]{1,0:T(8,128)(2,1)S(1)}, u32[]{:S(2)}) copy-start(bf16[64,1024]{1,0:T(8,128)(2,1)S(1)} %collective-permute-done.refs_1_) | copy-start | bytes 393220
  27.2 8.8 %collective-permute-start.5 = (bf16[64,1024]{1,0:T(8,128)(2,1)S(1)}, bf16[64,1024]{1,0:T(8,128)(2,1)S(1)}, u32[]{:S(2)}, u32[]{:S(2)}) collective-permute-start(bf16[64,1024]{1,0:T(8,128)(2,1)S(1)} %copy-done.13), channel_id=1, source_target_pairs={{0,24},{4,28},{8,16},{12,20},{16,8},{20,12},{24,0},{28,4},{1,25},{... | collective-permute-start | bytes 393224 | tf_op jit(solution)/shard_map/ppermute | solution.py:548
  30.9 7.8 %copy-start.12 = (bf16[64,1024]{1,0:T(8,128)(2,1)}, bf16[64,1024]{1,0:T(8,128)(2,1)S(1)}, u32[]{:S(2)}) copy-start(bf16[64,1024]{1,0:T(8,128)(2,1)S(1)} %collective-permute-done.1.refs_2_) | copy-start | bytes 393220
  30.9 7.8 %collective-permute-start.6 = (bf16[64,1024]{1,0:T(8,128)(2,1)S(1)}, bf16[64,1024]{1,0:T(8,128)(2,1)S(1)}, u32[]{:S(2)}, u32[]{:S(2)}) collective-permute-start(bf16[64,1024]{1,0:T(8,128)(2,1)S(1)} %copy-done.11), channel_id=1, source_target_pairs={{0,28},{4,24},{8,20},{12,16},{16,12},{20,8},{24,4},{28,0},{1,29},{... | collective-permute-start | bytes 393224 | tf_op jit(solution)/shard_map/ppermute | solution.py:548
  31.8 6.9 %copy-start.14 = (bf16[64,1024]{1,0:T(8,128)(2,1)}, bf16[64,1024]{1,0:T(8,128)(2,1)S(1)}, u32[]{:S(2)}) copy-start(bf16[64,1024]{1,0:T(8,128)(2,1)S(1)} %collective-permute-done.2.refs_3_) | copy-start | bytes 393220
  31.8 6.9 %copy-start.15 = (bf16[64,1024]{1,0:T(8,128)(2,1)}, bf16[64,1024]{1,0:T(8,128)(2,1)S(1)}, u32[]{:S(2)}) copy-start(bf16[64,1024]{1,0:T(8,128)(2,1)S(1)} %collective-permute-done.3.refs_4_) | copy-start | bytes 393220
  36.0 2.8 %copy-start.16 = (bf16[64,1024]{1,0:T(8,128)(2,1)}, bf16[64,1024]{1,0:T(8,128)(2,1)S(1)}, u32[]{:S(2)}) copy-start(bf16[64,1024]{1,0:T(8,128)(2,1)S(1)} %collective-permute-done.4.refs_5_) | copy-start | bytes 393220
  36.0 2.8 %copy-start.17 = (bf16[64,1024]{1,0:T(8,128)(2,1)}, bf16[64,1024]{1,0:T(8,128)(2,1)S(1)}, u32[]{:S(2)}) copy-start(bf16[64,1024]{1,0:T(8,128)(2,1)S(1)} %collective-permute-done.5.refs_6_) | copy-start | bytes 393220
  38.7 0.7 copy-start.18
  59.5 13.3 %copy-start = (f32[2,8,208,128]{3,2,1,0:T(8,128)S(1)}, f32[2,8,208,128]{3,2,1,0:T(8,128)}, u32[]{:S(2)}) copy-start(f32[2,8,208,128]{3,2,1,0:T(8,128)} %get-tuple-element.53) | copy-start | bytes 5111812
  59.6 3.9 %collective-permute-start.7 = (f32[2,8,208,128]{3,2,1,0:T(8,128)}, f32[2,8,208,128]{3,2,1,0:T(8,128)S(1)}, u32[]{:S(2)}, u32[]{:S(2)}) collective-permute-start(f32[2,8,208,128]{3,2,1,0:T(8,128)} %get-tuple-element.54), channel_id=1, source_target_pairs={{0,1},{1,0},{2,3},{3,2},{4,5},{5,4},{6,7},{7,6},{8,9},{9,8},{10,11... | collective-permute-start | bytes 5111816 | tf_op jit(solution)/shard_map/ppermute | solution.py:572
  64.7 8.2 %collective-permute-start.9 = (bf16[4,208,128]{2,1,0:T(8,128)(2,1)S(1)}, bf16[4,208,128]{2,1,0:T(8,128)(2,1)S(1)}, u32[]{:S(2)}, u32[]{:S(2)}) collective-permute-start(bf16[4,208,128]{2,1,0:T(8,128)(2,1)S(1)} %get-tuple-element.62), channel_id=1, source_target_pairs={{0,2},{1,3},{2,0},{3,1},{4,6},{5,7},{6,4},{7,5},{8,10},{9,11},{10,... | collective-permute-start | bytes 638984 | tf_op jit(solution)/shard_map/ppermute | solution.py:577
  66.3 15.9 %collective-permute-start.8 = (bf16[4,208,128]{2,1,0:T(8,128)(2,1)S(1)}, bf16[4,208,128]{2,1,0:T(8,128)(2,1)S(1)}, u32[]{:S(2)}, u32[]{:S(2)}) collective-permute-start(bf16[4,208,128]{2,1,0:T(8,128)(2,1)S(1)} %get-tuple-element.63), channel_id=1, source_target_pairs={{0,2},{1,3},{2,0},{3,1},{4,6},{5,7},{6,4},{7,5},{8,10},{9,11},{10,... | collective-permute-start | bytes 638984 | tf_op jit(solution)/shard_map/ppermute | solution.py:577
  72.9 10.8 %collective-permute-start.13 = (bf16[208,128]{1,0:T(8,128)(2,1)S(1)}, bf16[208,128]{1,0:T(8,128)(2,1)S(1)}, u32[]{:S(2)}, u32[]{:S(2)}) collective-permute-start(bf16[208,128]{1,0:T(8,128)(2,1)S(1)} %get-tuple-element.67), channel_id=1, source_target_pairs={{0,16},{4,20},{8,24},{12,28},{16,0},{20,4},{24,8},{28,12},{1,17},{... | collective-permute-start | bytes 159752 | tf_op jit(solution)/shard_map/ppermute | solution.py:548
  78.3 7.8 %collective-permute-start.16 = (bf16[208,128]{1,0:T(8,128)(2,1)S(1)}, bf16[208,128]{1,0:T(8,128)(2,1)S(1)}, u32[]{:S(2)}, u32[]{:S(2)}) collective-permute-start(bf16[208,128]{1,0:T(8,128)(2,1)S(1)} %get-tuple-element.68), channel_id=1, source_target_pairs={{0,28},{4,24},{8,20},{12,16},{16,12},{20,8},{24,4},{28,0},{1,29},{... | collective-permute-start | bytes 159752 | tf_op jit(solution)/shard_map/ppermute | solution.py:548
  78.9 7.1 %collective-permute-start.15 = (bf16[208,128]{1,0:T(8,128)(2,1)S(1)}, bf16[208,128]{1,0:T(8,128)(2,1)S(1)}, u32[]{:S(2)}, u32[]{:S(2)}) collective-permute-start(bf16[208,128]{1,0:T(8,128)(2,1)S(1)} %get-tuple-element.69), channel_id=1, source_target_pairs={{0,24},{4,28},{8,16},{12,20},{16,8},{20,12},{24,0},{28,4},{1,25},{... | collective-permute-start | bytes 159752 | tf_op jit(solution)/shard_map/ppermute | solution.py:548
  82.1 5.9 %collective-permute-start.14 = (bf16[208,128]{1,0:T(8,128)(2,1)S(1)}, bf16[208,128]{1,0:T(8,128)(2,1)S(1)}, u32[]{:S(2)}, u32[]{:S(2)}) collective-permute-start(bf16[208,128]{1,0:T(8,128)(2,1)S(1)} %get-tuple-element.70), channel_id=1, source_target_pairs={{0,20},{4,16},{8,28},{12,24},{16,4},{20,0},{24,12},{28,8},{1,21},{... | collective-permute-start | bytes 159752 | tf_op jit(solution)/shard_map/ppermute | solution.py:548
  82.2 5.8 %collective-permute-start.10 = (bf16[208,128]{1,0:T(8,128)(2,1)S(1)}, bf16[208,128]{1,0:T(8,128)(2,1)S(1)}, u32[]{:S(2)}, u32[]{:S(2)}) collective-permute-start(bf16[208,128]{1,0:T(8,128)(2,1)S(1)} %get-tuple-element.64), channel_id=1, source_target_pairs={{0,4},{4,0},{8,12},{12,8},{16,20},{20,16},{24,28},{28,24},{1,5},{5... | collective-permute-start | bytes 159752 | tf_op jit(solution)/shard_map/ppermute | solution.py:548
  83.7 5.0 %collective-permute-start.12 = (bf16[208,128]{1,0:T(8,128)(2,1)S(1)}, bf16[208,128]{1,0:T(8,128)(2,1)S(1)}, u32[]{:S(2)}, u32[]{:S(2)}) collective-permute-start(bf16[208,128]{1,0:T(8,128)(2,1)S(1)} %get-tuple-element.65), channel_id=1, source_target_pairs={{0,12},{4,8},{8,4},{12,0},{16,28},{20,24},{24,20},{28,16},{1,13},{... | collective-permute-start | bytes 159752 | tf_op jit(solution)/shard_map/ppermute | solution.py:548
  86.0 4.1 %collective-permute-start.11 = (bf16[208,128]{1,0:T(8,128)(2,1)S(1)}, bf16[208,128]{1,0:T(8,128)(2,1)S(1)}, u32[]{:S(2)}, u32[]{:S(2)}) collective-permute-start(bf16[208,128]{1,0:T(8,128)(2,1)S(1)} %get-tuple-element.66), channel_id=1, source_target_pairs={{0,8},{4,12},{8,0},{12,4},{16,24},{20,28},{24,16},{28,20},{1,9},{5... | collective-permute-start | bytes 159752 | tf_op jit(solution)/shard_map/ppermute | solution.py:548
  90.2 13.0 %copy-start.1 = (bf16[208,128]{1,0:T(8,128)(2,1)}, bf16[208,128]{1,0:T(8,128)(2,1)S(1)}, u32[]{:S(2)}) copy-start(bf16[208,128]{1,0:T(8,128)(2,1)S(1)} %fusion.16.refs_0_) | copy-start | bytes 159748
  90.2 6.0 %collective-permute-start.22 = (bf16[208,128]{1,0:T(8,128)(2,1)S(1)}, bf16[208,128]{1,0:T(8,128)(2,1)S(1)}, u32[]{:S(2)}, u32[]{:S(2)}) collective-permute-start(bf16[208,128]{1,0:T(8,128)(2,1)S(1)} %fusion.16.refs_0_), channel_id=1, source_target_pairs={{0,24},{4,28},{8,16},{12,20},{16,8},{20,12},{24,0},{28,4},{1,25},{... | collective-permute-start | bytes 159752 | tf_op jit(solution)/shard_map/ppermute | solution.py:548
  93.3 5.2 %collective-permute-start.20 = (bf16[208,128]{1,0:T(8,128)(2,1)S(1)}, bf16[208,128]{1,0:T(8,128)(2,1)S(1)}, u32[]{:S(2)}, u32[]{:S(2)}) collective-permute-start(bf16[208,128]{1,0:T(8,128)(2,1)S(1)} %fusion.16.refs_0_), channel_id=1, source_target_pairs={{0,16},{4,20},{8,24},{12,28},{16,0},{20,4},{24,8},{28,12},{1,17},{... | collective-permute-start | bytes 159752 | tf_op jit(solution)/shard_map/ppermute | solution.py:548
  93.3 5.6 %collective-permute-start.18 = (bf16[208,128]{1,0:T(8,128)(2,1)S(1)}, bf16[208,128]{1,0:T(8,128)(2,1)S(1)}, u32[]{:S(2)}, u32[]{:S(2)}) collective-permute-start(bf16[208,128]{1,0:T(8,128)(2,1)S(1)} %fusion.16.refs_0_), channel_id=1, source_target_pairs={{0,8},{4,12},{8,0},{12,4},{16,24},{20,28},{24,16},{28,20},{1,9},{5... | collective-permute-start | bytes 159752 | tf_op jit(solution)/shard_map/ppermute | solution.py:548
  94.7 5.8 %collective-permute-start.17 = (bf16[208,128]{1,0:T(8,128)(2,1)S(1)}, bf16[208,128]{1,0:T(8,128)(2,1)S(1)}, u32[]{:S(2)}, u32[]{:S(2)}) collective-permute-start(bf16[208,128]{1,0:T(8,128)(2,1)S(1)} %fusion.16.refs_0_), channel_id=1, source_target_pairs={{0,4},{4,0},{8,12},{12,8},{16,20},{20,16},{24,28},{28,24},{1,5},{5... | collective-permute-start | bytes 159752 | tf_op jit(solution)/shard_map/ppermute | solution.py:548
  96.2 7.0 %copy-start.2 = (bf16[208,128]{1,0:T(8,128)(2,1)}, bf16[208,128]{1,0:T(8,128)(2,1)S(1)}, u32[]{:S(2)}) copy-start(bf16[208,128]{1,0:T(8,128)(2,1)S(1)} %collective-permute-done.22.refs_6_) | copy-start | bytes 159748
  96.2 4.3 %collective-permute-start.23 = (bf16[208,128]{1,0:T(8,128)(2,1)S(1)}, bf16[208,128]{1,0:T(8,128)(2,1)S(1)}, u32[]{:S(2)}, u32[]{:S(2)}) collective-permute-start(bf16[208,128]{1,0:T(8,128)(2,1)S(1)} %collective-permute-done.22.refs_6_), channel_id=1, source_target_pairs={{0,4},{4,0},{8,12},{12,8},{16,20},{20,16},{24,28},{28,24},{1,5},{5... | collective-permute-start | bytes 159752 | tf_op jit(solution)/shard_map/ppermute | solution.py:548
  98.5 4.7 %copy-start.3 = (bf16[208,128]{1,0:T(8,128)(2,1)}, bf16[208,128]{1,0:T(8,128)(2,1)S(1)}, u32[]{:S(2)}) copy-start(bf16[208,128]{1,0:T(8,128)(2,1)S(1)} %collective-permute-done.20.refs_4_) | copy-start | bytes 159748
  98.5 4.1 %collective-permute-start.21 = (bf16[208,128]{1,0:T(8,128)(2,1)S(1)}, bf16[208,128]{1,0:T(8,128)(2,1)S(1)}, u32[]{:S(2)}, u32[]{:S(2)}) collective-permute-start(bf16[208,128]{1,0:T(8,128)(2,1)S(1)} %collective-permute-done.20.refs_4_), channel_id=1, source_target_pairs={{0,4},{4,0},{8,12},{12,8},{16,20},{20,16},{24,28},{28,24},{1,5},{5... | collective-permute-start | bytes 159752 | tf_op jit(solution)/shard_map/ppermute | solution.py:548
  98.9 4.3 %copy-start.4 = (bf16[208,128]{1,0:T(8,128)(2,1)}, bf16[208,128]{1,0:T(8,128)(2,1)S(1)}, u32[]{:S(2)}) copy-start(bf16[208,128]{1,0:T(8,128)(2,1)S(1)} %collective-permute-done.18.refs_2_) | copy-start | bytes 159748
  98.9 4.3 %collective-permute-start.19 = (bf16[208,128]{1,0:T(8,128)(2,1)S(1)}, bf16[208,128]{1,0:T(8,128)(2,1)S(1)}, u32[]{:S(2)}, u32[]{:S(2)}) collective-permute-start(bf16[208,128]{1,0:T(8,128)(2,1)S(1)} %collective-permute-done.18.refs_2_), channel_id=1, source_target_pairs={{0,4},{4,0},{8,12},{12,8},{16,20},{20,16},{24,28},{28,24},{1,5},{5... | collective-permute-start | bytes 159752 | tf_op jit(solution)/shard_map/ppermute | solution.py:548
  100.5 2.7 %copy-start.5 = (bf16[208,128]{1,0:T(8,128)(2,1)}, bf16[208,128]{1,0:T(8,128)(2,1)S(1)}, u32[]{:S(2)}) copy-start(bf16[208,128]{1,0:T(8,128)(2,1)S(1)} %collective-permute-done.17.refs_1_) | copy-start | bytes 159748
  100.5 2.7 %copy-start.6 = (bf16[208,128]{1,0:T(8,128)(2,1)}, bf16[208,128]{1,0:T(8,128)(2,1)S(1)}, u32[]{:S(2)}) copy-start(bf16[208,128]{1,0:T(8,128)(2,1)S(1)} %collective-permute-done.23.refs_7_) | copy-start | bytes 159748
  102.6 0.6 copy-start.7
  103.3 0.6 copy-start.8
Sparse Core Ops, SparseCore 0:
  10.3 22.8 all-gather.1

commit v5 on v3

--- a/solution.py
+++ b/solution.py
@@ -77,7 +77,7 @@
     depth, tap_count = proj_ref.shape[0], taps_ref.shape[0]
     packed_ref[:depth] = proj_ref[...]
     tail_ref[:tap_count] = taps_ref[...].astype(F32)
-    tail_ref[tap_count:] = gain_ref[...].astype(F32)
+    tail_ref[tap_count:] = gain_ref[...].astype(F32)[None, :]
     packed_ref[depth:] = tail_ref[...].astype(BF16)
     count = rows_ref.shape[0]
     rows = rows_ref[...]
@@ -177,31 +177,34 @@
     back_wide = [slice(BEHIND_AT[j], BEHIND_AT[j + 1]) for j in range(3)]
     back_block = [slice(BEHIND_AT[j], BEHIND_AT[j + 1]) for j in range(3, 6)]
 
-    take = take_ref[...]
-    number = lax.broadcasted_iota(jnp.int32, (slots, steps), 0)
-    odd = lax.broadcasted_iota(jnp.int32, (slots, steps), 1) % 2
-    here = number == take
-    even_hot = jnp.where(here & (odd == 0), 1.0, 0.0).astype(BF16)
-    odd_hot = jnp.where(here & (odd == 1), 1.0, 0.0).astype(BF16)
     first = jnp.concatenate([ref[:, :depth] for ref in arrived_refs], axis=0)
     second = jnp.concatenate([ref[:, depth:] for ref in arrived_refs], axis=0)
-    frames = dot_t(even_hot, first) + dot_t(odd_hot, second)
-    frames_ref[...] = frames.astype(BF16)
-    frames_t_ref[...] = jnp.transpose(frames).astype(BF16)
-    live = dot_t(even_hot + odd_hot, jnp.ones((slots, 128), BF16))
-    stat_ref[2] = live * scale
-
-    acc_ref[...] = jnp.zeros_like(acc_ref)
+    for rows in [slice(r, r + 128) for r in range(0, steps, 128)]:
+        take = take_ref[rows]
+        odd = lax.broadcasted_iota(jnp.int32, (128, 128), 0) % 2
+        lane = lax.broadcasted_iota(jnp.int32, (128, 128), 1)
+        even_take = jnp.where(odd == 0, take, -1)
+        odd_take = jnp.where(odd == 1, take, -1)
+        even_hot, odd_hot = [
+            jnp.concatenate(
+                [jnp.where(lane + at == t, 1.0, 0.0).astype(BF16) for at in range(0, slots, 128)], axis=1
+            )
+            for t in (even_take, odd_take)
+        ]
+        frames_ref[rows] = (dot(even_hot, first) + dot(odd_hot, second)).astype(BF16)
+        stat_ref[2, rows] = jnp.where(take >= 0, scale, 0.0)
+
     copies[0].wait()
-
-    def project(i, carry):
-        cols = pl.ds(pl.multiple_of(i * CH, CH), CH)
+    acc = jnp.zeros((steps, 128), F32)
+    for i in range(chunks):
+        cols = slice(i * CH, (i + 1) * CH)
         x = dot(frames_ref[...], params_ref[:depth, cols])
         x_ref[:, cols] = x
-        acc_ref[...] += x[:, :128] + x[:, 128:]
-        return carry
-
-    lax.fori_loop(0, chunks, project, 0)
+        acc = acc + x[:, :128] + x[:, 128:]
+        if i < steps // 128:
+            part_t = jnp.transpose(frames_ref[i * 128 : i * 128 + 128].astype(F32))
+            frames_t_ref[:, i * 128 : i * 128 + 128] = part_t.astype(BF16)
+    acc_ref[...] = acc
     mean = jnp.sum(acc_ref[...], axis=1, keepdims=True) * (1.0 / width)
     stat_ref[0] = jnp.broadcast_to(mean, (steps, 128))
 
@@ -274,7 +277,7 @@
         loss = jnp.zeros((1, CH), F32)
         for t, rows in enumerate(tiles):
             conv = c_b[rows]
-            sig = jax.nn.sigmoid(conv)
+            sig = 0.5 + 0.5 * jnp.tanh(0.5 * conv)
             go = up_ref[rows, cols].astype(F32) * twice(stat_ref[2, rows])
             out = x_ref[rows, cols] + conv * sig
             loss = loss + jnp.sum(out * go, axis=0, keepdims=True)
@@ -537,7 +540,7 @@
     ours = lax.axis_index("dp") if few else jnp.zeros((), jnp.int32)
     ids = [v.astype(jnp.int32).reshape(1, 1) for v in (place % 2, place // 2, ours)]
     wanted = send_rows[0, 0]
-    packed, *outgoing = pick(ids[2], wanted, cached[0, 0], in_proj, conv_kernel, norm_gain[None, :])
+    packed, *outgoing = pick(ids[2], wanted, cached[0, 0], in_proj, conv_kernel, norm_gain)
     params = lax.all_gather(packed, "fsdp", axis=1, tiled=True)
     outgoing, take_own, utt_own = lax.optimization_barrier(
         (outgoing, take_rows[0, 0], utt_index[0, 0])
@@ -555,7 +558,7 @@
         sent = outgoing[0].reshape(wanted.shape + outgoing[0].shape[1:])
         back_in = lax.all_to_all(sent, "dp", split_axis=0, concat_axis=0, tiled=True)
         arrived = [back_in.reshape(-1, back_in.shape[2])]
-    take = jnp.repeat(take_own, 2)[None, :]
+    take = jnp.broadcast_to(jnp.repeat(take_own, 2)[:, None], (2 * take_own.shape[0], 128))
     ahead, behind = prepare(jnp.repeat(utt_own, 2), f_hi, f_lo, back)
 
     depth, shard_cols = in_proj.shape
@@ -576,7 +579,7 @@
     far_in, near_in = [lax.ppermute(v, "fsdp", across) for v in sent]
     far_sum = keep[0, half:] + other[0, half:] + far_in.astype(F32)
     far_out = far_sum.astype(BF16)
-    near_in, far_out = lax.optimization_barrier((near_in, far_out))
+    near_in, _ = lax.optimization_barrier((near_in, far_out))
     near_sum = keep[0, :half] + other[0, :half] + near_in.astype(F32)
     near_out = near_sum.astype(BF16)
     if few:

time: 119 us -> 112 us (0.941)
  waiting for transfers between devices: 30.5 us -> 27 us
  local copies, waits for them, and re-layouts: 4.77 us -> 3.2 us
    ppermute x2, waiting for transfers between devices: 9.75 us -> 6.07 us  [per_device(): far_in, near_in = [lax.ppermute(v, 'fsdp', across) for v in sent]]
where the time goes in v5:
time: 112 us
  starting transfers between devices  35.2 us (31%)
  Pallas kernels  29.8 us (27%)
  waiting for transfers between devices  27 us (24%)
  between operations  14.3 us (13%)
  local copies, waits for them, and re-layouts  3.2 us (3%)
  other arithmetic  2.51 us (2%)
    ppermute x21, starting transfers between devices, swap(): return lax.ppermute(value, 'dp', [(i, i ^ k) for i in range(dp)])  33 us
    pallas_call x1, Pallas kernels, layer(): pl.pallas_call(functools.partial(layer_kernel, len(arrived)), out_shape=[...  19.3 us
    ppermute x21, waiting for transfers between devices, swap(): return lax.ppermute(value, 'dp', [(i, i ^ k) for i in range(dp)])  17.1 us
    ppermute x2, waiting for transfers between devices, per_device(): far_in, near_in = [lax.ppermute(v, 'fsdp', across) for v in sent]  6.07 us
    pallas_call x1, Pallas kernels, prepare(): pl.pallas_call(prep_kernel, out_shape=shapes, in_specs=vmem(4), out_specs...  5.59 us
    ppermute x1, waiting for transfers between devices, per_device(): other = lax.ppermute(send, 'fsdp', [(i, i ^ 1) for i in range(fsdp)])  3.8 us
    pallas_call x1, Pallas kernels, pick(): pl.pallas_call(pick_kernel, out_shape=[jax.ShapeDtypeStruct((proj.shape[0...  2.94 us
  transfers between devices with their start and end apart: 25, of which 11 were waited for; matrix products, arithmetic and copies ran while one was open for 3% of the time, Pallas kernels for 5%

profile of v5, /device:TPU:0, one launch (start us, length us, event | category | flops | bytes accessed | tf_op | source)
XLA Modules:
  0.0 112.0 jit_solution(12936375224329754455)
XLA Ops:
  7.2 0.0 all-gather.2.cloned.1.call-start
  7.2 2.9 %pick_rows.1 = (bf16[544,384]{1,0:T(8,128)(2,1)}, bf16[64,1024]{1,0:T(8,128)(2,1)}, bf16[64,1024]{1,0:T(8,128)(2,1)}, bf16[64,1024]{1,0:T(8,128)(2,1)}, bf16[64,...) custom-call(s32[1,1]{1,0:T(1,128)} %bitcast.ours_ref, ...), custom_call_target="tpu_custom_call" | custom-call | flops 268435456 | bytes 1572864 | tf_op jit(solution)/shard_map/pick_rows/pallas_call | solution.py:419
  10.2 0.0 all-gather.2.cloned.1.call-update
  10.2 3.0 %collective-permute-start = (bf16[64,1024]{1,0:T(8,128)(2,1)}, bf16[64,1024]{1,0:T(8,128)(2,1)S(1)}, u32[]{:S(2)}, u32[]{:S(2)}) collective-permute-start(bf16[64,1024]{1,0:T(8,128)(2,1)} %get-tuple-element.41), channel_id=1, source_target_pairs={{0,4},{4,0},{8,12},{12,8},{16,20},{20,16},{24,28},{28,24},{1,5},{5... | collective-permute-start | bytes 393224 | tf_op jit(solution)/shard_map/ppermute | solution.py:550
  13.2 1.6 %collective-permute-start.1 = (bf16[64,1024]{1,0:T(8,128)(2,1)}, bf16[64,1024]{1,0:T(8,128)(2,1)S(1)}, u32[]{:S(2)}, u32[]{:S(2)}) collective-permute-start(bf16[64,1024]{1,0:T(8,128)(2,1)} %get-tuple-element.42), channel_id=1, source_target_pairs={{0,8},{4,12},{8,0},{12,4},{16,24},{20,28},{24,16},{28,20},{1,9},{5... | collective-permute-start | bytes 393224 | tf_op jit(solution)/shard_map/ppermute | solution.py:550
  14.8 0.0 collective-permute-start.2
  14.8 3.0 %collective-permute-start.3 = (bf16[64,1024]{1,0:T(8,128)(2,1)}, bf16[64,1024]{1,0:T(8,128)(2,1)S(1)}, u32[]{:S(2)}, u32[]{:S(2)}) collective-permute-start(bf16[64,1024]{1,0:T(8,128)(2,1)} %get-tuple-element.44), channel_id=1, source_target_pairs={{0,16},{4,20},{8,24},{12,28},{16,0},{20,4},{24,8},{28,12},{1,17},{... | collective-permute-start | bytes 393224 | tf_op jit(solution)/shard_map/ppermute | solution.py:550
  17.8 1.3 %collective-permute-start.4 = (bf16[64,1024]{1,0:T(8,128)(2,1)}, bf16[64,1024]{1,0:T(8,128)(2,1)S(1)}, u32[]{:S(2)}, u32[]{:S(2)}) collective-permute-start(bf16[64,1024]{1,0:T(8,128)(2,1)} %get-tuple-element.45), channel_id=1, source_target_pairs={{0,20},{4,16},{8,28},{12,24},{16,4},{20,0},{24,12},{28,8},{1,21},{... | collective-permute-start | bytes 393224 | tf_op jit(solution)/shard_map/ppermute | solution.py:550
  19.0 0.7 broadcast_multiply_fusion
  19.7 0.1 broadcast_in_dim.36
  19.8 0.1 mul.12
  20.0 0.1 slice.98
  20.1 0.1 slice.97
  20.1 0.1 slice.92
  20.2 0.1 slice.93
  20.3 0.1 slice.91
  20.3 0.1 slice.90
  20.4 0.1 pad_add_fusion.2
  20.5 0.1 pad_add_fusion
  20.6 0.1 pad_add_fusion.3
  20.7 0.1 pad_add_fusion.5
  20.8 0.1 pad_add_fusion.1
  20.9 0.7 stack.31.pos_ref
  21.6 5.6 %prepare_transforms.1 = (bf16[256,4480]{1,0:T(8,128)(2,1)}, bf16[1408,768]{1,0:T(8,128)(2,1)}) custom-call(s32[8,896]{1,0:T(8,128)} %stack.31.pos_ref, bf16[256,256]{1,0:T(8,128)(2,1)} %constant.81.clone.hi_ref, bf16[256,256]{1,0:T(8,128)(2,1)} %constant.82.clone.lo_ref, bf16[256,768]{1,0:T(8,128)(2,1)} %constant.83.clone.back_ref), custom_call_target="tpu_custom_call" | custom-call | flops 3000000000 | bytes 8000000 | tf_op jit(solution)/shard_map/prepare_transforms/pallas_call | solution.py:474
  27.2 0.0 collective-permute-done.refs_1_
  27.2 3.7 %collective-permute-start.5 = (bf16[64,1024]{1,0:T(8,128)(2,1)S(1)}, bf16[64,1024]{1,0:T(8,128)(2,1)S(1)}, u32[]{:S(2)}, u32[]{:S(2)}) collective-permute-start(bf16[64,1024]{1,0:T(8,128)(2,1)S(1)} %copy-done.14), channel_id=1, source_target_pairs={{0,24},{4,28},{8,16},{12,20},{16,8},{20,12},{24,0},{28,4},{1,25},{... | collective-permute-start | bytes 393224 | tf_op jit(solution)/shard_map/ppermute | solution.py:550
  30.9 0.0 collective-permute-done.1.refs_2_
  30.9 0.1 collective-permute-start.6
  31.0 0.1 broadcast_in_dim.33
  31.1 0.1 broadcast_in_dim.34
  31.3 4.7 %collective-permute-done.4.refs_5_ = bf16[64,1024]{1,0:T(8,128)(2,1)S(1)} collective-permute-done((bf16[64,1024]{1,0:T(8,128)(2,1)}, bf16[64,1024]{1,0:T(8,128)(2,1)S(1)}, u32[]{:S(2)}, u32[]{:S(2)}) %collective-permute-start.4) | collective-permute-done | bytes 131104 | tf_op jit(solution)/shard_map/ppermute | solution.py:550
  36.0 2.7 %collective-permute-done.6.refs_7_ = bf16[64,1024]{1,0:T(8,128)(2,1)S(1)} collective-permute-done((bf16[64,1024]{1,0:T(8,128)(2,1)S(1)}, bf16[64,1024]{1,0:T(8,128)(2,1)S(1)}, u32[]{:S(2)}, u32[]{:S(2)}) %collective-permute-start.6) | collective-permute-done | bytes 131104 | tf_op jit(solution)/shard_map/ppermute | solution.py:550
  38.7 0.8 broadcast_in_dim.35.refs_8_
  39.6 19.3 %layer_step.1 = (f32[2,8,208,128]{3,2,1,0:T(8,128)}, f32[2,8,208,128]{3,2,1,0:T(8,128)}, f32[1,1]{1,0:T(1,128)}) custom-call(s32[1,1]{1,0:T(1,128)} %bitcast.1.core_ref, s32[1,1]{1,0:T(1,128)} %bitcast.2.side_ref, s32[1,1]{1,0:T(1,128)} %bitcast.ours_ref, bf16[64,1024]{1,0:T(8,128)(2,1)} %get-tuple-element.40.refs_0_, bf16[64,1024]{1,0:T(8,128)(2,1)} %copy-done.10, ...), custom_call_target="tpu_custom_call" | custom-call | flops 10000000000 | bytes 16000000 | tf_op jit(solution)/shard_map/layer_step/pallas_call | solution.py:517
  58.9 0.1 collective-permute-start.7
  58.9 3.8 %collective-permute-done.7 = f32[2,8,208,128]{3,2,1,0:T(8,128)S(1)} collective-permute-done((f32[2,8,208,128]{3,2,1,0:T(8,128)}, f32[2,8,208,128]{3,2,1,0:T(8,128)S(1)}, u32[]{:S(2)}, u32[]{:S(2)}) %collective-permute-start.7) | collective-permute-done | bytes 1703968 | tf_op jit(solution)/shard_map/ppermute | solution.py:574
  62.7 1.2 %fusion.8 = (bf16[4,208,128]{2,1,0:T(8,128)(2,1)S(1)}, bf16[4,208,128]{2,1,0:T(8,128)(2,1)S(1)}) fusion(f32[2,8,208,128]{3,2,1,0:T(8,128)S(1)} %collective-permute-done.7, f32[2,8,208,128]{3,2,1,0:T(8,128)} %get-tuple-element.53), kind=kLoop, calls=%fused_computation.12 | loop fusion | flops 425984 | bytes 2129920 | tf_op jit(solution)/shard_map/convert_element_type | solution.py:578
  64.0 1.6 %collective-permute-start.9 = (bf16[4,208,128]{2,1,0:T(8,128)(2,1)S(1)}, bf16[4,208,128]{2,1,0:T(8,128)(2,1)S(1)}, u32[]{:S(2)}, u32[]{:S(2)}) collective-permute-start(bf16[4,208,128]{2,1,0:T(8,128)(2,1)S(1)} %get-tuple-element.62), channel_id=1, source_target_pairs={{0,2},{1,3},{2,0},{3,1},{4,6},{5,7},{6,4},{7,5},{8,10},{9,11},{10,... | collective-permute-start | bytes 638984 | tf_op jit(solution)/shard_map/ppermute | solution.py:579
  65.6 0.5 collective-permute-start.8
  66.1 6.1 %collective-permute-done.9 = bf16[4,208,128]{2,1,0:T(8,128)(2,1)S(1)} collective-permute-done((bf16[4,208,128]{2,1,0:T(8,128)(2,1)S(1)}, bf16[4,208,128]{2,1,0:T(8,128)(2,1)S(1)}, u32[]{:S(2)}, u32[]{:S(2)}) %collective-permute-start.9) | collective-permute-done | bytes 213024 | tf_op jit(solution)/shard_map/ppermute | solution.py:579
  72.1 0.1 fusion.3
  72.2 5.4 %collective-permute-start.13 = (bf16[208,128]{1,0:T(8,128)(2,1)S(1)}, bf16[208,128]{1,0:T(8,128)(2,1)S(1)}, u32[]{:S(2)}, u32[]{:S(2)}) collective-permute-start(bf16[208,128]{1,0:T(8,128)(2,1)S(1)} %get-tuple-element.67), channel_id=1, source_target_pairs={{0,16},{4,20},{8,24},{12,28},{16,0},{20,4},{24,8},{28,12},{1,17},{... | collective-permute-start | bytes 159752 | tf_op jit(solution)/shard_map/ppermute | solution.py:550
  77.6 0.6 collective-permute-start.16
  78.2 3.2 %collective-permute-start.15 = (bf16[208,128]{1,0:T(8,128)(2,1)S(1)}, bf16[208,128]{1,0:T(8,128)(2,1)S(1)}, u32[]{:S(2)}, u32[]{:S(2)}) collective-permute-start(bf16[208,128]{1,0:T(8,128)(2,1)S(1)} %get-tuple-element.69), channel_id=1, source_target_pairs={{0,24},{4,28},{8,16},{12,20},{16,8},{20,12},{24,0},{28,4},{1,25},{... | collective-permute-start | bytes 159752 | tf_op jit(solution)/shard_map/ppermute | solution.py:550
  81.5 0.1 fusion.21
  81.5 1.5 %collective-permute-start.10 = (bf16[208,128]{1,0:T(8,128)(2,1)S(1)}, bf16[208,128]{1,0:T(8,128)(2,1)S(1)}, u32[]{:S(2)}, u32[]{:S(2)}) collective-permute-start(bf16[208,128]{1,0:T(8,128)(2,1)S(1)} %get-tuple-element.64), channel_id=1, source_target_pairs={{0,4},{4,0},{8,12},{12,8},{16,20},{20,16},{24,28},{28,24},{1,5},{5... | collective-permute-start | bytes 159752 | tf_op jit(solution)/shard_map/ppermute | solution.py:550
  83.0 2.3 %collective-permute-start.12 = (bf16[208,128]{1,0:T(8,128)(2,1)S(1)}, bf16[208,128]{1,0:T(8,128)(2,1)S(1)}, u32[]{:S(2)}, u32[]{:S(2)}) collective-permute-start(bf16[208,128]{1,0:T(8,128)(2,1)S(1)} %get-tuple-element.65), channel_id=1, source_target_pairs={{0,12},{4,8},{8,4},{12,0},{16,28},{20,24},{24,20},{28,16},{1,13},{... | collective-permute-start | bytes 159752 | tf_op jit(solution)/shard_map/ppermute | solution.py:550
  85.4 2.0 %collective-permute-done.14 = bf16[208,128]{1,0:T(8,128)(2,1)S(1)} collective-permute-done((bf16[208,128]{1,0:T(8,128)(2,1)S(1)}, bf16[208,128]{1,0:T(8,128)(2,1)S(1)}, u32[]{:S(2)}, u32[]{:S(2)}) %collective-permute-start.14) | collective-permute-done | bytes 53280 | tf_op jit(solution)/shard_map/ppermute | solution.py:550
  87.4 0.7 collective-permute-done.12
  88.1 1.4 %collective-permute-done.11 = bf16[208,128]{1,0:T(8,128)(2,1)S(1)} collective-permute-done((bf16[208,128]{1,0:T(8,128)(2,1)S(1)}, bf16[208,128]{1,0:T(8,128)(2,1)S(1)}, u32[]{:S(2)}, u32[]{:S(2)}) %collective-permute-start.11) | collective-permute-done | bytes 53280 | tf_op jit(solution)/shard_map/ppermute | solution.py:550
  89.5 0.1 fusion.16.refs_0_
  89.6 3.0 %collective-permute-start.22 = (bf16[208,128]{1,0:T(8,128)(2,1)S(1)}, bf16[208,128]{1,0:T(8,128)(2,1)S(1)}, u32[]{:S(2)}, u32[]{:S(2)}) collective-permute-start(bf16[208,128]{1,0:T(8,128)(2,1)S(1)} %fusion.16.refs_0_), channel_id=1, source_target_pairs={{0,24},{4,28},{8,16},{12,20},{16,8},{20,12},{24,0},{28,4},{1,25},{... | collective-permute-start | bytes 159752 | tf_op jit(solution)/shard_map/ppermute | solution.py:550
  92.6 1.4 %collective-permute-start.18 = (bf16[208,128]{1,0:T(8,128)(2,1)S(1)}, bf16[208,128]{1,0:T(8,128)(2,1)S(1)}, u32[]{:S(2)}, u32[]{:S(2)}) collective-permute-start(bf16[208,128]{1,0:T(8,128)(2,1)S(1)} %fusion.16.refs_0_), channel_id=1, source_target_pairs={{0,8},{4,12},{8,0},{12,4},{16,24},{20,28},{24,16},{28,20},{1,9},{5... | collective-permute-start | bytes 159752 | tf_op jit(solution)/shard_map/ppermute | solution.py:550
  94.0 0.4 collective-permute-start.17
  94.4 1.2 %collective-permute-done.22.refs_6_ = bf16[208,128]{1,0:T(8,128)(2,1)S(1)} collective-permute-done((bf16[208,128]{1,0:T(8,128)(2,1)S(1)}, bf16[208,128]{1,0:T(8,128)(2,1)S(1)}, u32[]{:S(2)}, u32[]{:S(2)}) %collective-permute-start.22) | collective-permute-done | bytes 53280 | tf_op jit(solution)/shard_map/ppermute | solution.py:550
  95.6 0.5 collective-permute-start.23
  96.0 1.8 %collective-permute-done.20.refs_4_ = bf16[208,128]{1,0:T(8,128)(2,1)S(1)} collective-permute-done((bf16[208,128]{1,0:T(8,128)(2,1)S(1)}, bf16[208,128]{1,0:T(8,128)(2,1)S(1)}, u32[]{:S(2)}, u32[]{:S(2)}) %collective-permute-start.20) | collective-permute-done | bytes 53280 | tf_op jit(solution)/shard_map/ppermute | solution.py:550
  97.8 0.4 collective-permute-start.21
  98.2 1.6 %collective-permute-start.19 = (bf16[208,128]{1,0:T(8,128)(2,1)S(1)}, bf16[208,128]{1,0:T(8,128)(2,1)S(1)}, u32[]{:S(2)}, u32[]{:S(2)}) collective-permute-start(bf16[208,128]{1,0:T(8,128)(2,1)S(1)} %collective-permute-done.18.refs_2_), channel_id=1, source_target_pairs={{0,4},{4,0},{8,12},{12,8},{16,20},{20,16},{24,28},{28,24},{1,5},{5... | collective-permute-start | bytes 159752 | tf_op jit(solution)/shard_map/ppermute | solution.py:550
  99.9 2.1 %collective-permute-done.21.refs_5_ = bf16[208,128]{1,0:T(8,128)(2,1)S(1)} collective-permute-done((bf16[208,128]{1,0:T(8,128)(2,1)S(1)}, bf16[208,128]{1,0:T(8,128)(2,1)S(1)}, u32[]{:S(2)}, u32[]{:S(2)}) %collective-permute-start.21) | collective-permute-done | bytes 53280 | tf_op jit(solution)/shard_map/ppermute | solution.py:550
  101.9 0.6 collective-permute-done.19.refs_3_
  102.5 0.0 copy-done.7
  102.6 0.6 copy-done.8
  103.2 2.0 %unpack_gradients.1 = (f32[512,384]{1,0:T(8,128)}, f32[31,384]{1,0:T(8,128)}, f32[384]{0:T(512)}) custom-call(s32[1,1]{1,0:T(1,128)} %bitcast.ours_ref, bf16[208,128]{1,0:T(8,128)(2,1)} %copy-done.1, bf16[208,128]{1,0:T(8,128)(2,1)} %copy-done.5, bf16[208,128]{1,0:T(8,128)(2,1)} %copy-done.4, bf16[208,128]{1,0:T(8,128)(2,1)} %copy-done.8, ...), custom_call_target="tpu_custom_call" | custom-call | flops 1000000 | bytes 1200000 | tf_op jit(solution)/shard_map/unpack_gradients/pallas_call | solution.py:434
  (72 shorter events, 0.2 us)
Async XLA Ops:
  7.2 31.5 %all-gather.2.cloned.1.call-start = ((), (), s32[]{:S(2)}) async-start(), calls=%async_computation | async-start | bytes 2088960 | tf_op jit(solution)/shard_map/all_gather | solution.py:544
  10.2 17.0 %collective-permute-start = (bf16[64,1024]{1,0:T(8,128)(2,1)}, bf16[64,1024]{1,0:T(8,128)(2,1)S(1)}, u32[]{:S(2)}, u32[]{:S(2)}) collective-permute-start(bf16[64,1024]{1,0:T(8,128)(2,1)} %get-tuple-element.41), channel_id=1, source_target_pairs={{0,4},{4,0},{8,12},{12,8},{16,20},{20,16},{24,28},{28,24},{1,5},{5... | collective-permute-start | bytes 393224 | tf_op jit(solution)/shard_map/ppermute | solution.py:550
  13.2 17.7 %collective-permute-start.1 = (bf16[64,1024]{1,0:T(8,128)(2,1)}, bf16[64,1024]{1,0:T(8,128)(2,1)S(1)}, u32[]{:S(2)}, u32[]{:S(2)}) collective-permute-start(bf16[64,1024]{1,0:T(8,128)(2,1)} %get-tuple-element.42), channel_id=1, source_target_pairs={{0,8},{4,12},{8,0},{12,4},{16,24},{20,28},{24,16},{28,20},{1,9},{5... | collective-permute-start | bytes 393224 | tf_op jit(solution)/shard_map/ppermute | solution.py:550
  14.8 16.5 %collective-permute-start.2 = (bf16[64,1024]{1,0:T(8,128)(2,1)}, bf16[64,1024]{1,0:T(8,128)(2,1)S(1)}, u32[]{:S(2)}, u32[]{:S(2)}) collective-permute-start(bf16[64,1024]{1,0:T(8,128)(2,1)} %get-tuple-element.43), channel_id=1, source_target_pairs={{0,12},{4,8},{8,4},{12,0},{16,28},{20,24},{24,20},{28,16},{1,13},{... | collective-permute-start | bytes 393224 | tf_op jit(solution)/shard_map/ppermute | solution.py:550
  14.8 16.5 %collective-permute-start.3 = (bf16[64,1024]{1,0:T(8,128)(2,1)}, bf16[64,1024]{1,0:T(8,128)(2,1)S(1)}, u32[]{:S(2)}, u32[]{:S(2)}) collective-permute-start(bf16[64,1024]{1,0:T(8,128)(2,1)} %get-tuple-element.44), channel_id=1, source_target_pairs={{0,16},{4,20},{8,24},{12,28},{16,0},{20,4},{24,8},{28,12},{1,17},{... | collective-permute-start | bytes 393224 | tf_op jit(solution)/shard_map/ppermute | solution.py:550
  17.8 18.2 %collective-permute-start.4 = (bf16[64,1024]{1,0:T(8,128)(2,1)}, bf16[64,1024]{1,0:T(8,128)(2,1)S(1)}, u32[]{:S(2)}, u32[]{:S(2)}) collective-permute-start(bf16[64,1024]{1,0:T(8,128)(2,1)} %get-tuple-element.45), channel_id=1, source_target_pairs={{0,20},{4,16},{8,28},{12,24},{16,4},{20,0},{24,12},{28,8},{1,21},{... | collective-permute-start | bytes 393224 | tf_op jit(solution)/shard_map/ppermute | solution.py:550
  21.6 5.6 %copy-start.14 = (bf16[64,1024]{1,0:T(8,128)(2,1)S(1)}, bf16[64,1024]{1,0:T(8,128)(2,1)}, u32[]{:S(2)}) copy-start(bf16[64,1024]{1,0:T(8,128)(2,1)} %get-tuple-element.46) | copy-start | bytes 393220
  21.6 9.3 %copy-start.12 = (bf16[64,1024]{1,0:T(8,128)(2,1)S(1)}, bf16[64,1024]{1,0:T(8,128)(2,1)}, u32[]{:S(2)}) copy-start(bf16[64,1024]{1,0:T(8,128)(2,1)} %get-tuple-element.47) | copy-start | bytes 393220
  21.6 9.4 %copy-start.9 = (s32[1,1,256]{2,1,0:T(1,128)S(1)}, s32[1,1,256]{2,1,0:T(1,128)}, u32[]{:S(2)}) copy-start(s32[1,1,256]{2,1,0:T(1,128)} %param.15) | copy-start | bytes 3076
  27.2 12.3 %copy-start.10 = (bf16[64,1024]{1,0:T(8,128)(2,1)}, bf16[64,1024]{1,0:T(8,128)(2,1)S(1)}, u32[]{:S(2)}) copy-start(bf16[64,1024]{1,0:T(8,128)(2,1)S(1)} %collective-permute-done.refs_1_) | copy-start | bytes 393220
  27.2 8.8 %collective-permute-start.5 = (bf16[64,1024]{1,0:T(8,128)(2,1)S(1)}, bf16[64,1024]{1,0:T(8,128)(2,1)S(1)}, u32[]{:S(2)}, u32[]{:S(2)}) collective-permute-start(bf16[64,1024]{1,0:T(8,128)(2,1)S(1)} %copy-done.14), channel_id=1, source_target_pairs={{0,24},{4,28},{8,16},{12,20},{16,8},{20,12},{24,0},{28,4},{1,25},{... | collective-permute-start | bytes 393224 | tf_op jit(solution)/shard_map/ppermute | solution.py:550
  30.9 8.7 %copy-start.11 = (bf16[64,1024]{1,0:T(8,128)(2,1)}, bf16[64,1024]{1,0:T(8,128)(2,1)S(1)}, u32[]{:S(2)}) copy-start(bf16[64,1024]{1,0:T(8,128)(2,1)S(1)} %collective-permute-done.1.refs_2_) | copy-start | bytes 393220
  30.9 7.8 %collective-permute-start.6 = (bf16[64,1024]{1,0:T(8,128)(2,1)S(1)}, bf16[64,1024]{1,0:T(8,128)(2,1)S(1)}, u32[]{:S(2)}, u32[]{:S(2)}) collective-permute-start(bf16[64,1024]{1,0:T(8,128)(2,1)S(1)} %copy-done.12), channel_id=1, source_target_pairs={{0,28},{4,24},{8,20},{12,16},{16,12},{20,8},{24,4},{28,0},{1,29},{... | collective-permute-start | bytes 393224 | tf_op jit(solution)/shard_map/ppermute | solution.py:550
  31.3 8.3 %copy-start.13 = (bf16[64,1024]{1,0:T(8,128)(2,1)}, bf16[64,1024]{1,0:T(8,128)(2,1)S(1)}, u32[]{:S(2)}) copy-start(bf16[64,1024]{1,0:T(8,128)(2,1)S(1)} %collective-permute-done.2.refs_3_) | copy-start | bytes 393220
  31.3 8.3 %copy-start.15 = (bf16[64,1024]{1,0:T(8,128)(2,1)}, bf16[64,1024]{1,0:T(8,128)(2,1)S(1)}, u32[]{:S(2)}) copy-start(bf16[64,1024]{1,0:T(8,128)(2,1)S(1)} %collective-permute-done.3.refs_4_) | copy-start | bytes 393220
  36.0 3.6 %copy-start.16 = (bf16[64,1024]{1,0:T(8,128)(2,1)}, bf16[64,1024]{1,0:T(8,128)(2,1)S(1)}, u32[]{:S(2)}) copy-start(bf16[64,1024]{1,0:T(8,128)(2,1)S(1)} %collective-permute-done.4.refs_5_) | copy-start | bytes 393220
  36.0 3.6 %copy-start.17 = (bf16[64,1024]{1,0:T(8,128)(2,1)}, bf16[64,1024]{1,0:T(8,128)(2,1)S(1)}, u32[]{:S(2)}) copy-start(bf16[64,1024]{1,0:T(8,128)(2,1)S(1)} %collective-permute-done.5.refs_6_) | copy-start | bytes 393220
  38.7 0.9 copy-start.18
  58.9 13.3 %copy-start = (f32[2,8,208,128]{3,2,1,0:T(8,128)S(1)}, f32[2,8,208,128]{3,2,1,0:T(8,128)}, u32[]{:S(2)}) copy-start(f32[2,8,208,128]{3,2,1,0:T(8,128)} %get-tuple-element.53) | copy-start | bytes 5111812
  58.9 3.9 %collective-permute-start.7 = (f32[2,8,208,128]{3,2,1,0:T(8,128)}, f32[2,8,208,128]{3,2,1,0:T(8,128)S(1)}, u32[]{:S(2)}, u32[]{:S(2)}) collective-permute-start(f32[2,8,208,128]{3,2,1,0:T(8,128)} %get-tuple-element.54), channel_id=1, source_target_pairs={{0,1},{1,0},{2,3},{3,2},{4,5},{5,4},{6,7},{7,6},{8,9},{9,8},{10,11... | collective-permute-start | bytes 5111816 | tf_op jit(solution)/shard_map/ppermute | solution.py:574
  64.0 8.2 %collective-permute-start.9 = (bf16[4,208,128]{2,1,0:T(8,128)(2,1)S(1)}, bf16[4,208,128]{2,1,0:T(8,128)(2,1)S(1)}, u32[]{:S(2)}, u32[]{:S(2)}) collective-permute-start(bf16[4,208,128]{2,1,0:T(8,128)(2,1)S(1)} %get-tuple-element.62), channel_id=1, source_target_pairs={{0,2},{1,3},{2,0},{3,1},{4,6},{5,7},{6,4},{7,5},{8,10},{9,11},{10,... | collective-permute-start | bytes 638984 | tf_op jit(solution)/shard_map/ppermute | solution.py:579
  65.6 15.9 %collective-permute-start.8 = (bf16[4,208,128]{2,1,0:T(8,128)(2,1)S(1)}, bf16[4,208,128]{2,1,0:T(8,128)(2,1)S(1)}, u32[]{:S(2)}, u32[]{:S(2)}) collective-permute-start(bf16[4,208,128]{2,1,0:T(8,128)(2,1)S(1)} %get-tuple-element.63), channel_id=1, source_target_pairs={{0,2},{1,3},{2,0},{3,1},{4,6},{5,7},{6,4},{7,5},{8,10},{9,11},{10,... | collective-permute-start | bytes 638984 | tf_op jit(solution)/shard_map/ppermute | solution.py:579
  72.2 10.8 %collective-permute-start.13 = (bf16[208,128]{1,0:T(8,128)(2,1)S(1)}, bf16[208,128]{1,0:T(8,128)(2,1)S(1)}, u32[]{:S(2)}, u32[]{:S(2)}) collective-permute-start(bf16[208,128]{1,0:T(8,128)(2,1)S(1)} %get-tuple-element.67), channel_id=1, source_target_pairs={{0,16},{4,20},{8,24},{12,28},{16,0},{20,4},{24,8},{28,12},{1,17},{... | collective-permute-start | bytes 159752 | tf_op jit(solution)/shard_map/ppermute | solution.py:550
  77.6 7.8 %collective-permute-start.16 = (bf16[208,128]{1,0:T(8,128)(2,1)S(1)}, bf16[208,128]{1,0:T(8,128)(2,1)S(1)}, u32[]{:S(2)}, u32[]{:S(2)}) collective-permute-start(bf16[208,128]{1,0:T(8,128)(2,1)S(1)} %get-tuple-element.68), channel_id=1, source_target_pairs={{0,28},{4,24},{8,20},{12,16},{16,12},{20,8},{24,4},{28,0},{1,29},{... | collective-permute-start | bytes 159752 | tf_op jit(solution)/shard_map/ppermute | solution.py:550
  78.2 7.1 %collective-permute-start.15 = (bf16[208,128]{1,0:T(8,128)(2,1)S(1)}, bf16[208,128]{1,0:T(8,128)(2,1)S(1)}, u32[]{:S(2)}, u32[]{:S(2)}) collective-permute-start(bf16[208,128]{1,0:T(8,128)(2,1)S(1)} %get-tuple-element.69), channel_id=1, source_target_pairs={{0,24},{4,28},{8,16},{12,20},{16,8},{20,12},{24,0},{28,4},{1,25},{... | collective-permute-start | bytes 159752 | tf_op jit(solution)/shard_map/ppermute | solution.py:550
  81.4 5.9 %collective-permute-start.14 = (bf16[208,128]{1,0:T(8,128)(2,1)S(1)}, bf16[208,128]{1,0:T(8,128)(2,1)S(1)}, u32[]{:S(2)}, u32[]{:S(2)}) collective-permute-start(bf16[208,128]{1,0:T(8,128)(2,1)S(1)} %get-tuple-element.70), channel_id=1, source_target_pairs={{0,20},{4,16},{8,28},{12,24},{16,4},{20,0},{24,12},{28,8},{1,21},{... | collective-permute-start | bytes 159752 | tf_op jit(solution)/shard_map/ppermute | solution.py:550
  81.5 5.8 %collective-permute-start.10 = (bf16[208,128]{1,0:T(8,128)(2,1)S(1)}, bf16[208,128]{1,0:T(8,128)(2,1)S(1)}, u32[]{:S(2)}, u32[]{:S(2)}) collective-permute-start(bf16[208,128]{1,0:T(8,128)(2,1)S(1)} %get-tuple-element.64), channel_id=1, source_target_pairs={{0,4},{4,0},{8,12},{12,8},{16,20},{20,16},{24,28},{28,24},{1,5},{5... | collective-permute-start | bytes 159752 | tf_op jit(solution)/shard_map/ppermute | solution.py:550
  83.0 5.0 %collective-permute-start.12 = (bf16[208,128]{1,0:T(8,128)(2,1)S(1)}, bf16[208,128]{1,0:T(8,128)(2,1)S(1)}, u32[]{:S(2)}, u32[]{:S(2)}) collective-permute-start(bf16[208,128]{1,0:T(8,128)(2,1)S(1)} %get-tuple-element.65), channel_id=1, source_target_pairs={{0,12},{4,8},{8,4},{12,0},{16,28},{20,24},{24,20},{28,16},{1,13},{... | collective-permute-start | bytes 159752 | tf_op jit(solution)/shard_map/ppermute | solution.py:550
  85.3 4.1 %collective-permute-start.11 = (bf16[208,128]{1,0:T(8,128)(2,1)S(1)}, bf16[208,128]{1,0:T(8,128)(2,1)S(1)}, u32[]{:S(2)}, u32[]{:S(2)}) collective-permute-start(bf16[208,128]{1,0:T(8,128)(2,1)S(1)} %get-tuple-element.66), channel_id=1, source_target_pairs={{0,8},{4,12},{8,0},{12,4},{16,24},{20,28},{24,16},{28,20},{1,9},{5... | collective-permute-start | bytes 159752 | tf_op jit(solution)/shard_map/ppermute | solution.py:550
  89.5 13.0 %copy-start.1 = (bf16[208,128]{1,0:T(8,128)(2,1)}, bf16[208,128]{1,0:T(8,128)(2,1)S(1)}, u32[]{:S(2)}) copy-start(bf16[208,128]{1,0:T(8,128)(2,1)S(1)} %fusion.16.refs_0_) | copy-start | bytes 159748
  89.6 6.0 %collective-permute-start.22 = (bf16[208,128]{1,0:T(8,128)(2,1)S(1)}, bf16[208,128]{1,0:T(8,128)(2,1)S(1)}, u32[]{:S(2)}, u32[]{:S(2)}) collective-permute-start(bf16[208,128]{1,0:T(8,128)(2,1)S(1)} %fusion.16.refs_0_), channel_id=1, source_target_pairs={{0,24},{4,28},{8,16},{12,20},{16,8},{20,12},{24,0},{28,4},{1,25},{... | collective-permute-start | bytes 159752 | tf_op jit(solution)/shard_map/ppermute | solution.py:550
  92.6 5.2 %collective-permute-start.20 = (bf16[208,128]{1,0:T(8,128)(2,1)S(1)}, bf16[208,128]{1,0:T(8,128)(2,1)S(1)}, u32[]{:S(2)}, u32[]{:S(2)}) collective-permute-start(bf16[208,128]{1,0:T(8,128)(2,1)S(1)} %fusion.16.refs_0_), channel_id=1, source_target_pairs={{0,16},{4,20},{8,24},{12,28},{16,0},{20,4},{24,8},{28,12},{1,17},{... | collective-permute-start | bytes 159752 | tf_op jit(solution)/shard_map/ppermute | solution.py:550
  92.6 5.6 %collective-permute-start.18 = (bf16[208,128]{1,0:T(8,128)(2,1)S(1)}, bf16[208,128]{1,0:T(8,128)(2,1)S(1)}, u32[]{:S(2)}, u32[]{:S(2)}) collective-permute-start(bf16[208,128]{1,0:T(8,128)(2,1)S(1)} %fusion.16.refs_0_), channel_id=1, source_target_pairs={{0,8},{4,12},{8,0},{12,4},{16,24},{20,28},{24,16},{28,20},{1,9},{5... | collective-permute-start | bytes 159752 | tf_op jit(solution)/shard_map/ppermute | solution.py:550
  94.0 5.8 %collective-permute-start.17 = (bf16[208,128]{1,0:T(8,128)(2,1)S(1)}, bf16[208,128]{1,0:T(8,128)(2,1)S(1)}, u32[]{:S(2)}, u32[]{:S(2)}) collective-permute-start(bf16[208,128]{1,0:T(8,128)(2,1)S(1)} %fusion.16.refs_0_), channel_id=1, source_target_pairs={{0,4},{4,0},{8,12},{12,8},{16,20},{20,16},{24,28},{28,24},{1,5},{5... | collective-permute-start | bytes 159752 | tf_op jit(solution)/shard_map/ppermute | solution.py:550
  95.6 7.0 %copy-start.2 = (bf16[208,128]{1,0:T(8,128)(2,1)}, bf16[208,128]{1,0:T(8,128)(2,1)S(1)}, u32[]{:S(2)}) copy-start(bf16[208,128]{1,0:T(8,128)(2,1)S(1)} %collective-permute-done.22.refs_6_) | copy-start | bytes 159748
  95.6 4.3 %collective-permute-start.23 = (bf16[208,128]{1,0:T(8,128)(2,1)S(1)}, bf16[208,128]{1,0:T(8,128)(2,1)S(1)}, u32[]{:S(2)}, u32[]{:S(2)}) collective-permute-start(bf16[208,128]{1,0:T(8,128)(2,1)S(1)} %collective-permute-done.22.refs_6_), channel_id=1, source_target_pairs={{0,4},{4,0},{8,12},{12,8},{16,20},{20,16},{24,28},{28,24},{1,5},{5... | collective-permute-start | bytes 159752 | tf_op jit(solution)/shard_map/ppermute | solution.py:550
  97.8 4.7 %copy-start.3 = (bf16[208,128]{1,0:T(8,128)(2,1)}, bf16[208,128]{1,0:T(8,128)(2,1)S(1)}, u32[]{:S(2)}) copy-start(bf16[208,128]{1,0:T(8,128)(2,1)S(1)} %collective-permute-done.20.refs_4_) | copy-start | bytes 159748
  97.8 4.1 %collective-permute-start.21 = (bf16[208,128]{1,0:T(8,128)(2,1)S(1)}, bf16[208,128]{1,0:T(8,128)(2,1)S(1)}, u32[]{:S(2)}, u32[]{:S(2)}) collective-permute-start(bf16[208,128]{1,0:T(8,128)(2,1)S(1)} %collective-permute-done.20.refs_4_), channel_id=1, source_target_pairs={{0,4},{4,0},{8,12},{12,8},{16,20},{20,16},{24,28},{28,24},{1,5},{5... | collective-permute-start | bytes 159752 | tf_op jit(solution)/shard_map/ppermute | solution.py:550
  98.2 4.3 %copy-start.4 = (bf16[208,128]{1,0:T(8,128)(2,1)}, bf16[208,128]{1,0:T(8,128)(2,1)S(1)}, u32[]{:S(2)}) copy-start(bf16[208,128]{1,0:T(8,128)(2,1)S(1)} %collective-permute-done.18.refs_2_) | copy-start | bytes 159748
  98.2 4.3 %collective-permute-start.19 = (bf16[208,128]{1,0:T(8,128)(2,1)S(1)}, bf16[208,128]{1,0:T(8,128)(2,1)S(1)}, u32[]{:S(2)}, u32[]{:S(2)}) collective-permute-start(bf16[208,128]{1,0:T(8,128)(2,1)S(1)} %collective-permute-done.18.refs_2_), channel_id=1, source_target_pairs={{0,4},{4,0},{8,12},{12,8},{16,20},{20,16},{24,28},{28,24},{1,5},{5... | collective-permute-start | bytes 159752 | tf_op jit(solution)/shard_map/ppermute | solution.py:550
  99.8 2.7 %copy-start.5 = (bf16[208,128]{1,0:T(8,128)(2,1)}, bf16[208,128]{1,0:T(8,128)(2,1)S(1)}, u32[]{:S(2)}) copy-start(bf16[208,128]{1,0:T(8,128)(2,1)S(1)} %collective-permute-done.17.refs_1_) | copy-start | bytes 159748
  99.8 2.7 %copy-start.6 = (bf16[208,128]{1,0:T(8,128)(2,1)}, bf16[208,128]{1,0:T(8,128)(2,1)S(1)}, u32[]{:S(2)}) copy-start(bf16[208,128]{1,0:T(8,128)(2,1)S(1)} %collective-permute-done.23.refs_7_) | copy-start | bytes 159748
  101.9 0.6 copy-start.7
  102.6 0.6 copy-start.8
Sparse Core Ops, SparseCore 0:
  10.3 22.8 all-gather.1

commit v6 on v5

--- a/solution.py
+++ b/solution.py
@@ -25,6 +25,8 @@
 F32 = jnp.float32
 BF16 = jnp.bfloat16
 VMEM_LIMIT = 60 * 1024 * 1024
+LAYER_LIMIT = 52 * 1024 * 1024
+UNPACK_LIMIT = 16 * 1024 * 1024
 FEW = 16
 
 
@@ -126,7 +128,9 @@
         gain_ref[lanes] = last[taps_ref.shape[0] : taps_ref.shape[0] + 1].reshape(128)
 
 
-def prep_kernel(pos_ref, hi_ref, lo_ref, back_ref, ahead_ref, behind_ref):
+def prep_kernel(take_ref, pos_ref, hi_ref, lo_ref, back_ref, column_ref, ahead_ref, behind_ref):
+    wide = jnp.broadcast_to(take_ref[...].astype(F32), (128, take_ref.shape[1]))
+    column_ref[...] = jnp.transpose(wide).astype(jnp.int32)
     f_hi = hi_ref[...]
     f_lo = lo_ref[...]
     back = back_ref[...]
@@ -441,7 +445,7 @@
         in_specs=[SCALARS] + vmem(len(pieces)),
         out_specs=vmem(3),
         scratch_shapes=[pltpu.VMEM((parts, part, 128), F32)],
-        compiler_params=pltpu.CompilerParams(vmem_limit_bytes=VMEM_LIMIT),
+        compiler_params=pltpu.CompilerParams(vmem_limit_bytes=UNPACK_LIMIT),
         cost_estimate=pl.CostEstimate(flops=10**6, bytes_accessed=12 * 10**5, transcendentals=0),
         name="unpack_gradients",
     )(ours, *pieces)
@@ -466,20 +470,21 @@
     return jnp.stack(lines)
 
 
-def prepare(utterances, f_hi, f_lo, back):
+def prepare(take, utterances, f_hi, f_lo, back):
     shapes = [
+        jax.ShapeDtypeStruct((take.shape[1], 128), jnp.int32),
         jax.ShapeDtypeStruct((POINTS, AHEAD_AT[-1]), BF16),
         jax.ShapeDtypeStruct((BEHIND_AT[-1], 3 * POINTS), BF16),
     ]
     return pl.pallas_call(
         prep_kernel,
         out_shape=shapes,
-        in_specs=vmem(4),
-        out_specs=vmem(2),
+        in_specs=vmem(5),
+        out_specs=vmem(3),
         compiler_params=pltpu.CompilerParams(vmem_limit_bytes=VMEM_LIMIT),
         cost_estimate=pl.CostEstimate(flops=3 * 10**9, bytes_accessed=8 * 10**6, transcendentals=0),
         name="prepare_transforms",
-    )(positions(utterances), f_hi, f_lo, back)
+    )(take, positions(utterances), f_hi, f_lo, back)
 
 
 def layer(
@@ -524,7 +529,7 @@
         in_specs=[SCALARS] * 3 + vmem(len(arrived) + 3) + [hbm] * 4,
         out_specs=vmem(3),
         scratch_shapes=scratch,
-        compiler_params=pltpu.CompilerParams(vmem_limit_bytes=VMEM_LIMIT),
+        compiler_params=pltpu.CompilerParams(vmem_limit_bytes=LAYER_LIMIT),
         cost_estimate=pl.CostEstimate(flops=10**10, bytes_accessed=16 * 10**6, transcendentals=10**6),
         name="layer_step",
     )(*ids, *arrived, take, tap_fwd, lags, params, upstream, ahead, behind)
@@ -558,8 +563,9 @@
         sent = outgoing[0].reshape(wanted.shape + outgoing[0].shape[1:])
         back_in = lax.all_to_all(sent, "dp", split_axis=0, concat_axis=0, tiled=True)
         arrived = [back_in.reshape(-1, back_in.shape[2])]
-    take = jnp.broadcast_to(jnp.repeat(take_own, 2)[:, None], (2 * take_own.shape[0], 128))
-    ahead, behind = prepare(jnp.repeat(utt_own, 2), f_hi, f_lo, back)
+    take, ahead, behind = prepare(
+        jnp.repeat(take_own, 2)[None, :], jnp.repeat(utt_own, 2), f_hi, f_lo, back
+    )
 
     depth, shard_cols = in_proj.shape
     held = depth + 32

time: 112 us -> 110 us (0.982)
  Pallas kernels: 29.8 us -> 28 us
  waiting for transfers between devices: 27 us -> 25.2 us
  starting transfers between devices: 35.2 us -> 36.4 us
    ppermute x21, waiting for transfers between devices: 17.1 us -> 15.3 us  [swap(): return lax.ppermute(value, 'dp', [(i, i ^ k) for i in range(dp)])]
    ppermute x21, starting transfers between devices: 33 us -> 34.2 us  [swap(): return lax.ppermute(value, 'dp', [(i, i ^ k) for i in range(dp)])]
  transfers between devices with their start and end apart: 25 -> 25, of which waited for: 11 -> 10; matrix products, arithmetic and copies ran while one was open for 3% -> 3% of each run, Pallas kernels for 5% -> 5%
where the time goes in v6:
time: 110 us
  starting transfers between devices  36.4 us (33%)
  Pallas kernels  28 us (25%)
  waiting for transfers between devices  25.2 us (23%)
  between operations  14.3 us (13%)
  local copies, waits for them, and re-layouts  3.21 us (3%)
  other arithmetic  2.51 us (2%)
    ppermute x21, starting transfers between devices, swap(): return lax.ppermute(value, 'dp', [(i, i ^ k) for i in range(dp)])  34.2 us
    pallas_call x1, Pallas kernels, layer(): pl.pallas_call(functools.partial(layer_kernel, len(arrived)), out_shape=[...  18.5 us
    ppermute x21, waiting for transfers between devices, swap(): return lax.ppermute(value, 'dp', [(i, i ^ k) for i in range(dp)])  15.3 us
    ppermute x2, waiting for transfers between devices, per_device(): far_in, near_in = [lax.ppermute(v, 'fsdp', across) for v in sent]  6.07 us
    pallas_call x1, Pallas kernels, prepare(): pl.pallas_call(prep_kernel, out_shape=shapes, in_specs=vmem(5), out_specs...  5.65 us
    ppermute x1, waiting for transfers between devices, per_device(): other = lax.ppermute(send, 'fsdp', [(i, i ^ 1) for i in range(fsdp)])  3.8 us
    pallas_call x1, Pallas kernels, pick(): pl.pallas_call(pick_kernel, out_shape=[jax.ShapeDtypeStruct((proj.shape[0...  2.93 us
  transfers between devices with their start and end apart: 25, of which 10 were waited for; matrix products, arithmetic and copies ran while one was open for 3% of the time, Pallas kernels for 5%

profile of v6, /device:TPU:0, one launch (start us, length us, event | category | flops | bytes accessed | tf_op | source)
XLA Modules:
  0.0 109.6 jit_solution(11558545994135680730)
XLA Ops:
  7.2 0.0 all-gather.2.cloned.1.call-start
  7.2 2.9 %pick_rows.1 = (bf16[544,384]{1,0:T(8,128)(2,1)}, bf16[64,1024]{1,0:T(8,128)(2,1)}, bf16[64,1024]{1,0:T(8,128)(2,1)}, bf16[64,1024]{1,0:T(8,128)(2,1)}, bf16[64,...) custom-call(s32[1,1]{1,0:T(1,128)} %bitcast.ours_ref, ...), custom_call_target="tpu_custom_call" | custom-call | flops 268435456 | bytes 1572864 | tf_op jit(solution)/shard_map/pick_rows/pallas_call | solution.py:423
  10.2 0.0 all-gather.2.cloned.1.call-update
  10.2 3.0 %collective-permute-start = (bf16[64,1024]{1,0:T(8,128)(2,1)}, bf16[64,1024]{1,0:T(8,128)(2,1)S(1)}, u32[]{:S(2)}, u32[]{:S(2)}) collective-permute-start(bf16[64,1024]{1,0:T(8,128)(2,1)} %get-tuple-element.42), channel_id=1, source_target_pairs={{0,4},{4,0},{8,12},{12,8},{16,20},{20,16},{24,28},{28,24},{1,5},{5... | collective-permute-start | bytes 393224 | tf_op jit(solution)/shard_map/ppermute | solution.py:555
  13.2 1.6 %collective-permute-start.1 = (bf16[64,1024]{1,0:T(8,128)(2,1)}, bf16[64,1024]{1,0:T(8,128)(2,1)S(1)}, u32[]{:S(2)}, u32[]{:S(2)}) collective-permute-start(bf16[64,1024]{1,0:T(8,128)(2,1)} %get-tuple-element.43), channel_id=1, source_target_pairs={{0,8},{4,12},{8,0},{12,4},{16,24},{20,28},{24,16},{28,20},{1,9},{5... | collective-permute-start | bytes 393224 | tf_op jit(solution)/shard_map/ppermute | solution.py:555
  14.8 0.0 collective-permute-start.2
  14.8 3.0 %collective-permute-start.3 = (bf16[64,1024]{1,0:T(8,128)(2,1)}, bf16[64,1024]{1,0:T(8,128)(2,1)S(1)}, u32[]{:S(2)}, u32[]{:S(2)}) collective-permute-start(bf16[64,1024]{1,0:T(8,128)(2,1)} %get-tuple-element.45), channel_id=1, source_target_pairs={{0,16},{4,20},{8,24},{12,28},{16,0},{20,4},{24,8},{28,12},{1,17},{... | collective-permute-start | bytes 393224 | tf_op jit(solution)/shard_map/ppermute | solution.py:555
  17.8 1.3 %collective-permute-start.4 = (bf16[64,1024]{1,0:T(8,128)(2,1)}, bf16[64,1024]{1,0:T(8,128)(2,1)S(1)}, u32[]{:S(2)}, u32[]{:S(2)}) collective-permute-start(bf16[64,1024]{1,0:T(8,128)(2,1)} %get-tuple-element.46), channel_id=1, source_target_pairs={{0,20},{4,16},{8,28},{12,24},{16,4},{20,0},{24,12},{28,8},{1,21},{... | collective-permute-start | bytes 393224 | tf_op jit(solution)/shard_map/ppermute | solution.py:555
  19.0 0.7 broadcast_multiply_fusion
  19.7 0.1 broadcast_in_dim.27
  19.8 0.1 mul.12
  20.0 0.1 slice.98
  20.1 0.1 slice.97
  20.1 0.1 slice.92
  20.2 0.1 slice.93
  20.3 0.1 slice.91
  20.4 0.1 slice.90
  20.4 0.1 pad_add_fusion.2
  20.5 0.1 pad_add_fusion
  20.6 0.1 pad_add_fusion.3
  20.7 0.1 pad_add_fusion.5
  20.8 0.1 pad_add_fusion.1
  20.9 0.1 broadcast_in_dim.26
  21.0 0.7 broadcast_in_dim_reshape.3.take_ref
  21.8 0.7 stack.31.pos_ref
  22.4 3.7 %collective-permute-start.5 = (bf16[64,1024]{1,0:T(8,128)(2,1)}, bf16[64,1024]{1,0:T(8,128)(2,1)S(1)}, u32[]{:S(2)}, u32[]{:S(2)}) collective-permute-start(bf16[64,1024]{1,0:T(8,128)(2,1)} %get-tuple-element.47), channel_id=1, source_target_pairs={{0,24},{4,28},{8,16},{12,20},{16,8},{20,12},{24,0},{28,4},{1,25},{... | collective-permute-start | bytes 393224 | tf_op jit(solution)/shard_map/ppermute | solution.py:555
  26.1 0.1 collective-permute-start.6
  26.2 5.6 %prepare_transforms.1 = (s32[512,128]{1,0:T(8,128)}, bf16[256,4480]{1,0:T(8,128)(2,1)}, bf16[1408,768]{1,0:T(8,128)(2,1)}) custom-call(s32[1,512]{1,0:T(1,128)} %broadcast_in_dim_reshape.3.take_ref, s32[8,896]{1,0:T(8,128)} %stack.31.pos_ref, bf16[256,256]{1,0:T(8,128)(2,1)} %constant.81.clone.hi_ref, bf16[256,256]{1,0:T(8,128)(2,1)} %constant.82.clone.lo_ref, ...), custom_call_target="tpu_custom_call" | custom-call | flops 3000000000 | bytes 8000000 | tf_op jit(solution)/shard_map/prepare_transforms/pallas_call | solution.py:479
  31.8 0.0 collective-permute-done.2.refs_3_
  31.8 0.0 collective-permute-done.3.refs_4_
  31.8 5.6 %collective-permute-done.4.refs_5_ = bf16[64,1024]{1,0:T(8,128)(2,1)S(1)} collective-permute-done((bf16[64,1024]{1,0:T(8,128)(2,1)}, bf16[64,1024]{1,0:T(8,128)(2,1)S(1)}, u32[]{:S(2)}, u32[]{:S(2)}) %collective-permute-start.4) | collective-permute-done | bytes 131104 | tf_op jit(solution)/shard_map/ppermute | solution.py:555
  37.4 0.0 collective-permute-done.5.refs_6_
  37.4 0.0 all-gather.2.cloned.1.call-done.refs_11_
  37.4 0.9 copy-done.3
  38.4 18.5 %layer_step.1 = (f32[2,8,208,128]{3,2,1,0:T(8,128)}, f32[2,8,208,128]{3,2,1,0:T(8,128)}, f32[1,1]{1,0:T(1,128)}) custom-call(s32[1,1]{1,0:T(1,128)} %bitcast.1.core_ref, s32[1,1]{1,0:T(1,128)} %bitcast.2.side_ref, s32[1,1]{1,0:T(1,128)} %bitcast.ours_ref, bf16[64,1024]{1,0:T(8,128)(2,1)S(1)} %copy-done.2, bf16[64,1024]{1,0:T(8,128)(2,1)S(1)} %collective-permute-done.refs_1_, ...), custom_call_target="tpu_custom_call" | custom-call | flops 10000000000 | bytes 16000000 | tf_op jit(solution)/shard_map/layer_step/pallas_call | solution.py:522
  56.9 0.1 collective-permute-start.7
  56.9 3.8 %collective-permute-done.7 = f32[2,8,208,128]{3,2,1,0:T(8,128)S(1)} collective-permute-done((f32[2,8,208,128]{3,2,1,0:T(8,128)}, f32[2,8,208,128]{3,2,1,0:T(8,128)S(1)}, u32[]{:S(2)}, u32[]{:S(2)}) %collective-permute-start.7) | collective-permute-done | bytes 1703968 | tf_op jit(solution)/shard_map/ppermute | solution.py:580
  60.7 1.2 %fusion.8 = (bf16[4,208,128]{2,1,0:T(8,128)(2,1)S(1)}, bf16[4,208,128]{2,1,0:T(8,128)(2,1)S(1)}) fusion(f32[2,8,208,128]{3,2,1,0:T(8,128)S(1)} %collective-permute-done.7, f32[2,8,208,128]{3,2,1,0:T(8,128)} %get-tuple-element.55), kind=kLoop, calls=%fused_computation.12 | loop fusion | flops 425984 | bytes 2129920 | tf_op jit(solution)/shard_map/convert_element_type | solution.py:584
  62.0 1.6 %collective-permute-start.9 = (bf16[4,208,128]{2,1,0:T(8,128)(2,1)S(1)}, bf16[4,208,128]{2,1,0:T(8,128)(2,1)S(1)}, u32[]{:S(2)}, u32[]{:S(2)}) collective-permute-start(bf16[4,208,128]{2,1,0:T(8,128)(2,1)S(1)} %get-tuple-element.64), channel_id=1, source_target_pairs={{0,2},{1,3},{2,0},{3,1},{4,6},{5,7},{6,4},{7,5},{8,10},{9,11},{10,... | collective-permute-start | bytes 638984 | tf_op jit(solution)/shard_map/ppermute | solution.py:585
  63.6 0.5 collective-permute-start.8
  64.0 6.1 %collective-permute-done.9 = bf16[4,208,128]{2,1,0:T(8,128)(2,1)S(1)} collective-permute-done((bf16[4,208,128]{2,1,0:T(8,128)(2,1)S(1)}, bf16[4,208,128]{2,1,0:T(8,128)(2,1)S(1)}, u32[]{:S(2)}, u32[]{:S(2)}) %collective-permute-start.9) | collective-permute-done | bytes 213024 | tf_op jit(solution)/shard_map/ppermute | solution.py:585
  70.1 0.1 fusion.3
  70.2 6.6 %collective-permute-start.13 = (bf16[208,128]{1,0:T(8,128)(2,1)S(1)}, bf16[208,128]{1,0:T(8,128)(2,1)S(1)}, u32[]{:S(2)}, u32[]{:S(2)}) collective-permute-start(bf16[208,128]{1,0:T(8,128)(2,1)S(1)} %get-tuple-element.69), channel_id=1, source_target_pairs={{0,16},{4,20},{8,24},{12,28},{16,0},{20,4},{24,8},{28,12},{1,17},{... | collective-permute-start | bytes 159752 | tf_op jit(solution)/shard_map/ppermute | solution.py:555
  76.9 0.7 collective-permute-start.16
  77.5 3.2 %collective-permute-start.15 = (bf16[208,128]{1,0:T(8,128)(2,1)S(1)}, bf16[208,128]{1,0:T(8,128)(2,1)S(1)}, u32[]{:S(2)}, u32[]{:S(2)}) collective-permute-start(bf16[208,128]{1,0:T(8,128)(2,1)S(1)} %get-tuple-element.71), channel_id=1, source_target_pairs={{0,24},{4,28},{8,16},{12,20},{16,8},{20,12},{24,0},{28,4},{1,25},{... | collective-permute-start | bytes 159752 | tf_op jit(solution)/shard_map/ppermute | solution.py:555
  80.7 0.1 fusion.21
  80.8 1.5 %collective-permute-start.10 = (bf16[208,128]{1,0:T(8,128)(2,1)S(1)}, bf16[208,128]{1,0:T(8,128)(2,1)S(1)}, u32[]{:S(2)}, u32[]{:S(2)}) collective-permute-start(bf16[208,128]{1,0:T(8,128)(2,1)S(1)} %get-tuple-element.66), channel_id=1, source_target_pairs={{0,4},{4,0},{8,12},{12,8},{16,20},{20,16},{24,28},{28,24},{1,5},{5... | collective-permute-start | bytes 159752 | tf_op jit(solution)/shard_map/ppermute | solution.py:555
  82.3 0.0 collective-permute-done.13
  82.3 2.3 %collective-permute-start.12 = (bf16[208,128]{1,0:T(8,128)(2,1)S(1)}, bf16[208,128]{1,0:T(8,128)(2,1)S(1)}, u32[]{:S(2)}, u32[]{:S(2)}) collective-permute-start(bf16[208,128]{1,0:T(8,128)(2,1)S(1)} %get-tuple-element.67), channel_id=1, source_target_pairs={{0,12},{4,8},{8,4},{12,0},{16,28},{20,24},{24,20},{28,16},{1,13},{... | collective-permute-start | bytes 159752 | tf_op jit(solution)/shard_map/ppermute | solution.py:555
  84.6 2.0 %collective-permute-done.14 = bf16[208,128]{1,0:T(8,128)(2,1)S(1)} collective-permute-done((bf16[208,128]{1,0:T(8,128)(2,1)S(1)}, bf16[208,128]{1,0:T(8,128)(2,1)S(1)}, u32[]{:S(2)}, u32[]{:S(2)}) %collective-permute-start.14) | collective-permute-done | bytes 53280 | tf_op jit(solution)/shard_map/ppermute | solution.py:555
  86.6 0.7 collective-permute-done.12
  87.3 1.4 %collective-permute-done.11 = bf16[208,128]{1,0:T(8,128)(2,1)S(1)} collective-permute-done((bf16[208,128]{1,0:T(8,128)(2,1)S(1)}, bf16[208,128]{1,0:T(8,128)(2,1)S(1)}, u32[]{:S(2)}, u32[]{:S(2)}) %collective-permute-start.11) | collective-permute-done | bytes 53280 | tf_op jit(solution)/shard_map/ppermute | solution.py:555
  88.7 0.1 fusion.16.refs_0_
  88.8 3.1 %collective-permute-start.22 = (bf16[208,128]{1,0:T(8,128)(2,1)S(1)}, bf16[208,128]{1,0:T(8,128)(2,1)S(1)}, u32[]{:S(2)}, u32[]{:S(2)}) collective-permute-start(bf16[208,128]{1,0:T(8,128)(2,1)S(1)} %fusion.16.refs_0_), channel_id=1, source_target_pairs={{0,24},{4,28},{8,16},{12,20},{16,8},{20,12},{24,0},{28,4},{1,25},{... | collective-permute-start | bytes 159752 | tf_op jit(solution)/shard_map/ppermute | solution.py:555
  91.9 1.4 %collective-permute-start.18 = (bf16[208,128]{1,0:T(8,128)(2,1)S(1)}, bf16[208,128]{1,0:T(8,128)(2,1)S(1)}, u32[]{:S(2)}, u32[]{:S(2)}) collective-permute-start(bf16[208,128]{1,0:T(8,128)(2,1)S(1)} %fusion.16.refs_0_), channel_id=1, source_target_pairs={{0,8},{4,12},{8,0},{12,4},{16,24},{20,28},{24,16},{28,20},{1,9},{5... | collective-permute-start | bytes 159752 | tf_op jit(solution)/shard_map/ppermute | solution.py:555
  93.3 0.4 collective-permute-start.17
  93.7 1.1 %collective-permute-done.22.refs_6_ = bf16[208,128]{1,0:T(8,128)(2,1)S(1)} collective-permute-done((bf16[208,128]{1,0:T(8,128)(2,1)S(1)}, bf16[208,128]{1,0:T(8,128)(2,1)S(1)}, u32[]{:S(2)}, u32[]{:S(2)}) %collective-permute-start.22) | collective-permute-done | bytes 53280 | tf_op jit(solution)/shard_map/ppermute | solution.py:555
  94.8 0.5 collective-permute-start.23
  95.3 1.8 %collective-permute-done.20.refs_4_ = bf16[208,128]{1,0:T(8,128)(2,1)S(1)} collective-permute-done((bf16[208,128]{1,0:T(8,128)(2,1)S(1)}, bf16[208,128]{1,0:T(8,128)(2,1)S(1)}, u32[]{:S(2)}, u32[]{:S(2)}) %collective-permute-start.20) | collective-permute-done | bytes 53280 | tf_op jit(solution)/shard_map/ppermute | solution.py:555
  97.1 0.4 collective-permute-start.21
  97.5 1.6 %collective-permute-start.19 = (bf16[208,128]{1,0:T(8,128)(2,1)S(1)}, bf16[208,128]{1,0:T(8,128)(2,1)S(1)}, u32[]{:S(2)}, u32[]{:S(2)}) collective-permute-start(bf16[208,128]{1,0:T(8,128)(2,1)S(1)} %collective-permute-done.18.refs_2_), channel_id=1, source_target_pairs={{0,4},{4,0},{8,12},{12,8},{16,20},{20,16},{24,28},{28,24},{1,5},{5... | collective-permute-start | bytes 159752 | tf_op jit(solution)/shard_map/ppermute | solution.py:555
  99.1 2.1 %collective-permute-done.21.refs_5_ = bf16[208,128]{1,0:T(8,128)(2,1)S(1)} collective-permute-done((bf16[208,128]{1,0:T(8,128)(2,1)S(1)}, bf16[208,128]{1,0:T(8,128)(2,1)S(1)}, u32[]{:S(2)}, u32[]{:S(2)}) %collective-permute-start.21) | collective-permute-done | bytes 53280 | tf_op jit(solution)/shard_map/ppermute | solution.py:555
  101.2 0.6 collective-permute-done.19.refs_3_
  101.8 1.0 unpack_gradients.1
  (45 shorter events, 0.2 us)
Async XLA Ops:
  7.2 13.8 %copy-start.5 = (s32[1,1,256]{2,1,0:T(1,128)S(1)}, s32[1,1,256]{2,1,0:T(1,128)}, u32[]{:S(2)}) copy-start(s32[1,1,256]{2,1,0:T(1,128)} %param.15) | copy-start | bytes 3076
  7.2 30.2 %all-gather.2.cloned.1.call-start = ((), (), s32[]{:S(2)}) async-start(), calls=%async_computation | async-start | bytes 2088960 | tf_op jit(solution)/shard_map/all_gather | solution.py:549
  10.2 12.3 %collective-permute-start = (bf16[64,1024]{1,0:T(8,128)(2,1)}, bf16[64,1024]{1,0:T(8,128)(2,1)S(1)}, u32[]{:S(2)}, u32[]{:S(2)}) collective-permute-start(bf16[64,1024]{1,0:T(8,128)(2,1)} %get-tuple-element.42), channel_id=1, source_target_pairs={{0,4},{4,0},{8,12},{12,8},{16,20},{20,16},{24,28},{28,24},{1,5},{5... | collective-permute-start | bytes 393224 | tf_op jit(solution)/shard_map/ppermute | solution.py:555
  13.2 12.9 %collective-permute-start.1 = (bf16[64,1024]{1,0:T(8,128)(2,1)}, bf16[64,1024]{1,0:T(8,128)(2,1)S(1)}, u32[]{:S(2)}, u32[]{:S(2)}) collective-permute-start(bf16[64,1024]{1,0:T(8,128)(2,1)} %get-tuple-element.43), channel_id=1, source_target_pairs={{0,8},{4,12},{8,0},{12,4},{16,24},{20,28},{24,16},{28,20},{1,9},{5... | collective-permute-start | bytes 393224 | tf_op jit(solution)/shard_map/ppermute | solution.py:555
  14.8 17.1 %collective-permute-start.2 = (bf16[64,1024]{1,0:T(8,128)(2,1)}, bf16[64,1024]{1,0:T(8,128)(2,1)S(1)}, u32[]{:S(2)}, u32[]{:S(2)}) collective-permute-start(bf16[64,1024]{1,0:T(8,128)(2,1)} %get-tuple-element.44), channel_id=1, source_target_pairs={{0,12},{4,8},{8,4},{12,0},{16,28},{20,24},{24,20},{28,16},{1,13},{... | collective-permute-start | bytes 393224 | tf_op jit(solution)/shard_map/ppermute | solution.py:555
  14.8 17.1 %collective-permute-start.3 = (bf16[64,1024]{1,0:T(8,128)(2,1)}, bf16[64,1024]{1,0:T(8,128)(2,1)S(1)}, u32[]{:S(2)}, u32[]{:S(2)}) collective-permute-start(bf16[64,1024]{1,0:T(8,128)(2,1)} %get-tuple-element.45), channel_id=1, source_target_pairs={{0,16},{4,20},{8,24},{12,28},{16,0},{20,4},{24,8},{28,12},{1,17},{... | collective-permute-start | bytes 393224 | tf_op jit(solution)/shard_map/ppermute | solution.py:555
  17.8 19.6 %collective-permute-start.4 = (bf16[64,1024]{1,0:T(8,128)(2,1)}, bf16[64,1024]{1,0:T(8,128)(2,1)S(1)}, u32[]{:S(2)}, u32[]{:S(2)}) collective-permute-start(bf16[64,1024]{1,0:T(8,128)(2,1)} %get-tuple-element.46), channel_id=1, source_target_pairs={{0,20},{4,16},{8,28},{12,24},{16,4},{20,0},{24,12},{28,8},{1,21},{... | collective-permute-start | bytes 393224 | tf_op jit(solution)/shard_map/ppermute | solution.py:555
  22.4 15.0 %copy-start = (bf16[256,64]{1,0:T(8,128)(2,1)S(1)}, bf16[256,64]{1,0:T(8,128)(2,1)}, u32[]{:S(2)}) copy-start(bf16[256,64]{1,0:T(8,128)(2,1)} %constant.84.clone.refs_9_) | copy-start | bytes 98308
  22.4 15.0 %copy-start.1 = (bf16[32,768]{1,0:T(8,128)(2,1)S(1)}, bf16[32,768]{1,0:T(8,128)(2,1)}, u32[]{:S(2)}) copy-start(bf16[32,768]{1,0:T(8,128)(2,1)} %constant.85.clone.refs_10_) | copy-start | bytes 147460
  22.4 15.0 %copy-start.2 = (bf16[64,1024]{1,0:T(8,128)(2,1)S(1)}, bf16[64,1024]{1,0:T(8,128)(2,1)}, u32[]{:S(2)}) copy-start(bf16[64,1024]{1,0:T(8,128)(2,1)} %get-tuple-element.41.refs_0_) | copy-start | bytes 393220
  22.4 14.9 %collective-permute-start.5 = (bf16[64,1024]{1,0:T(8,128)(2,1)}, bf16[64,1024]{1,0:T(8,128)(2,1)S(1)}, u32[]{:S(2)}, u32[]{:S(2)}) collective-permute-start(bf16[64,1024]{1,0:T(8,128)(2,1)} %get-tuple-element.47), channel_id=1, source_target_pairs={{0,24},{4,28},{8,16},{12,20},{16,8},{20,12},{24,0},{28,4},{1,25},{... | collective-permute-start | bytes 393224 | tf_op jit(solution)/shard_map/ppermute | solution.py:555
  26.1 11.3 %collective-permute-start.6 = (bf16[64,1024]{1,0:T(8,128)(2,1)}, bf16[64,1024]{1,0:T(8,128)(2,1)S(1)}, u32[]{:S(2)}, u32[]{:S(2)}) collective-permute-start(bf16[64,1024]{1,0:T(8,128)(2,1)} %get-tuple-element.48), channel_id=1, source_target_pairs={{0,28},{4,24},{8,20},{12,16},{16,12},{20,8},{24,4},{28,0},{1,29},{... | collective-permute-start | bytes 393224 | tf_op jit(solution)/shard_map/ppermute | solution.py:555
  37.4 1.0 copy-start.3
  56.8 13.3 %copy-start.4 = (f32[2,8,208,128]{3,2,1,0:T(8,128)S(1)}, f32[2,8,208,128]{3,2,1,0:T(8,128)}, u32[]{:S(2)}) copy-start(f32[2,8,208,128]{3,2,1,0:T(8,128)} %get-tuple-element.55) | copy-start | bytes 5111812
  56.9 3.9 %collective-permute-start.7 = (f32[2,8,208,128]{3,2,1,0:T(8,128)}, f32[2,8,208,128]{3,2,1,0:T(8,128)S(1)}, u32[]{:S(2)}, u32[]{:S(2)}) collective-permute-start(f32[2,8,208,128]{3,2,1,0:T(8,128)} %get-tuple-element.56), channel_id=1, source_target_pairs={{0,1},{1,0},{2,3},{3,2},{4,5},{5,4},{6,7},{7,6},{8,9},{9,8},{10,11... | collective-permute-start | bytes 5111816 | tf_op jit(solution)/shard_map/ppermute | solution.py:580
  62.0 8.2 %collective-permute-start.9 = (bf16[4,208,128]{2,1,0:T(8,128)(2,1)S(1)}, bf16[4,208,128]{2,1,0:T(8,128)(2,1)S(1)}, u32[]{:S(2)}, u32[]{:S(2)}) collective-permute-start(bf16[4,208,128]{2,1,0:T(8,128)(2,1)S(1)} %get-tuple-element.64), channel_id=1, source_target_pairs={{0,2},{1,3},{2,0},{3,1},{4,6},{5,7},{6,4},{7,5},{8,10},{9,11},{10,... | collective-permute-start | bytes 638984 | tf_op jit(solution)/shard_map/ppermute | solution.py:585
  63.6 17.1 %collective-permute-start.8 = (bf16[4,208,128]{2,1,0:T(8,128)(2,1)S(1)}, bf16[4,208,128]{2,1,0:T(8,128)(2,1)S(1)}, u32[]{:S(2)}, u32[]{:S(2)}) collective-permute-start(bf16[4,208,128]{2,1,0:T(8,128)(2,1)S(1)} %get-tuple-element.65), channel_id=1, source_target_pairs={{0,2},{1,3},{2,0},{3,1},{4,6},{5,7},{6,4},{7,5},{8,10},{9,11},{10,... | collective-permute-start | bytes 638984 | tf_op jit(solution)/shard_map/ppermute | solution.py:585
  70.2 12.1 %collective-permute-start.13 = (bf16[208,128]{1,0:T(8,128)(2,1)S(1)}, bf16[208,128]{1,0:T(8,128)(2,1)S(1)}, u32[]{:S(2)}, u32[]{:S(2)}) collective-permute-start(bf16[208,128]{1,0:T(8,128)(2,1)S(1)} %get-tuple-element.69), channel_id=1, source_target_pairs={{0,16},{4,20},{8,24},{12,28},{16,0},{20,4},{24,8},{28,12},{1,17},{... | collective-permute-start | bytes 159752 | tf_op jit(solution)/shard_map/ppermute | solution.py:555
  76.9 7.8 %collective-permute-start.16 = (bf16[208,128]{1,0:T(8,128)(2,1)S(1)}, bf16[208,128]{1,0:T(8,128)(2,1)S(1)}, u32[]{:S(2)}, u32[]{:S(2)}) collective-permute-start(bf16[208,128]{1,0:T(8,128)(2,1)S(1)} %get-tuple-element.70), channel_id=1, source_target_pairs={{0,28},{4,24},{8,20},{12,16},{16,12},{20,8},{24,4},{28,0},{1,29},{... | collective-permute-start | bytes 159752 | tf_op jit(solution)/shard_map/ppermute | solution.py:555
  77.5 7.1 %collective-permute-start.15 = (bf16[208,128]{1,0:T(8,128)(2,1)S(1)}, bf16[208,128]{1,0:T(8,128)(2,1)S(1)}, u32[]{:S(2)}, u32[]{:S(2)}) collective-permute-start(bf16[208,128]{1,0:T(8,128)(2,1)S(1)} %get-tuple-element.71), channel_id=1, source_target_pairs={{0,24},{4,28},{8,16},{12,20},{16,8},{20,12},{24,0},{28,4},{1,25},{... | collective-permute-start | bytes 159752 | tf_op jit(solution)/shard_map/ppermute | solution.py:555
  80.7 5.9 %collective-permute-start.14 = (bf16[208,128]{1,0:T(8,128)(2,1)S(1)}, bf16[208,128]{1,0:T(8,128)(2,1)S(1)}, u32[]{:S(2)}, u32[]{:S(2)}) collective-permute-start(bf16[208,128]{1,0:T(8,128)(2,1)S(1)} %get-tuple-element.72), channel_id=1, source_target_pairs={{0,20},{4,16},{8,28},{12,24},{16,4},{20,0},{24,12},{28,8},{1,21},{... | collective-permute-start | bytes 159752 | tf_op jit(solution)/shard_map/ppermute | solution.py:555
  80.8 5.8 %collective-permute-start.10 = (bf16[208,128]{1,0:T(8,128)(2,1)S(1)}, bf16[208,128]{1,0:T(8,128)(2,1)S(1)}, u32[]{:S(2)}, u32[]{:S(2)}) collective-permute-start(bf16[208,128]{1,0:T(8,128)(2,1)S(1)} %get-tuple-element.66), channel_id=1, source_target_pairs={{0,4},{4,0},{8,12},{12,8},{16,20},{20,16},{24,28},{28,24},{1,5},{5... | collective-permute-start | bytes 159752 | tf_op jit(solution)/shard_map/ppermute | solution.py:555
  82.3 5.0 %collective-permute-start.12 = (bf16[208,128]{1,0:T(8,128)(2,1)S(1)}, bf16[208,128]{1,0:T(8,128)(2,1)S(1)}, u32[]{:S(2)}, u32[]{:S(2)}) collective-permute-start(bf16[208,128]{1,0:T(8,128)(2,1)S(1)} %get-tuple-element.67), channel_id=1, source_target_pairs={{0,12},{4,8},{8,4},{12,0},{16,28},{20,24},{24,20},{28,16},{1,13},{... | collective-permute-start | bytes 159752 | tf_op jit(solution)/shard_map/ppermute | solution.py:555
  84.6 4.1 %collective-permute-start.11 = (bf16[208,128]{1,0:T(8,128)(2,1)S(1)}, bf16[208,128]{1,0:T(8,128)(2,1)S(1)}, u32[]{:S(2)}, u32[]{:S(2)}) collective-permute-start(bf16[208,128]{1,0:T(8,128)(2,1)S(1)} %get-tuple-element.68), channel_id=1, source_target_pairs={{0,8},{4,12},{8,0},{12,4},{16,24},{20,28},{24,16},{28,20},{1,9},{5... | collective-permute-start | bytes 159752 | tf_op jit(solution)/shard_map/ppermute | solution.py:555
  88.8 6.0 %collective-permute-start.22 = (bf16[208,128]{1,0:T(8,128)(2,1)S(1)}, bf16[208,128]{1,0:T(8,128)(2,1)S(1)}, u32[]{:S(2)}, u32[]{:S(2)}) collective-permute-start(bf16[208,128]{1,0:T(8,128)(2,1)S(1)} %fusion.16.refs_0_), channel_id=1, source_target_pairs={{0,24},{4,28},{8,16},{12,20},{16,8},{20,12},{24,0},{28,4},{1,25},{... | collective-permute-start | bytes 159752 | tf_op jit(solution)/shard_map/ppermute | solution.py:555
  91.9 5.2 %collective-permute-start.20 = (bf16[208,128]{1,0:T(8,128)(2,1)S(1)}, bf16[208,128]{1,0:T(8,128)(2,1)S(1)}, u32[]{:S(2)}, u32[]{:S(2)}) collective-permute-start(bf16[208,128]{1,0:T(8,128)(2,1)S(1)} %fusion.16.refs_0_), channel_id=1, source_target_pairs={{0,16},{4,20},{8,24},{12,28},{16,0},{20,4},{24,8},{28,12},{1,17},{... | collective-permute-start | bytes 159752 | tf_op jit(solution)/shard_map/ppermute | solution.py:555
  91.9 5.6 %collective-permute-start.18 = (bf16[208,128]{1,0:T(8,128)(2,1)S(1)}, bf16[208,128]{1,0:T(8,128)(2,1)S(1)}, u32[]{:S(2)}, u32[]{:S(2)}) collective-permute-start(bf16[208,128]{1,0:T(8,128)(2,1)S(1)} %fusion.16.refs_0_), channel_id=1, source_target_pairs={{0,8},{4,12},{8,0},{12,4},{16,24},{20,28},{24,16},{28,20},{1,9},{5... | collective-permute-start | bytes 159752 | tf_op jit(solution)/shard_map/ppermute | solution.py:555
  93.3 5.9 %collective-permute-start.17 = (bf16[208,128]{1,0:T(8,128)(2,1)S(1)}, bf16[208,128]{1,0:T(8,128)(2,1)S(1)}, u32[]{:S(2)}, u32[]{:S(2)}) collective-permute-start(bf16[208,128]{1,0:T(8,128)(2,1)S(1)} %fusion.16.refs_0_), channel_id=1, source_target_pairs={{0,4},{4,0},{8,12},{12,8},{16,20},{20,16},{24,28},{28,24},{1,5},{5... | collective-permute-start | bytes 159752 | tf_op jit(solution)/shard_map/ppermute | solution.py:555
  94.8 4.3 %collective-permute-start.23 = (bf16[208,128]{1,0:T(8,128)(2,1)S(1)}, bf16[208,128]{1,0:T(8,128)(2,1)S(1)}, u32[]{:S(2)}, u32[]{:S(2)}) collective-permute-start(bf16[208,128]{1,0:T(8,128)(2,1)S(1)} %collective-permute-done.22.refs_6_), channel_id=1, source_target_pairs={{0,4},{4,0},{8,12},{12,8},{16,20},{20,16},{24,28},{28,24},{1,5},{5... | collective-permute-start | bytes 159752 | tf_op jit(solution)/shard_map/ppermute | solution.py:555
  97.1 4.1 %collective-permute-start.21 = (bf16[208,128]{1,0:T(8,128)(2,1)S(1)}, bf16[208,128]{1,0:T(8,128)(2,1)S(1)}, u32[]{:S(2)}, u32[]{:S(2)}) collective-permute-start(bf16[208,128]{1,0:T(8,128)(2,1)S(1)} %collective-permute-done.20.refs_4_), channel_id=1, source_target_pairs={{0,4},{4,0},{8,12},{12,8},{16,20},{20,16},{24,28},{28,24},{1,5},{5... | collective-permute-start | bytes 159752 | tf_op jit(solution)/shard_map/ppermute | solution.py:555
  97.5 4.3 %collective-permute-start.19 = (bf16[208,128]{1,0:T(8,128)(2,1)S(1)}, bf16[208,128]{1,0:T(8,128)(2,1)S(1)}, u32[]{:S(2)}, u32[]{:S(2)}) collective-permute-start(bf16[208,128]{1,0:T(8,128)(2,1)S(1)} %collective-permute-done.18.refs_2_), channel_id=1, source_target_pairs={{0,4},{4,0},{8,12},{12,8},{16,20},{20,16},{24,28},{28,24},{1,5},{5... | collective-permute-start | bytes 159752 | tf_op jit(solution)/shard_map/ppermute | solution.py:555
Sparse Core Ops, SparseCore 0:
  10.3 22.8 all-gather.1

commit v7 on v6

--- a/solution.py
+++ b/solution.py
@@ -522,8 +522,8 @@
     return pl.pallas_call(
         functools.partial(layer_kernel, len(arrived)),
         out_shape=[
-            jax.ShapeDtypeStruct((halves, parts, part, 128), F32),
-            jax.ShapeDtypeStruct((halves, parts, part, 128), F32),
+            pltpu.VMEM((halves, parts, part, 128), F32),
+            pltpu.VMEM((halves, parts, part, 128), F32),
             jax.ShapeDtypeStruct((1, 1), F32),
         ],
         in_specs=[SCALARS] * 3 + vmem(len(arrived) + 3) + [hbm] * 4,
@@ -582,10 +582,11 @@
     across = [(i, i ^ 2) for i in range(fsdp)]
     spans = ((half, dp), (0, half))
     sent = [(keep[1, low:high] + other[1, low:high]).astype(BF16) for low, high in spans]
-    far_in, near_in = [lax.ppermute(v, "fsdp", across) for v in sent]
+    far_in = lax.ppermute(sent[0], "fsdp", across)
     far_sum = keep[0, half:] + other[0, half:] + far_in.astype(F32)
     far_out = far_sum.astype(BF16)
-    near_in, _ = lax.optimization_barrier((near_in, far_out))
+    near_sent, _ = lax.optimization_barrier((sent[1], far_out))
+    near_in = lax.ppermute(near_sent, "fsdp", across)
     near_sum = keep[0, :half] + other[0, :half] + near_in.astype(F32)
     near_out = near_sum.astype(BF16)
     if few:

time: 110 us -> 108 us (0.982)
  starting transfers between devices: 36.4 us -> 37.6 us
  other arithmetic: 2.51 us -> 1.38 us
    convert_element_type x1, other arithmetic: 1.22 us -> 0.09 us  [per_device(): (keep[1, low:high] + other[1, low:high]).astype(BF16)]
    ppermute x2, starting transfers between devices: 2.09 us -> 3.2 us  [the longest x1 1.6 us: per_device(): far_in = lax.ppermute(sent[0], 'fsdp', across)]
where the time goes in v7:
time: 108 us
  starting transfers between devices  37.6 us (35%)
  Pallas kernels  27.5 us (25%)
  waiting for transfers between devices  24.3 us (22%)
  between operations  14.3 us (13%)
  local copies, waits for them, and re-layouts  2.94 us (3%)
  other arithmetic  1.38 us (1%)
    ppermute x21, starting transfers between devices, swap(): return lax.ppermute(value, 'dp', [(i, i ^ k) for i in range(dp)])  34.3 us
    pallas_call x1, Pallas kernels, layer(): pl.pallas_call(functools.partial(layer_kernel, len(arrived)), out_shape=[...  17.9 us
    ppermute x21, waiting for transfers between devices, swap(): return lax.ppermute(value, 'dp', [(i, i ^ k) for i in range(dp)])  15 us
    ppermute x1, waiting for transfers between devices, per_device(): far_in = lax.ppermute(sent[0], 'fsdp', across)  5.76 us
    pallas_call x1, Pallas kernels, prepare(): pl.pallas_call(prep_kernel, out_shape=shapes, in_specs=vmem(5), out_specs...  5.69 us
    ppermute x1, waiting for transfers between devices, per_device(): other = lax.ppermute(send, 'fsdp', [(i, i ^ 1) for i in range(fsdp)])  3.58 us
    pallas_call x1, Pallas kernels, pick(): pl.pallas_call(pick_kernel, out_shape=[jax.ShapeDtypeStruct((proj.shape[0...  2.92 us
  transfers between devices with their start and end apart: 25, of which 10 were waited for; matrix products, arithmetic and copies ran while one was open for 3% of the time, Pallas kernels for 5%

profile of v7, /device:TPU:0, one launch (start us, length us, event | category | flops | bytes accessed | tf_op | source)
XLA Modules:
  0.0 108.0 jit_solution(7724954688185582494)
XLA Ops:
  7.2 0.0 all-gather.2.cloned.1.call-start
  7.2 2.9 %pick_rows.1 = (bf16[544,384]{1,0:T(8,128)(2,1)}, bf16[64,1024]{1,0:T(8,128)(2,1)}, bf16[64,1024]{1,0:T(8,128)(2,1)}, bf16[64,1024]{1,0:T(8,128)(2,1)}, bf16[64,...) custom-call(s32[1,1]{1,0:T(1,128)} %bitcast.ours_ref, ...), custom_call_target="tpu_custom_call" | custom-call | flops 268435456 | bytes 1572864 | tf_op jit(solution)/shard_map/pick_rows/pallas_call | solution.py:423
  10.1 0.0 all-gather.2.cloned.1.call-update
  10.2 3.0 %collective-permute-start = (bf16[64,1024]{1,0:T(8,128)(2,1)}, bf16[64,1024]{1,0:T(8,128)(2,1)S(1)}, u32[]{:S(2)}, u32[]{:S(2)}) collective-permute-start(bf16[64,1024]{1,0:T(8,128)(2,1)} %get-tuple-element.42), channel_id=1, source_target_pairs={{0,4},{4,0},{8,12},{12,8},{16,20},{20,16},{24,28},{28,24},{1,5},{5... | collective-permute-start | bytes 393224 | tf_op jit(solution)/shard_map/ppermute | solution.py:555
  13.2 1.6 %collective-permute-start.1 = (bf16[64,1024]{1,0:T(8,128)(2,1)}, bf16[64,1024]{1,0:T(8,128)(2,1)S(1)}, u32[]{:S(2)}, u32[]{:S(2)}) collective-permute-start(bf16[64,1024]{1,0:T(8,128)(2,1)} %get-tuple-element.43), channel_id=1, source_target_pairs={{0,8},{4,12},{8,0},{12,4},{16,24},{20,28},{24,16},{28,20},{1,9},{5... | collective-permute-start | bytes 393224 | tf_op jit(solution)/shard_map/ppermute | solution.py:555
  14.8 3.0 %collective-permute-start.3 = (bf16[64,1024]{1,0:T(8,128)(2,1)}, bf16[64,1024]{1,0:T(8,128)(2,1)S(1)}, u32[]{:S(2)}, u32[]{:S(2)}) collective-permute-start(bf16[64,1024]{1,0:T(8,128)(2,1)} %get-tuple-element.45), channel_id=1, source_target_pairs={{0,16},{4,20},{8,24},{12,28},{16,0},{20,4},{24,8},{28,12},{1,17},{... | collective-permute-start | bytes 393224 | tf_op jit(solution)/shard_map/ppermute | solution.py:555
  17.8 1.3 %collective-permute-start.4 = (bf16[64,1024]{1,0:T(8,128)(2,1)}, bf16[64,1024]{1,0:T(8,128)(2,1)S(1)}, u32[]{:S(2)}, u32[]{:S(2)}) collective-permute-start(bf16[64,1024]{1,0:T(8,128)(2,1)} %get-tuple-element.46), channel_id=1, source_target_pairs={{0,20},{4,16},{8,28},{12,24},{16,4},{20,0},{24,12},{28,8},{1,21},{... | collective-permute-start | bytes 393224 | tf_op jit(solution)/shard_map/ppermute | solution.py:555
  19.0 0.7 broadcast_multiply_fusion
  19.7 0.1 broadcast_in_dim.27
  19.8 0.1 mul.12
  20.0 0.1 slice.98
  20.0 0.1 slice.97
  20.1 0.1 slice.92
  20.2 0.1 slice.93
  20.3 0.1 slice.91
  20.3 0.1 slice.90
  20.4 0.1 pad_add_fusion.2
  20.5 0.1 pad_add_fusion
  20.6 0.1 pad_add_fusion.3
  20.7 0.1 pad_add_fusion.5
  20.8 0.1 pad_add_fusion.1
  20.9 0.1 broadcast_in_dim.26
  21.0 0.7 broadcast_in_dim_reshape.3.take_ref
  21.8 0.7 stack.31.pos_ref
  22.4 0.0 collective-permute-done.refs_1_
  22.4 3.6 %collective-permute-start.5 = (bf16[64,1024]{1,0:T(8,128)(2,1)}, bf16[64,1024]{1,0:T(8,128)(2,1)S(1)}, u32[]{:S(2)}, u32[]{:S(2)}) collective-permute-start(bf16[64,1024]{1,0:T(8,128)(2,1)} %get-tuple-element.47), channel_id=1, source_target_pairs={{0,24},{4,28},{8,16},{12,20},{16,8},{20,12},{24,0},{28,4},{1,25},{... | collective-permute-start | bytes 393224 | tf_op jit(solution)/shard_map/ppermute | solution.py:555
  26.0 0.0 collective-permute-done.1.refs_2_
  26.0 0.1 collective-permute-start.6
  26.1 5.7 %prepare_transforms.1 = (s32[512,128]{1,0:T(8,128)}, bf16[256,4480]{1,0:T(8,128)(2,1)}, bf16[1408,768]{1,0:T(8,128)(2,1)}) custom-call(s32[1,512]{1,0:T(1,128)} %broadcast_in_dim_reshape.3.take_ref, s32[8,896]{1,0:T(8,128)} %stack.31.pos_ref, bf16[256,256]{1,0:T(8,128)(2,1)} %constant.81.clone.hi_ref, bf16[256,256]{1,0:T(8,128)(2,1)} %constant.82.clone.lo_ref, ...), custom_call_target="tpu_custom_call" | custom-call | flops 3000000000 | bytes 8000000 | tf_op jit(solution)/shard_map/prepare_transforms/pallas_call | solution.py:479
  31.8 5.5 %collective-permute-done.4.refs_5_ = bf16[64,1024]{1,0:T(8,128)(2,1)S(1)} collective-permute-done((bf16[64,1024]{1,0:T(8,128)(2,1)}, bf16[64,1024]{1,0:T(8,128)(2,1)S(1)}, u32[]{:S(2)}, u32[]{:S(2)}) %collective-permute-start.4) | collective-permute-done | bytes 131104 | tf_op jit(solution)/shard_map/ppermute | solution.py:555
  37.4 0.0 all-gather.2.cloned.1.call-done.refs_11_
  37.4 0.6 copy-done.5
  38.0 0.0 copy-done.6
  38.1 0.1 copy-done.7
  38.1 17.9 %layer_step.1 = (f32[2,8,208,128]{3,2,1,0:T(8,128)S(1)}, f32[2,8,208,128]{3,2,1,0:T(8,128)S(1)}, f32[1,1]{1,0:T(1,128)}) custom-call(s32[1,1]{1,0:T(1,128)} %bitcast.1.core_ref, s32[1,1]{1,0:T(1,128)} %bitcast.2.side_ref, s32[1,1]{1,0:T(1,128)} %bitcast.ours_ref, bf16[64,1024]{1,0:T(8,128)(2,1)} %get-tuple-element.41.refs_0_, bf16[64,1024]{1,0:T(8,128)(2,1)} %copy-done.1, ...), custom_call_target="tpu_custom_call" | custom-call | flops 10000000000 | bytes 16000000 | tf_op jit(solution)/shard_map/layer_step/pallas_call | solution.py:522
  56.0 0.1 collective-permute-start.7
  56.1 3.6 %collective-permute-done.7 = f32[2,8,208,128]{3,2,1,0:T(8,128)S(1)} collective-permute-done((f32[2,8,208,128]{3,2,1,0:T(8,128)S(1)}, f32[2,8,208,128]{3,2,1,0:T(8,128)S(1)}, u32[]{:S(2)}, u32[]{:S(2)}) %collective-permute-start.7) | collective-permute-done | bytes 1703968 | tf_op jit(solution)/shard_map/ppermute | solution.py:580
  59.7 0.1 fusion.8
  59.8 1.6 %collective-permute-start.8 = (bf16[4,208,128]{2,1,0:T(8,128)(2,1)S(1)}, bf16[4,208,128]{2,1,0:T(8,128)(2,1)S(1)}, u32[]{:S(2)}, u32[]{:S(2)}) collective-permute-start(bf16[4,208,128]{2,1,0:T(8,128)(2,1)S(1)} %get-tuple-element.64), channel_id=1, source_target_pairs={{0,2},{1,3},{2,0},{3,1},{4,6},{5,7},{6,4},{7,5},{8,10},{9,11},{10,... | collective-permute-start | bytes 638984 | tf_op jit(solution)/shard_map/ppermute | solution.py:585
  61.4 5.8 %collective-permute-done.8 = bf16[4,208,128]{2,1,0:T(8,128)(2,1)S(1)} collective-permute-done((bf16[4,208,128]{2,1,0:T(8,128)(2,1)S(1)}, bf16[4,208,128]{2,1,0:T(8,128)(2,1)S(1)}, u32[]{:S(2)}, u32[]{:S(2)}) %collective-permute-start.8) | collective-permute-done | bytes 213024 | tf_op jit(solution)/shard_map/ppermute | solution.py:585
  67.1 0.1 fusion.3
  67.2 1.6 %collective-permute-start.9 = (bf16[4,208,128]{2,1,0:T(8,128)(2,1)S(1)}, bf16[4,208,128]{2,1,0:T(8,128)(2,1)S(1)}, u32[]{:S(2)}, u32[]{:S(2)}) collective-permute-start(bf16[4,208,128]{2,1,0:T(8,128)(2,1)S(1)} %get-tuple-element.57), channel_id=1, source_target_pairs={{0,2},{1,3},{2,0},{3,1},{4,6},{5,7},{6,4},{7,5},{8,10},{9,11},{10,... | collective-permute-start | bytes 638984 | tf_op jit(solution)/shard_map/ppermute | solution.py:589
  68.8 6.6 %collective-permute-start.13 = (bf16[208,128]{1,0:T(8,128)(2,1)S(1)}, bf16[208,128]{1,0:T(8,128)(2,1)S(1)}, u32[]{:S(2)}, u32[]{:S(2)}) collective-permute-start(bf16[208,128]{1,0:T(8,128)(2,1)S(1)} %get-tuple-element.69), channel_id=1, source_target_pairs={{0,16},{4,20},{8,24},{12,28},{16,0},{20,4},{24,8},{28,12},{1,17},{... | collective-permute-start | bytes 159752 | tf_op jit(solution)/shard_map/ppermute | solution.py:555
  75.4 0.8 collective-permute-start.16
  76.2 3.0 %collective-permute-start.15 = (bf16[208,128]{1,0:T(8,128)(2,1)S(1)}, bf16[208,128]{1,0:T(8,128)(2,1)S(1)}, u32[]{:S(2)}, u32[]{:S(2)}) collective-permute-start(bf16[208,128]{1,0:T(8,128)(2,1)S(1)} %get-tuple-element.71), channel_id=1, source_target_pairs={{0,24},{4,28},{8,16},{12,20},{16,8},{20,12},{24,0},{28,4},{1,25},{... | collective-permute-start | bytes 159752 | tf_op jit(solution)/shard_map/ppermute | solution.py:555
  79.3 0.1 fusion.21
  79.4 1.5 %collective-permute-start.10 = (bf16[208,128]{1,0:T(8,128)(2,1)S(1)}, bf16[208,128]{1,0:T(8,128)(2,1)S(1)}, u32[]{:S(2)}, u32[]{:S(2)}) collective-permute-start(bf16[208,128]{1,0:T(8,128)(2,1)S(1)} %get-tuple-element.66), channel_id=1, source_target_pairs={{0,4},{4,0},{8,12},{12,8},{16,20},{20,16},{24,28},{28,24},{1,5},{5... | collective-permute-start | bytes 159752 | tf_op jit(solution)/shard_map/ppermute | solution.py:555
  80.9 2.3 %collective-permute-start.12 = (bf16[208,128]{1,0:T(8,128)(2,1)S(1)}, bf16[208,128]{1,0:T(8,128)(2,1)S(1)}, u32[]{:S(2)}, u32[]{:S(2)}) collective-permute-start(bf16[208,128]{1,0:T(8,128)(2,1)S(1)} %get-tuple-element.67), channel_id=1, source_target_pairs={{0,12},{4,8},{8,4},{12,0},{16,28},{20,24},{24,20},{28,16},{1,13},{... | collective-permute-start | bytes 159752 | tf_op jit(solution)/shard_map/ppermute | solution.py:555
  83.2 2.0 %collective-permute-done.14 = bf16[208,128]{1,0:T(8,128)(2,1)S(1)} collective-permute-done((bf16[208,128]{1,0:T(8,128)(2,1)S(1)}, bf16[208,128]{1,0:T(8,128)(2,1)S(1)}, u32[]{:S(2)}, u32[]{:S(2)}) %collective-permute-start.14) | collective-permute-done | bytes 53280 | tf_op jit(solution)/shard_map/ppermute | solution.py:555
  85.2 0.7 collective-permute-done.12
  85.9 1.4 %collective-permute-done.11 = bf16[208,128]{1,0:T(8,128)(2,1)S(1)} collective-permute-done((bf16[208,128]{1,0:T(8,128)(2,1)S(1)}, bf16[208,128]{1,0:T(8,128)(2,1)S(1)}, u32[]{:S(2)}, u32[]{:S(2)}) %collective-permute-start.11) | collective-permute-done | bytes 53280 | tf_op jit(solution)/shard_map/ppermute | solution.py:555
  87.3 0.1 fusion.16.refs_0_
  87.4 3.0 %collective-permute-start.22 = (bf16[208,128]{1,0:T(8,128)(2,1)S(1)}, bf16[208,128]{1,0:T(8,128)(2,1)S(1)}, u32[]{:S(2)}, u32[]{:S(2)}) collective-permute-start(bf16[208,128]{1,0:T(8,128)(2,1)S(1)} %fusion.16.refs_0_), channel_id=1, source_target_pairs={{0,24},{4,28},{8,16},{12,20},{16,8},{20,12},{24,0},{28,4},{1,25},{... | collective-permute-start | bytes 159752 | tf_op jit(solution)/shard_map/ppermute | solution.py:555
  90.4 1.4 %collective-permute-start.18 = (bf16[208,128]{1,0:T(8,128)(2,1)S(1)}, bf16[208,128]{1,0:T(8,128)(2,1)S(1)}, u32[]{:S(2)}, u32[]{:S(2)}) collective-permute-start(bf16[208,128]{1,0:T(8,128)(2,1)S(1)} %fusion.16.refs_0_), channel_id=1, source_target_pairs={{0,8},{4,12},{8,0},{12,4},{16,24},{20,28},{24,16},{28,20},{1,9},{5... | collective-permute-start | bytes 159752 | tf_op jit(solution)/shard_map/ppermute | solution.py:555
  91.8 0.5 collective-permute-start.17
  92.3 1.0 collective-permute-done.22.refs_6_
  93.4 0.5 collective-permute-start.23
  93.9 1.6 %collective-permute-done.20.refs_4_ = bf16[208,128]{1,0:T(8,128)(2,1)S(1)} collective-permute-done((bf16[208,128]{1,0:T(8,128)(2,1)S(1)}, bf16[208,128]{1,0:T(8,128)(2,1)S(1)}, u32[]{:S(2)}, u32[]{:S(2)}) %collective-permute-start.20) | collective-permute-done | bytes 53280 | tf_op jit(solution)/shard_map/ppermute | solution.py:555
  95.4 0.6 collective-permute-start.21
  96.0 1.4 %collective-permute-start.19 = (bf16[208,128]{1,0:T(8,128)(2,1)S(1)}, bf16[208,128]{1,0:T(8,128)(2,1)S(1)}, u32[]{:S(2)}, u32[]{:S(2)}) collective-permute-start(bf16[208,128]{1,0:T(8,128)(2,1)S(1)} %collective-permute-done.18.refs_2_), channel_id=1, source_target_pairs={{0,4},{4,0},{8,12},{12,8},{16,20},{20,16},{24,28},{28,24},{1,5},{5... | collective-permute-start | bytes 159752 | tf_op jit(solution)/shard_map/ppermute | solution.py:555
  97.5 0.0 collective-permute-done.23.refs_7_
  97.5 2.1 %collective-permute-done.21.refs_5_ = bf16[208,128]{1,0:T(8,128)(2,1)S(1)} collective-permute-done((bf16[208,128]{1,0:T(8,128)(2,1)S(1)}, bf16[208,128]{1,0:T(8,128)(2,1)S(1)}, u32[]{:S(2)}, u32[]{:S(2)}) %collective-permute-start.21) | collective-permute-done | bytes 53280 | tf_op jit(solution)/shard_map/ppermute | solution.py:555
  99.6 0.6 collective-permute-done.19.refs_3_
  100.2 1.0 unpack_gradients.1
  (49 shorter events, 0.2 us)
Async XLA Ops:
  7.2 13.7 %copy-start = (s32[1,1,256]{2,1,0:T(1,128)S(1)}, s32[1,1,256]{2,1,0:T(1,128)}, u32[]{:S(2)}) copy-start(s32[1,1,256]{2,1,0:T(1,128)} %param.15) | copy-start | bytes 3076
  7.2 30.2 %all-gather.2.cloned.1.call-start = ((), (), s32[]{:S(2)}) async-start(), calls=%async_computation | async-start | bytes 2088960 | tf_op jit(solution)/shard_map/all_gather | solution.py:549
  10.2 12.2 %collective-permute-start = (bf16[64,1024]{1,0:T(8,128)(2,1)}, bf16[64,1024]{1,0:T(8,128)(2,1)S(1)}, u32[]{:S(2)}, u32[]{:S(2)}) collective-permute-start(bf16[64,1024]{1,0:T(8,128)(2,1)} %get-tuple-element.42), channel_id=1, source_target_pairs={{0,4},{4,0},{8,12},{12,8},{16,20},{20,16},{24,28},{28,24},{1,5},{5... | collective-permute-start | bytes 393224 | tf_op jit(solution)/shard_map/ppermute | solution.py:555
  13.2 12.9 %collective-permute-start.1 = (bf16[64,1024]{1,0:T(8,128)(2,1)}, bf16[64,1024]{1,0:T(8,128)(2,1)S(1)}, u32[]{:S(2)}, u32[]{:S(2)}) collective-permute-start(bf16[64,1024]{1,0:T(8,128)(2,1)} %get-tuple-element.43), channel_id=1, source_target_pairs={{0,8},{4,12},{8,0},{12,4},{16,24},{20,28},{24,16},{28,20},{1,9},{5... | collective-permute-start | bytes 393224 | tf_op jit(solution)/shard_map/ppermute | solution.py:555
  14.8 17.0 %collective-permute-start.2 = (bf16[64,1024]{1,0:T(8,128)(2,1)}, bf16[64,1024]{1,0:T(8,128)(2,1)S(1)}, u32[]{:S(2)}, u32[]{:S(2)}) collective-permute-start(bf16[64,1024]{1,0:T(8,128)(2,1)} %get-tuple-element.44), channel_id=1, source_target_pairs={{0,12},{4,8},{8,4},{12,0},{16,28},{20,24},{24,20},{28,16},{1,13},{... | collective-permute-start | bytes 393224 | tf_op jit(solution)/shard_map/ppermute | solution.py:555
  14.8 17.0 %collective-permute-start.3 = (bf16[64,1024]{1,0:T(8,128)(2,1)}, bf16[64,1024]{1,0:T(8,128)(2,1)S(1)}, u32[]{:S(2)}, u32[]{:S(2)}) collective-permute-start(bf16[64,1024]{1,0:T(8,128)(2,1)} %get-tuple-element.45), channel_id=1, source_target_pairs={{0,16},{4,20},{8,24},{12,28},{16,0},{20,4},{24,8},{28,12},{1,17},{... | collective-permute-start | bytes 393224 | tf_op jit(solution)/shard_map/ppermute | solution.py:555
  17.8 19.6 %collective-permute-start.4 = (bf16[64,1024]{1,0:T(8,128)(2,1)}, bf16[64,1024]{1,0:T(8,128)(2,1)S(1)}, u32[]{:S(2)}, u32[]{:S(2)}) collective-permute-start(bf16[64,1024]{1,0:T(8,128)(2,1)} %get-tuple-element.46), channel_id=1, source_target_pairs={{0,20},{4,16},{8,28},{12,24},{16,4},{20,0},{24,12},{28,8},{1,21},{... | collective-permute-start | bytes 393224 | tf_op jit(solution)/shard_map/ppermute | solution.py:555
  22.4 9.4 %copy-start.1 = (bf16[64,1024]{1,0:T(8,128)(2,1)}, bf16[64,1024]{1,0:T(8,128)(2,1)S(1)}, u32[]{:S(2)}) copy-start(bf16[64,1024]{1,0:T(8,128)(2,1)S(1)} %collective-permute-done.refs_1_) | copy-start | bytes 393220
  22.4 14.9 %collective-permute-start.5 = (bf16[64,1024]{1,0:T(8,128)(2,1)}, bf16[64,1024]{1,0:T(8,128)(2,1)S(1)}, u32[]{:S(2)}, u32[]{:S(2)}) collective-permute-start(bf16[64,1024]{1,0:T(8,128)(2,1)} %get-tuple-element.47), channel_id=1, source_target_pairs={{0,24},{4,28},{8,16},{12,20},{16,8},{20,12},{24,0},{28,4},{1,25},{... | collective-permute-start | bytes 393224 | tf_op jit(solution)/shard_map/ppermute | solution.py:555
  26.0 5.8 %copy-start.2 = (bf16[64,1024]{1,0:T(8,128)(2,1)}, bf16[64,1024]{1,0:T(8,128)(2,1)S(1)}, u32[]{:S(2)}) copy-start(bf16[64,1024]{1,0:T(8,128)(2,1)S(1)} %collective-permute-done.1.refs_2_) | copy-start | bytes 393220
  26.0 11.3 %collective-permute-start.6 = (bf16[64,1024]{1,0:T(8,128)(2,1)}, bf16[64,1024]{1,0:T(8,128)(2,1)S(1)}, u32[]{:S(2)}, u32[]{:S(2)}) collective-permute-start(bf16[64,1024]{1,0:T(8,128)(2,1)} %get-tuple-element.48), channel_id=1, source_target_pairs={{0,28},{4,24},{8,20},{12,16},{16,12},{20,8},{24,4},{28,0},{1,29},{... | collective-permute-start | bytes 393224 | tf_op jit(solution)/shard_map/ppermute | solution.py:555
  31.8 5.6 %copy-start.3 = (bf16[64,1024]{1,0:T(8,128)(2,1)}, bf16[64,1024]{1,0:T(8,128)(2,1)S(1)}, u32[]{:S(2)}) copy-start(bf16[64,1024]{1,0:T(8,128)(2,1)S(1)} %collective-permute-done.2.refs_3_) | copy-start | bytes 393220
  31.8 5.6 %copy-start.4 = (bf16[64,1024]{1,0:T(8,128)(2,1)}, bf16[64,1024]{1,0:T(8,128)(2,1)S(1)}, u32[]{:S(2)}) copy-start(bf16[64,1024]{1,0:T(8,128)(2,1)S(1)} %collective-permute-done.3.refs_4_) | copy-start | bytes 393220
  37.4 0.6 copy-start.5
  37.4 0.7 copy-start.6
  37.4 0.7 copy-start.7
  56.0 3.7 %collective-permute-start.7 = (f32[2,8,208,128]{3,2,1,0:T(8,128)S(1)}, f32[2,8,208,128]{3,2,1,0:T(8,128)S(1)}, u32[]{:S(2)}, u32[]{:S(2)}) collective-permute-start(f32[2,8,208,128]{3,2,1,0:T(8,128)S(1)} %get-tuple-element.56), channel_id=1, source_target_pairs={{0,1},{1,0},{2,3},{3,2},{4,5},{5,4},{6,7},{7,6},{8,9},{9,8},{10,11... | collective-permute-start | bytes 5111816 | tf_op jit(solution)/shard_map/ppermute | solution.py:580
  59.8 7.4 %collective-permute-start.8 = (bf16[4,208,128]{2,1,0:T(8,128)(2,1)S(1)}, bf16[4,208,128]{2,1,0:T(8,128)(2,1)S(1)}, u32[]{:S(2)}, u32[]{:S(2)}) collective-permute-start(bf16[4,208,128]{2,1,0:T(8,128)(2,1)S(1)} %get-tuple-element.64), channel_id=1, source_target_pairs={{0,2},{1,3},{2,0},{3,1},{4,6},{5,7},{6,4},{7,5},{8,10},{9,11},{10,... | collective-permute-start | bytes 638984 | tf_op jit(solution)/shard_map/ppermute | solution.py:585
  67.2 12.0 %collective-permute-start.9 = (bf16[4,208,128]{2,1,0:T(8,128)(2,1)S(1)}, bf16[4,208,128]{2,1,0:T(8,128)(2,1)S(1)}, u32[]{:S(2)}, u32[]{:S(2)}) collective-permute-start(bf16[4,208,128]{2,1,0:T(8,128)(2,1)S(1)} %get-tuple-element.57), channel_id=1, source_target_pairs={{0,2},{1,3},{2,0},{3,1},{4,6},{5,7},{6,4},{7,5},{8,10},{9,11},{10,... | collective-permute-start | bytes 638984 | tf_op jit(solution)/shard_map/ppermute | solution.py:589
  68.8 12.0 %collective-permute-start.13 = (bf16[208,128]{1,0:T(8,128)(2,1)S(1)}, bf16[208,128]{1,0:T(8,128)(2,1)S(1)}, u32[]{:S(2)}, u32[]{:S(2)}) collective-permute-start(bf16[208,128]{1,0:T(8,128)(2,1)S(1)} %get-tuple-element.69), channel_id=1, source_target_pairs={{0,16},{4,20},{8,24},{12,28},{16,0},{20,4},{24,8},{28,12},{1,17},{... | collective-permute-start | bytes 159752 | tf_op jit(solution)/shard_map/ppermute | solution.py:555
  75.4 7.8 %collective-permute-start.16 = (bf16[208,128]{1,0:T(8,128)(2,1)S(1)}, bf16[208,128]{1,0:T(8,128)(2,1)S(1)}, u32[]{:S(2)}, u32[]{:S(2)}) collective-permute-start(bf16[208,128]{1,0:T(8,128)(2,1)S(1)} %get-tuple-element.70), channel_id=1, source_target_pairs={{0,28},{4,24},{8,20},{12,16},{16,12},{20,8},{24,4},{28,0},{1,29},{... | collective-permute-start | bytes 159752 | tf_op jit(solution)/shard_map/ppermute | solution.py:555
  76.2 7.0 %collective-permute-start.15 = (bf16[208,128]{1,0:T(8,128)(2,1)S(1)}, bf16[208,128]{1,0:T(8,128)(2,1)S(1)}, u32[]{:S(2)}, u32[]{:S(2)}) collective-permute-start(bf16[208,128]{1,0:T(8,128)(2,1)S(1)} %get-tuple-element.71), channel_id=1, source_target_pairs={{0,24},{4,28},{8,16},{12,20},{16,8},{20,12},{24,0},{28,4},{1,25},{... | collective-permute-start | bytes 159752 | tf_op jit(solution)/shard_map/ppermute | solution.py:555
  79.3 5.9 %collective-permute-start.14 = (bf16[208,128]{1,0:T(8,128)(2,1)S(1)}, bf16[208,128]{1,0:T(8,128)(2,1)S(1)}, u32[]{:S(2)}, u32[]{:S(2)}) collective-permute-start(bf16[208,128]{1,0:T(8,128)(2,1)S(1)} %get-tuple-element.72), channel_id=1, source_target_pairs={{0,20},{4,16},{8,28},{12,24},{16,4},{20,0},{24,12},{28,8},{1,21},{... | collective-permute-start | bytes 159752 | tf_op jit(solution)/shard_map/ppermute | solution.py:555
  79.4 5.8 %collective-permute-start.10 = (bf16[208,128]{1,0:T(8,128)(2,1)S(1)}, bf16[208,128]{1,0:T(8,128)(2,1)S(1)}, u32[]{:S(2)}, u32[]{:S(2)}) collective-permute-start(bf16[208,128]{1,0:T(8,128)(2,1)S(1)} %get-tuple-element.66), channel_id=1, source_target_pairs={{0,4},{4,0},{8,12},{12,8},{16,20},{20,16},{24,28},{28,24},{1,5},{5... | collective-permute-start | bytes 159752 | tf_op jit(solution)/shard_map/ppermute | solution.py:555
  80.9 5.0 %collective-permute-start.12 = (bf16[208,128]{1,0:T(8,128)(2,1)S(1)}, bf16[208,128]{1,0:T(8,128)(2,1)S(1)}, u32[]{:S(2)}, u32[]{:S(2)}) collective-permute-start(bf16[208,128]{1,0:T(8,128)(2,1)S(1)} %get-tuple-element.67), channel_id=1, source_target_pairs={{0,12},{4,8},{8,4},{12,0},{16,28},{20,24},{24,20},{28,16},{1,13},{... | collective-permute-start | bytes 159752 | tf_op jit(solution)/shard_map/ppermute | solution.py:555
  83.2 4.1 %collective-permute-start.11 = (bf16[208,128]{1,0:T(8,128)(2,1)S(1)}, bf16[208,128]{1,0:T(8,128)(2,1)S(1)}, u32[]{:S(2)}, u32[]{:S(2)}) collective-permute-start(bf16[208,128]{1,0:T(8,128)(2,1)S(1)} %get-tuple-element.68), channel_id=1, source_target_pairs={{0,8},{4,12},{8,0},{12,4},{16,24},{20,28},{24,16},{28,20},{1,9},{5... | collective-permute-start | bytes 159752 | tf_op jit(solution)/shard_map/ppermute | solution.py:555
  87.4 6.0 %collective-permute-start.22 = (bf16[208,128]{1,0:T(8,128)(2,1)S(1)}, bf16[208,128]{1,0:T(8,128)(2,1)S(1)}, u32[]{:S(2)}, u32[]{:S(2)}) collective-permute-start(bf16[208,128]{1,0:T(8,128)(2,1)S(1)} %fusion.16.refs_0_), channel_id=1, source_target_pairs={{0,24},{4,28},{8,16},{12,20},{16,8},{20,12},{24,0},{28,4},{1,25},{... | collective-permute-start | bytes 159752 | tf_op jit(solution)/shard_map/ppermute | solution.py:555
  90.4 5.0 %collective-permute-start.20 = (bf16[208,128]{1,0:T(8,128)(2,1)S(1)}, bf16[208,128]{1,0:T(8,128)(2,1)S(1)}, u32[]{:S(2)}, u32[]{:S(2)}) collective-permute-start(bf16[208,128]{1,0:T(8,128)(2,1)S(1)} %fusion.16.refs_0_), channel_id=1, source_target_pairs={{0,16},{4,20},{8,24},{12,28},{16,0},{20,4},{24,8},{28,12},{1,17},{... | collective-permute-start | bytes 159752 | tf_op jit(solution)/shard_map/ppermute | solution.py:555
  90.4 5.6 %collective-permute-start.18 = (bf16[208,128]{1,0:T(8,128)(2,1)S(1)}, bf16[208,128]{1,0:T(8,128)(2,1)S(1)}, u32[]{:S(2)}, u32[]{:S(2)}) collective-permute-start(bf16[208,128]{1,0:T(8,128)(2,1)S(1)} %fusion.16.refs_0_), channel_id=1, source_target_pairs={{0,8},{4,12},{8,0},{12,4},{16,24},{20,28},{24,16},{28,20},{1,9},{5... | collective-permute-start | bytes 159752 | tf_op jit(solution)/shard_map/ppermute | solution.py:555
  91.8 5.7 %collective-permute-start.17 = (bf16[208,128]{1,0:T(8,128)(2,1)S(1)}, bf16[208,128]{1,0:T(8,128)(2,1)S(1)}, u32[]{:S(2)}, u32[]{:S(2)}) collective-permute-start(bf16[208,128]{1,0:T(8,128)(2,1)S(1)} %fusion.16.refs_0_), channel_id=1, source_target_pairs={{0,4},{4,0},{8,12},{12,8},{16,20},{20,16},{24,28},{28,24},{1,5},{5... | collective-permute-start | bytes 159752 | tf_op jit(solution)/shard_map/ppermute | solution.py:555
  93.4 4.1 %collective-permute-start.23 = (bf16[208,128]{1,0:T(8,128)(2,1)S(1)}, bf16[208,128]{1,0:T(8,128)(2,1)S(1)}, u32[]{:S(2)}, u32[]{:S(2)}) collective-permute-start(bf16[208,128]{1,0:T(8,128)(2,1)S(1)} %collective-permute-done.22.refs_6_), channel_id=1, source_target_pairs={{0,4},{4,0},{8,12},{12,8},{16,20},{20,16},{24,28},{28,24},{1,5},{5... | collective-permute-start | bytes 159752 | tf_op jit(solution)/shard_map/ppermute | solution.py:555
  95.4 4.1 %collective-permute-start.21 = (bf16[208,128]{1,0:T(8,128)(2,1)S(1)}, bf16[208,128]{1,0:T(8,128)(2,1)S(1)}, u32[]{:S(2)}, u32[]{:S(2)}) collective-permute-start(bf16[208,128]{1,0:T(8,128)(2,1)S(1)} %collective-permute-done.20.refs_4_), channel_id=1, source_target_pairs={{0,4},{4,0},{8,12},{12,8},{16,20},{20,16},{24,28},{28,24},{1,5},{5... | collective-permute-start | bytes 159752 | tf_op jit(solution)/shard_map/ppermute | solution.py:555
  96.0 4.1 %collective-permute-start.19 = (bf16[208,128]{1,0:T(8,128)(2,1)S(1)}, bf16[208,128]{1,0:T(8,128)(2,1)S(1)}, u32[]{:S(2)}, u32[]{:S(2)}) collective-permute-start(bf16[208,128]{1,0:T(8,128)(2,1)S(1)} %collective-permute-done.18.refs_2_), channel_id=1, source_target_pairs={{0,4},{4,0},{8,12},{12,8},{16,20},{20,16},{24,28},{28,24},{1,5},{5... | collective-permute-start | bytes 159752 | tf_op jit(solution)/shard_map/ppermute | solution.py:555
Sparse Core Ops, SparseCore 0:
  10.3 22.8 all-gather.1
